TPU v7x, 256 devices: a whole 4x4x8 slice. The times are simulated.
256 devices in a mesh: gx: 4 (over x), gy: 2 (over core), gz: 32 (over z, y).
Axes of the slice: x: 4, y: 4, z: 8, core: 2. Of those that a mesh axis runs over, the one named last changes fastest.
Arguments:
- correction: float32 [512, 64, 512], P('gz', 'gx', 'gy'), may hold values from -6 to 6
- residual: float32 [512, 64, 512], P('gz', 'gx', 'gy'), may hold values from -4 to 6
- state: float32 [512, 64, 512], P('gz', 'gx', 'gy'), may hold values from -1 to 1
- spacing_level: int32 [512], replicated, may hold values from 0 to 3
- line_colour: int32 [64, 512], P('gx', 'gy'), may hold values from 0 to 1
Outputs:
- smoothed: float32 [512, 64, 512], P('gz', 'gx', 'gy')
All inputs are finite; a program needn't handle non-finite values.
Results may differ from a plain program's by a relative error of at most 0.0003.
Values sent between devices are 32-bit elements; how exact they have to be, the bound alone decides.
No kernel may reach another device: no remote copies, remote signals or barrier semaphores. Data moves between devices by JAX's collectives and lax.ppermute only.
A program may use at most 64 MiB of HBM per device.

v0:
```python
import jax
import jax.numpy as jnp
from jax import lax
from jax.sharding import Mesh
from jax.sharding import PartitionSpec as P

GZ = ("gz_0", "gz_1")


coef_z = 1000.0
coef_x = 0.3
coef_y = 0.2
bratu_lambda = 0.2


def gathered_by_axis(value, axes, dim):
    for axis in reversed(axes):
        value = lax.all_gather(value, axis, axis=dim, tiled=True)
    return value


def padded_2(value, sides, width):
    edges = {}
    for axis, dim in sides:
        devices, length = (lax.axis_size(axis), value.shape[dim])
        up = [(i, (i + 1) % devices) for i in range(devices - 1)]
        last = lax.slice_in_dim(value, length - width, length, axis=dim)
        first = lax.slice_in_dim(value, 0, width, axis=dim)
        edges[dim] = (
            lax.ppermute(last, axis, up),
            lax.ppermute(first, axis, [(b, a) for a, b in up]),
        )
    done = []
    for _, dim in sides:
        low, high = edges[dim]
        around = [(width, width) if d in done else (0, 0) for d in range(value.ndim)]
        value = jnp.concatenate([jnp.pad(low, around), value, jnp.pad(high, around)], axis=dim)
        done.append(dim)
    return value


def laid_out(blocks, dim):
    blocks = jnp.moveaxis(blocks, 0, dim)
    lengths = blocks.shape
    return blocks.reshape(*lengths[:dim], lengths[dim] * lengths[dim + 1], *lengths[dim + 2 :])


def from_everyone(value, axis):
    copies = jnp.broadcast_to(value, (lax.axis_size(axis), *value.shape))
    return lax.all_to_all(copies, axis, split_axis=0, concat_axis=0, tiled=True)


def gather_directly(value, axis, dim):
    return laid_out(from_everyone(value, axis), dim)


def face_coupling(spacing_level):
    spacing_cells = 0.8 * jnp.power(1.3, spacing_level.astype(jnp.float32))
    inner_faces = coef_z * 2.0 / (spacing_cells[:-1] + spacing_cells[1:])
    nothing = jnp.zeros((1,), jnp.float32)
    face_low = jnp.concatenate([nothing, inner_faces])
    face_high = jnp.concatenate([inner_faces, nothing])
    return (spacing_cells, face_low, face_high)


def move_rows(values, stride, filler):
    length = values.shape[0]
    padding = jnp.full((abs(stride),) + values.shape[1:], filler, values.dtype)
    if stride > 0:
        return jnp.concatenate([padding, values[: length - stride]], 0)
    return jnp.concatenate([values[-stride:], padding], 0)


def factor_local(below_coef, centre, above_coef):
    length = centre.shape[0]
    sections = []
    stride = 1
    while stride < length:
        before_low = move_rows(below_coef, stride, 0.0)
        before_mid = move_rows(centre, stride, 1.0)
        before_high = move_rows(above_coef, stride, 0.0)
        beyond_low = move_rows(below_coef, -stride, 0.0)
        beyond_mid = move_rows(centre, -stride, 1.0)
        beyond_high = move_rows(above_coef, -stride, 0.0)
        weight_low = -below_coef / before_mid
        weight_high = -above_coef / beyond_mid
        centre = centre + weight_low * before_high + weight_high * beyond_low
        below_coef = weight_low * before_low
        above_coef = weight_high * beyond_high
        sections.append((weight_low, weight_high))
        stride = stride * 2
    return (sections, centre)


def apply_local(source, sections, centre):
    stride = 1
    for weight_low, weight_high in sections:
        source = (
            source
            + weight_low * move_rows(source, stride, 0.0)
            + weight_high * move_rows(source, -stride, 0.0)
        )
        stride = stride * 2
    return source / centre


def on_device(correction, residual, state, spacing_level, line_colour):
    depth = correction.shape[0]
    device_place = lax.axis_index(GZ)
    spacing_all, face_low_all, face_high_all = face_coupling(spacing_level)
    offset_rows = device_place * depth
    spacing_cells = lax.dynamic_slice_in_dim(spacing_all, offset_rows, depth)
    face_low = lax.dynamic_slice_in_dim(face_low_all, offset_rows, depth)
    face_high = lax.dynamic_slice_in_dim(face_high_all, offset_rows, depth)
    column = spacing_cells[:, None, None]
    centre = (face_low + face_high)[:, None, None] + column * (
        2.0 * coef_x + 2.0 * coef_y - bratu_lambda * jnp.exp(state)
    )
    line_shape = centre.shape
    row_column = jnp.arange(depth)[:, None, None]
    edge_rows = (row_column == 0) | (row_column == depth - 1)
    low_full = jnp.broadcast_to((-face_low)[:, None, None], line_shape)
    high_full = jnp.broadcast_to((-face_high)[:, None, None], line_shape)
    inner_low = jnp.where((row_column <= 1) | (row_column == depth - 1), 0.0, low_full)
    inner_high = jnp.where((row_column >= depth - 2) | (row_column == 0), 0.0, high_full)
    inner_centre = jnp.where(edge_rows, 1.0, centre)
    sections_local, centre_local = factor_local(inner_low, inner_centre, inner_high)
    from_first = apply_local(
        jnp.where(row_column == 1, -low_full, 0.0), sections_local, centre_local
    )
    from_last = apply_local(
        jnp.where(row_column == depth - 2, -high_full, 0.0), sections_local, centre_local
    )
    first_low = low_full[0]
    first_mid = centre[0] + high_full[0] * from_first[1]
    first_high = high_full[0] * from_last[1]
    last_low = low_full[depth - 1] * from_first[depth - 2]
    last_mid = centre[depth - 1] + low_full[depth - 1] * from_last[depth - 2]
    last_high = high_full[depth - 1]
    coupled = jnp.stack(
        [
            jnp.stack([first_low, last_low], 0),
            jnp.stack([first_mid, last_mid], 0),
            jnp.stack([first_high, last_high], 0),
        ],
        0,
    )
    gathered = gathered_by_axis(coupled, GZ, 1)
    sections_reduced, centre_reduced = factor_local(gathered[0], gathered[1], gathered[2])
    iterate = correction
    for colour in range(2):
        padded = padded_2(iterate, (("gx", 1), ("gy", 2)), 1)
        beside = coef_x * (padded[:, 2:, 1:-1] + padded[:, :-2, 1:-1]) + coef_y * (
            padded[:, 1:-1, 2:] + padded[:, 1:-1, :-2]
        )
        source = column * (residual + beside)
        interior = apply_local(jnp.where(edge_rows, 0.0, source), sections_local, centre_local)
        first_source = source[0] - high_full[0] * interior[1]
        last_source = source[depth - 1] - low_full[depth - 1] * interior[depth - 2]
        source_pair = jnp.stack([first_source, last_source], 0)
        all_sources = gather_directly(source_pair, GZ, 0)
        solution = apply_local(all_sources, sections_reduced, centre_reduced)
        ends_value = lax.dynamic_slice_in_dim(solution, 2 * device_place, 2, 0)
        first_cell = ends_value[0]
        last_cell = ends_value[1]
        inside = interior + from_first * first_cell[None] + from_last * last_cell[None]
        solved = jnp.where(
            row_column == 0,
            first_cell[None],
            jnp.where(row_column == depth - 1, last_cell[None], inside),
        )
        iterate = jnp.where((line_colour == colour)[None], solved, iterate)
    return iterate


def solution(mesh):
    finer = Mesh(
        mesh.devices.reshape(mesh.shape["gx"], mesh.shape["gy"], 8, 4), ("gx", "gy", "gz_0", "gz_1")
    )
    in_specs = (P(GZ, "gx", "gy"), P(GZ, "gx", "gy"), P(GZ, "gx", "gy"), P(), P("gx", "gy"))
    out_specs = P(GZ, "gx", "gy")
    return jax.shard_map(
        on_device, mesh=finer, in_specs=in_specs, out_specs=out_specs, check_vma=False
    )
```

profile of v0, /device:TPU:6, one launch (start us, length us, event | category | flops | bytes accessed | tf_op | source)
XLA Modules:
  0.0 188.4 jit_solution(12435043617073529275)
XLA Ops:
  6.5 1.1 fusion.81
  7.7 1.3 collective-permute-start.2
  9.0 3.0 %collective-permute-start.3 = (f32[16,16,1]{2,1,0:T(8,128)S(1)}, f32[16,16,1]{2,1,0:T(8,128)S(1)}, u32[]{:S(2)}, u32[]{:S(2)}) collective-permute-start(f32[16,16,1]{2,1,0:T(8,128)S(1)} %get-tuple-element.160), channel_id=1, source_target_pairs={{0,32},{1,33},{2,34},{3,35},{4,36},{5,37},{6,38},{7,39},{8,40},{9,... | collective-permute-start | bytes 3080 | tf_op jit(solution)/shard_map/ppermute | solution.py:30
  12.0 1.0 fusion.82
  13.0 2.7 %collective-permute-start = (f32[16,1,256]{2,1,0:T(1,128)S(1)}, f32[16,1,256]{2,1,0:T(1,128)S(1)}, u32[]{:S(2)}, u32[]{:S(2)}) collective-permute-start(f32[16,1,256]{2,1,0:T(1,128)S(1)} %get-tuple-element.162), channel_id=1, source_target_pairs={{64,0},{128,64},{192,128},{65,1},{129,65},{193,129},{66,2},{130,66... | collective-permute-start | bytes 49160 | tf_op jit(solution)/shard_map/ppermute | solution.py:31
  15.8 1.3 collective-permute-start.1
  19.8 1.6 collective-permute-done.1
  21.4 1.1 broadcast_select_fusion.6
  25.6 0.7 copy-done.4
  26.3 1.3 slice_multiply_fusion.5
  28.9 14.1 %all_gather.6 = f32[3,8,16,256]{3,2,1,0:T(8,128)} all-gather(f32[3,2,16,256]{3,2,1,0:T(8,128)S(1)} %pad_maximum_fusion.12), channel_id=1, replica_groups=mesh['gx'=4,'gy'=2,'gz_0'=8,'gz_1'=4] {'gz_1'}, dimensions={1}, use_global_device_ids=true | all-gather | bytes 491520 | tf_op jit(solution)/shard_map/all_gather | solution.py:18
  43.3 2.0 %fusion.37 = (f32[1,16,256]{2,1,0:T(8,128)S(1)}, f32[1,16,256]{2,1,0:T(8,128)S(1)}) fusion(f32[16,16,256]{2,1,0:T(8,128)S(1)} %add_divide_fusion.3, f32[16,16,256]{2,1,0:T(8,128)} %get-tuple-element.43, f32[]{:T(128)} %bitcast, f32[]{:T(128)} %bitcast.1), kind=kLoop, calls=%fused_computation.167 | loop fusion | flops 16384 | bytes 98312 | tf_op jit(solution)/shard_map/sub | solution.py:158
  45.3 1.1 broadcast_in_dim.164
  46.5 10.6 %all-to-all-start = ((f32[32,2,16,256]{3,2,1,0:T(8,128)}), f32[32,2,16,256]{3,2,1,0:T(8,128)S(1)}, u32[]{:S(2)}, u32[]{:S(2)}) async-start(f32[32,2,16,256]{3,2,1,0:T(8,128)} %broadcast_in_dim.164), calls=%async_computation | async-start | bytes 2097152 | tf_op jit(solution)/shard_map/all_to_all | solution.py:50
  57.6 35.3 %all-to-all-done = f32[32,2,16,256]{3,2,1,0:T(8,128)S(1)} async-done(((f32[32,2,16,256]{3,2,1,0:T(8,128)}), f32[32,2,16,256]{3,2,1,0:T(8,128)S(1)}, u32[]{:S(2)}, u32[]{:S(2)}) %all-to-all-start) | async-done | bytes 1048608 | tf_op jit(solution)/shard_map/all_to_all | solution.py:50
  92.9 1.6 fusion.69
  94.5 14.2 %all-gather.2.cloned.1.call-done = f32[3,64,16,256]{3,2,1,0:T(8,128)} async-done(((f32[3,8,16,256]{3,2,1,0:T(8,128)}), f32[3,64,16,256]{3,2,1,0:T(8,128)}) %all-gather.2.cloned.1.call-update) | async-done | bytes 3145744 | tf_op jit(solution)/shard_map/all_gather | solution.py:18
  108.8 3.7 %slice_bitcast_fusion.1 = (f32[63,16,256]{2,1,0:T(8,128)S(1)}, f32[63,16,256]{2,1,0:T(8,128)S(1)}, f32[63,16,256]{2,1,0:T(8,128)S(1)}, f32[63,16,256]{2,1,0:T(8,...) fusion(f32[3,64,16,256]{3,2,1,0:T(8,128)} %all-gather.2.cloned.1.call-done), kind=kLoop, calls=%fused_computation.48 | loop fusion | bytes 12386304 | tf_op jit(solution)/shard_map/slice | solution.py:71
  113.1 0.9 multiply_add_fusion.14
  115.2 1.4 multiply_add_fusion.13
  118.3 1.3 multiply_add_fusion.11
  120.1 0.7 multiply_add_fusion.10
  121.9 0.9 multiply_add_fusion.9
  125.0 1.1 multiply_add_fusion.6
  127.6 3.1 %collective-permute-start.4 = (f32[16,1,256]{2,1,0:T(1,128)S(1)}, f32[16,1,256]{2,1,0:T(1,128)S(1)}, u32[]{:S(2)}, u32[]{:S(2)}) collective-permute-start(f32[16,1,256]{2,1,0:T(1,128)S(1)} %get-tuple-element.142), channel_id=1, source_target_pairs={{64,0},{128,64},{192,128},{65,1},{129,65},{193,129},{66,2},{130,66... | collective-permute-start | bytes 49160 | tf_op jit(solution)/shard_map/ppermute | solution.py:31
  130.7 1.3 collective-permute-start.5
  132.1 1.3 collective-permute-start.6
  133.4 3.0 %collective-permute-start.7 = (f32[16,16,1]{2,1,0:T(8,128)S(1)}, f32[16,16,1]{2,1,0:T(8,128)S(1)}, u32[]{:S(2)}, u32[]{:S(2)}) collective-permute-start(f32[16,16,1]{2,1,0:T(8,128)S(1)} %get-tuple-element.140), channel_id=1, source_target_pairs={{0,32},{1,33},{2,34},{3,35},{4,36},{5,37},{6,38},{7,39},{8,40},{9,... | collective-permute-start | bytes 3080 | tf_op jit(solution)/shard_map/ppermute | solution.py:30
  136.5 1.0 collective-permute-done.7
  139.2 1.3 fusion.33
  140.7 35.6 %all_to_all.10 = f32[32,2,16,256]{3,2,1,0:T(8,128)S(1)} all-to-all(f32[32,2,16,256]{3,2,1,0:T(8,128)S(1)} %broadcast_in_dim.174), channel_id=1, replica_groups=mesh['gx'=4,'gy'=2,'gz_0'=8,'gz_1'=4] {'gz_0','gz_1'}, dimensions={0} | all-to-all | bytes 2097152 | tf_op jit(solution)/shard_map/all_to_all | solution.py:50
  180.8 0.8 select_select_fusion
  (164 shorter events, 22.3 us)
Async XLA Ops:
  6.5 14.9 %copy-start.3 = (f32[16,16,256]{2,1,0:T(8,128)S(1)}, f32[16,16,256]{2,1,0:T(8,128)}, u32[]{:S(2)}) copy-start(f32[16,16,256]{2,1,0:T(8,128)} %param.5) | copy-start | bytes 786436
  6.5 14.9 %copy-start.18 = (f32[16,16,256]{2,1,0:T(8,128)S(1)}, f32[16,16,256]{2,1,0:T(8,128)}, u32[]{:S(2)}) copy-start(f32[16,16,256]{2,1,0:T(8,128)} %param.6) | copy-start | bytes 786436
  6.5 14.9 %copy-start.20 = (f32[16,16,256]{2,1,0:T(8,128)S(1)}, f32[16,16,256]{2,1,0:T(8,128)}, u32[]{:S(2)}) copy-start(f32[16,16,256]{2,1,0:T(8,128)} %param.7) | copy-start | bytes 786436
  6.5 102.2 %all-gather.2.cloned.1.call-start = ((), (), s32[]{:S(2)}) async-start(), calls=%async_computation.2 | async-start | bytes 3538944 | tf_op jit(solution)/shard_map/all_gather | solution.py:18
  7.7 12.1 %collective-permute-start.2 = (f32[16,16,1]{2,1,0:T(8,128)S(1)}, f32[16,16,1]{2,1,0:T(8,128)S(1)}, u32[]{:S(2)}, u32[]{:S(2)}) collective-permute-start(f32[16,16,1]{2,1,0:T(8,128)S(1)} %get-tuple-element.159), channel_id=1, source_target_pairs={{32,0},{33,1},{34,2},{35,3},{36,4},{37,5},{38,6},{39,7},{40,8},{41... | collective-permute-start | bytes 3080 | tf_op jit(solution)/shard_map/ppermute | solution.py:31
  9.0 10.8 %collective-permute-start.3 = (f32[16,16,1]{2,1,0:T(8,128)S(1)}, f32[16,16,1]{2,1,0:T(8,128)S(1)}, u32[]{:S(2)}, u32[]{:S(2)}) collective-permute-start(f32[16,16,1]{2,1,0:T(8,128)S(1)} %get-tuple-element.160), channel_id=1, source_target_pairs={{0,32},{1,33},{2,34},{3,35},{4,36},{5,37},{6,38},{7,39},{8,40},{9,... | collective-permute-start | bytes 3080 | tf_op jit(solution)/shard_map/ppermute | solution.py:30
  13.0 6.8 %collective-permute-start = (f32[16,1,256]{2,1,0:T(1,128)S(1)}, f32[16,1,256]{2,1,0:T(1,128)S(1)}, u32[]{:S(2)}, u32[]{:S(2)}) collective-permute-start(f32[16,1,256]{2,1,0:T(1,128)S(1)} %get-tuple-element.162), channel_id=1, source_target_pairs={{64,0},{128,64},{192,128},{65,1},{129,65},{193,129},{66,2},{130,66... | collective-permute-start | bytes 49160 | tf_op jit(solution)/shard_map/ppermute | solution.py:31
  15.8 5.6 %collective-permute-start.1 = (f32[16,1,256]{2,1,0:T(1,128)S(1)}, f32[16,1,256]{2,1,0:T(1,128)S(1)}, u32[]{:S(2)}, u32[]{:S(2)}) collective-permute-start(f32[16,1,256]{2,1,0:T(1,128)S(1)} %get-tuple-element.161), channel_id=1, source_target_pairs={{0,64},{64,128},{128,192},{1,65},{65,129},{129,193},{2,66},{66,130... | collective-permute-start | bytes 49160 | tf_op jit(solution)/shard_map/ppermute | solution.py:30
  24.3 0.8 copy-start.8
  25.2 17.9 %copy-start.12 = (f32[8,16,256]{2,1,0:T(8,128)}, f32[8,16,256]{2,1,0:T(8,128)S(1)}, u32[]{:S(2)}) copy-start(f32[8,16,256]{2,1,0:T(8,128)S(1)} %get-tuple-element.163) | copy-start | bytes 393220
  25.2 17.9 %copy-start.14 = (f32[8,16,256]{2,1,0:T(8,128)}, f32[8,16,256]{2,1,0:T(8,128)S(1)}, u32[]{:S(2)}) copy-start(f32[8,16,256]{2,1,0:T(8,128)S(1)} %get-tuple-element.164) | copy-start | bytes 393220
  25.2 18.0 %copy-start.10 = (f32[8,16,256]{2,1,0:T(8,128)}, f32[8,16,256]{2,1,0:T(8,128)S(1)}, u32[]{:S(2)}) copy-start(f32[8,16,256]{2,1,0:T(8,128)S(1)} %slice.711) | copy-start | bytes 393220
  43.0 14.6 %copy-start.21 = (s32[16,256]{1,0:T(8,128)S(1)}, s32[16,256]{1,0:T(8,128)}, u32[]{:S(2)}) copy-start(s32[16,256]{1,0:T(8,128)} %param.9) | copy-start | bytes 49156
  43.3 3.2 %copy-start.16 = (f32[16,16,256]{2,1,0:T(8,128)}, f32[16,16,256]{2,1,0:T(8,128)S(1)}, u32[]{:S(2)}) copy-start(f32[16,16,256]{2,1,0:T(8,128)S(1)} %add_divide_fusion.3) | copy-start | bytes 786436
  46.5 46.5 %all-to-all-start = ((f32[32,2,16,256]{3,2,1,0:T(8,128)}), f32[32,2,16,256]{3,2,1,0:T(8,128)S(1)}, u32[]{:S(2)}, u32[]{:S(2)}) async-start(f32[32,2,16,256]{3,2,1,0:T(8,128)} %broadcast_in_dim.164), calls=%async_computation | async-start | bytes 2097152 | tf_op jit(solution)/shard_map/all_to_all | solution.py:50
  108.8 3.7 %copy-start = (f32[3,64,16,256]{3,2,1,0:T(8,128)S(1)}, f32[3,64,16,256]{3,2,1,0:T(8,128)}, u32[]{:S(2)}) copy-start(f32[3,64,16,256]{3,2,1,0:T(8,128)} %all-gather.2.cloned.1.call-done) | copy-start | bytes 9437188
  108.8 4.0 %copy-start.1 = (f32[63,16,256]{2,1,0:T(8,128)S(1)}, f32[63,16,256]{2,1,0:T(8,128)}, u32[]{:S(2)}) copy-start(f32[63,16,256]{2,1,0:T(8,128)} %get-tuple-element.112) | copy-start | bytes 3096580
  108.8 4.3 %copy-start.2 = (f32[63,16,256]{2,1,0:T(8,128)S(1)}, f32[63,16,256]{2,1,0:T(8,128)}, u32[]{:S(2)}) copy-start(f32[63,16,256]{2,1,0:T(8,128)} %get-tuple-element.113) | copy-start | bytes 3096580
  126.4 1.0 copy-start.5
  126.4 1.0 copy-start.17
  126.4 1.0 copy-start.22
  126.4 1.0 copy-start.23
  127.1 10.4 %copy-start.19 = (f32[16,16,256]{2,1,0:T(8,128)S(1)}, f32[16,16,256]{2,1,0:T(8,128)}, u32[]{:S(2)}) copy-start(f32[16,16,256]{2,1,0:T(8,128)} %param.6) | copy-start | bytes 786436
  127.6 9.9 %collective-permute-start.4 = (f32[16,1,256]{2,1,0:T(1,128)S(1)}, f32[16,1,256]{2,1,0:T(1,128)S(1)}, u32[]{:S(2)}, u32[]{:S(2)}) collective-permute-start(f32[16,1,256]{2,1,0:T(1,128)S(1)} %get-tuple-element.142), channel_id=1, source_target_pairs={{64,0},{128,64},{192,128},{65,1},{129,65},{193,129},{66,2},{130,66... | collective-permute-start | bytes 49160 | tf_op jit(solution)/shard_map/ppermute | solution.py:31
  130.7 6.7 %collective-permute-start.5 = (f32[16,1,256]{2,1,0:T(1,128)S(1)}, f32[16,1,256]{2,1,0:T(1,128)S(1)}, u32[]{:S(2)}, u32[]{:S(2)}) collective-permute-start(f32[16,1,256]{2,1,0:T(1,128)S(1)} %get-tuple-element.141), channel_id=1, source_target_pairs={{0,64},{64,128},{128,192},{1,65},{65,129},{129,193},{2,66},{66,130... | collective-permute-start | bytes 49160 | tf_op jit(solution)/shard_map/ppermute | solution.py:30
  132.1 4.4 %collective-permute-start.6 = (f32[16,16,1]{2,1,0:T(8,128)S(1)}, f32[16,16,1]{2,1,0:T(8,128)S(1)}, u32[]{:S(2)}, u32[]{:S(2)}) collective-permute-start(f32[16,16,1]{2,1,0:T(8,128)S(1)} %get-tuple-element.139), channel_id=1, source_target_pairs={{32,0},{33,1},{34,2},{35,3},{36,4},{37,5},{38,6},{39,7},{40,8},{41... | collective-permute-start | bytes 3080 | tf_op jit(solution)/shard_map/ppermute | solution.py:31
  133.4 4.0 %collective-permute-start.7 = (f32[16,16,1]{2,1,0:T(8,128)S(1)}, f32[16,16,1]{2,1,0:T(8,128)S(1)}, u32[]{:S(2)}, u32[]{:S(2)}) collective-permute-start(f32[16,16,1]{2,1,0:T(8,128)S(1)} %get-tuple-element.140), channel_id=1, source_target_pairs={{0,32},{1,33},{2,34},{3,35},{4,36},{5,37},{6,38},{7,39},{8,40},{9,... | collective-permute-start | bytes 3080 | tf_op jit(solution)/shard_map/ppermute | solution.py:30
  137.8 1.0 copy-start.7
  137.8 1.0 copy-start.9
  137.9 1.1 copy-start.11
  137.9 1.1 copy-start.13
  137.9 1.1 copy-start.15
  (2 other events, 1.4 us)
Sparse Core Ops, SparseCore 0:
  43.1 65.5 all-gather.1
where the time goes:
time: 191 us; the launch traced here: 188 us
  waiting for transfers between devices  52.1 us (27%)
  blocking collectives  49.8 us (26%)
  starting transfers between devices  27.7 us (15%)
  other arithmetic  24.4 us (13%)
  local copies, waits for them, and re-layouts  20 us (10%)
  between operations  14.5 us (8%)
    all_to_all x1, blocking collectives, from_everyone(): return lax.all_to_all(copies, axis, split_axis=0, concat_axis=0, tiled=True)  35.6 us
    all_to_all x1, waiting for transfers between devices, from_everyone(): return lax.all_to_all(copies, axis, split_axis=0, concat_axis=0, tiled=True)  35.3 us
    all_gather x1, waiting for transfers between devices, gathered_by_axis(): value = lax.all_gather(value, axis, axis=dim, tiled=True)  14.2 us
    all_gather x1, blocking collectives, gathered_by_axis(): value = lax.all_gather(value, axis, axis=dim, tiled=True)  14.1 us
    all_to_all x1, starting transfers between devices, from_everyone(): return lax.all_to_all(copies, axis, split_axis=0, concat_axis=0, tiled=True)  10.6 us
    add x16, other arithmetic, apply_local(): source + weight_low * move_rows(source, stride, 0.0)  9.15 us
    ppermute x4, starting transfers between devices, padded_2(): lax.ppermute(last, axis, up)  8.67 us
    ppermute x4, starting transfers between devices, padded_2(): lax.ppermute(first, axis, [(b, a) for a, b in up])  8.46 us
  transfers between devices with their start and end apart: 10, of which 4 were waited for; matrix products, arithmetic and copies ran while one was open for 5% of the time, Pallas kernels for 0%

commit v1 on v0

v1 whole, which is shorter than its diff:
```python
import jax
import jax.numpy as jnp
from jax import lax
from jax.experimental import pallas as pl
from jax.experimental.pallas import tpu as pltpu
from jax.sharding import PartitionSpec as P

coef_z = 1000.0
coef_x = 0.3
coef_y = 0.2
bratu_lambda = 0.2

D = 16
X = 16
Y = 256
L = 128
B = 32
R = 32

XHI, YH, XLO0, OWN15, YOWN, XLO1 = 0, 2, 3, 4, 6, 7
WXM, WXP, WYP = 20, 24, 28


def iota(shape, dim):
    return lax.broadcasted_iota(jnp.int32, shape, dim)


def row_coefficients(level_ref):
    base = lax.axis_index("gz") * D
    last = level_ref.shape[0] - 1

    def spacing(row):
        level = level_ref[jnp.clip(base + row, 0, last)]
        once = jnp.where((level & 1) == 1, jnp.float32(1.3), jnp.float32(1.0))
        twice = jnp.where((level & 2) == 2, jnp.float32(1.3 * 1.3), jnp.float32(1.0))
        return jnp.float32(0.8) * (once * twice)

    around = [spacing(row) for row in range(-1, D + 1)]
    faces = []
    for i in range(D + 1):
        inside = (base + i > 0) & (base + i <= last)
        face = jnp.float32(coef_z * 2.0) / (around[i] + around[i + 1])
        faces.append(jnp.where(inside, face, jnp.float32(0.0)))
    return around[1 : D + 1], faces


def centre_of(spacing, low, high, state):
    return (low + high) + spacing * ((2.0 * coef_x + 2.0 * coef_y) - bratu_lambda * jnp.exp(state))


def transposed(rows):
    short = L - rows.shape[0]
    if short:
        rows = jnp.concatenate([rows, jnp.zeros((short, L), rows.dtype)], 0)
    return jnp.transpose(rows)


def at(k):
    return slice(k * X, (k + 1) * X)


def beside_after_first(face, h_source, h_inv, low, high, h_line):
    value = low
    forwards = []
    for k in range(D - 1):
        rows = slice(k * 8, (k + 1) * 8)
        value = (h_source[rows, :] + face[k] * value) * h_inv[rows, :]
        forwards.append(value)
    value = high
    h_line[(D - 1) * 8 :, :] = value
    for k in range(D - 2, -1, -1):
        rows = slice(k * 8, (k + 1) * 8)
        value = forwards[k] + (face[k + 1] * h_inv[rows, :]) * value
        h_line[rows, :] = value


def own_after_first(face, source, inv, tint, low, high, v_first):
    value = low
    for k in range(D - 1):
        value = (source[at(k), :] + face[k] * value) * inv[at(k), :]
        v_first[at(k), :] = value
    value = high
    for k in range(D - 1, -1, -1):
        if k < D - 1:
            value = v_first[at(k), :] + (face[k + 1] * inv[at(k), :]) * value
        v_first[at(k), :] = jnp.where(tint == 0, value, 0.0)


def beside_sum(v_first, h_line, column, k, left_core):
    row, lane = iota((X, Y), 0), iota((X, Y), 1)
    lines = v_first[at(k), :]
    sides = h_line[k * 8 : (k + 1) * 8, :]
    lo = jnp.concatenate([sides[XLO0 : XLO0 + 1], sides[XLO1 : XLO1 + 1]], 1)
    hi = jnp.concatenate([sides[XHI : XHI + 1], sides[XHI + 1 : XHI + 2]], 1)

    left = jnp.where(lane == 0, jnp.where(left_core, 0.0, column), pltpu.roll(lines, 1, 1))
    right = jnp.where(
        lane == Y - 1, jnp.where(left_core, column, 0.0), pltpu.roll(lines, Y - 1, 1)
    )
    in_x = jnp.where(row == 0, lo, pltpu.roll(lines, 1, 0)) + jnp.where(
        row == X - 1, hi, pltpu.roll(lines, X - 1, 0)
    )
    return coef_x * in_x + coef_y * (left + right)


def pack_x_kernel(corr, res, state, colour, lo, hi):
    for out, edge, inner in ((lo, 0, 1), (hi, X - 1, X - 2)):
        for i, (ref, x) in enumerate(((corr, edge), (corr, inner), (res, edge), (state, edge))):
            for k in range(D):
                out[i * D + k : i * D + k + 1, :] = ref[k * X + x : k * X + x + 1, :]
        row = colour[edge : edge + 1, :].astype(jnp.float32)
        out[4 * D : 4 * D + 8, :] = jnp.broadcast_to(row, (8, Y))


def pack_y_kernel(corr, res, state, colour, after, out):
    left_core = lax.axis_index("gy") == 0

    def columns(value):
        near = jnp.where(left_core, value[:, L:], value[:, :L])
        return jnp.concatenate([transposed(near[i : i + L]) for i in range(0, near.shape[0], L)], 1)

    def picked(turned, inner):
        return jnp.where(left_core, turned[L - 1 - inner : L - inner], turned[inner : inner + 1])

    field = columns(corr[...])
    out[0:1, :] = picked(field, 0)
    out[1:2, :] = picked(field, 1)
    out[2:3, :] = picked(columns(res[...]), 0)
    out[3:4, :] = picked(columns(state[...]), 0)
    row = picked(columns(colour[...].astype(jnp.float32)), 0)
    out[4:8, :] = jnp.broadcast_to(jnp.concatenate([row, row], 1), (4, Y))


def factor_kernel(level, state, inv, e_first, e_last, k_own, w_x, w_y):
    spacing, face = row_coefficients(level)

    def rows(ref, k):
        return ref[k * X : (k + 1) * X, :]

    ratios, forward = [], []
    ratio = running = None
    for k in range(D - 1):
        pivot = centre_of(spacing[k], face[k], face[k + 1], rows(state, k))
        if k:
            pivot = pivot - face[k] * ratio
        inverse = 1.0 / pivot
        scaled = face[k] * inverse
        running = scaled * running if k else scaled
        ratio = face[k + 1] * inverse
        inv[k * X : (k + 1) * X, :] = inverse
        e_first[k * X : (k + 1) * X, :] = running
    inv[(D - 1) * X :, :] = jnp.zeros((X, Y), jnp.float32)
    e_first[(D - 1) * X :, :] = jnp.zeros((X, Y), jnp.float32)
    e_last[(D - 1) * X :, :] = jnp.ones((X, Y), jnp.float32)
    zero, one = jnp.zeros((X, Y), jnp.float32), jnp.ones((X, Y), jnp.float32)
    first, last = zero, one
    wx = [zero, zero, zero, one * (coef_x * spacing[D - 1])]
    wy = [zero, zero, zero, one * (coef_y * spacing[D - 1])]
    for k in range(D - 2, -1, -1):
        ratio = face[k + 1] * rows(inv, k)
        first = rows(e_first, k) + ratio * first
        last = ratio * last
        e_first[k * X : (k + 1) * X, :] = first
        e_last[k * X : (k + 1) * X, :] = last
        if k == D - 2:
            k_own[X : 2 * X, :] = face[D - 1] * first
            centre = centre_of(spacing[D - 1], face[D - 1], face[D], rows(state, D - 1))
            k_own[2 * X :, :] = centre - face[D - 1] * last
        before = (pltpu.roll(first, 1, 0), pltpu.roll(last, 1, 0))
        after = (pltpu.roll(first, Y - 1, 1), pltpu.roll(last, Y - 1, 1))
        for a, mine in enumerate((first, last)):
            in_x, in_y = (coef_x * spacing[k]) * mine, (coef_y * spacing[k]) * mine
            for b in range(2):
                wx[2 * a + b] = wx[2 * a + b] + in_x * before[b]
                wy[2 * a + b] = wy[2 * a + b] + in_y * after[b]
    k_own[:X, :] = face[0] * first
    for i in range(4):
        w_x[i * X : (i + 1) * X, :] = wx[i]
        w_y[i * X : (i + 1) * X, :] = wy[i]


def interface_kernel(
    level, corr, res, colour, inv, e_first, e_last, k_own, w_x, w_y,
    own_lo, own_hi, got_lo, got_hi, own_y, got_y, cross_lo, cross_hi,
    message, source, h_source, h_inv,
    y_scratch, h_state, h_before, h_first, h_last, h_line, v_first,
):
    spacing, face = row_coefficients(level)
    left_core = lax.axis_index("gy") == 0
    has_lo, has_hi = lax.axis_index("gx") > 0, lax.axis_index("gx") < lax.axis_size("gx") - 1
    row = iota((X, Y), 0)
    lane = iota((X, Y), 1)

    def plane(ref, i):
        return ref[i * D : (i + 1) * D, :]

    def spread(ref):
        for k in range(D):
            at = k % 8 * X
            tile = ref[:, k // 8 * L : (k // 8 + 1) * L]
            y_scratch[k * 8 : (k + 1) * 8, :] = pltpu.roll(tile, L - at, 1) if at else tile
        return [y_scratch[pl.ds(q, D, stride=8), :] for q in range(5)]

    yh_corr, yh_next, yh_res, yh_state, yh_colour = spread(got_y)
    yo_corr, unused, unused, yo_state, unused = spread(own_y)
    yh_colour = yh_colour[0:1]

    small_lane = iota((D, L), 1)

    def corner(ref, there):
        value = jnp.where(left_core, ref[:, 0:1], ref[:, Y - 1 : Y])
        return jnp.where(there, value, 0.0)

    corner_lo, corner_hi = corner(cross_lo, has_lo), corner(cross_hi, has_hi)

    h_state[...] = jnp.zeros_like(h_state)
    h_before[...] = jnp.zeros_like(h_before)

    below = jnp.where(small_lane == 0, corner_lo, pltpu.roll(yh_corr, 1, 1))
    above = jnp.where(small_lane == X - 1, corner_hi, pltpu.roll(yh_corr, L - 1, 1))
    yh_source = yh_res + (coef_x * (below + above) + coef_y * (yo_corr + yh_next))
    h_before[pl.ds(YH, D, stride=8), :] = jnp.where(yh_colour == 0.0, yh_source, 0.0)
    h_state[pl.ds(YH, D, stride=8), :] = yh_state
    h_state[pl.ds(YOWN, D, stride=8), :] = yo_state
    beside_corr = []
    row_k = iota((D, Y), 0)
    lane_k = iota((D, Y), 1)
    for got, own, there, at_corner, places in (
        (got_lo, own_lo, has_lo, corner_lo, (XLO0, XLO1)),
        (got_hi, own_hi, has_hi, corner_hi, (XHI, XHI + 1)),
    ):
        near = jnp.where(there, plane(got, 0), 0.0)
        beside_corr.append(near)
        left = jnp.where(lane_k == 0, jnp.where(left_core, 0.0, at_corner), pltpu.roll(near, 1, 1))
        right = jnp.where(
            lane_k == Y - 1, jnp.where(left_core, at_corner, 0.0), pltpu.roll(near, Y - 1, 1)
        )
        value = plane(got, 2) + (coef_x * (plane(got, 1) + plane(own, 0)) + coef_y * (left + right))
        value = jnp.where(there & (got[4 * D : 4 * D + 1, :] == 0.0), value, 0.0)
        states = plane(got, 3)
        for c, place in enumerate(places):
            h_before[pl.ds(place, D, stride=8), :] = value[:, c * L : (c + 1) * L]
            h_state[pl.ds(place, D, stride=8), :] = states[:, c * L : (c + 1) * L]
    edge_state = plane(own_hi, 3)
    for c in range(2):
        h_state[pl.ds(OWN15 + c, D, stride=8), :] = edge_state[:, c * L : (c + 1) * L]

    def rows8(ref, k):
        return ref[k * 8 : (k + 1) * 8, :]

    ratio = running = None
    inverses, forwards = [], []
    for k in range(D - 1):
        pivot = centre_of(spacing[k], face[k], face[k + 1], rows8(h_state, k))
        if k:
            pivot = pivot - face[k] * ratio
        inverse = 1.0 / pivot
        scaled = face[k] * inverse
        running = scaled * running if k else scaled
        ratio = face[k + 1] * inverse
        inverses.append(inverse)
        forwards.append(running)
        h_inv[k * 8 : (k + 1) * 8, :] = inverse
    h_inv[(D - 1) * 8 :, :] = jnp.zeros((8, L), jnp.float32)
    zero, one = jnp.zeros((8, L), jnp.float32), jnp.ones((8, L), jnp.float32)
    place8 = iota((8, L), 0)
    weight = jnp.where((place8 == YOWN) | (place8 == YH), jnp.float32(coef_y), jnp.float32(coef_x))
    first, last = zero, one
    hw = [zero, zero, zero, weight * spacing[D - 1]]
    hs = spacing[D - 1] * rows8(h_before, D - 1)
    h_source[(D - 1) * 8 :, :] = hs
    hf = [zero, hs]
    hk = [None, None, None]
    h_first[(D - 1) * 8 :, :] = zero
    h_last[(D - 1) * 8 :, :] = one * (coef_x * spacing[D - 1])
    for k in range(D - 2, -1, -1):
        ratio = face[k + 1] * inverses[k]
        first = forwards[k] + ratio * first
        last = ratio * last
        if k == D - 2:
            hk[1] = face[D - 1] * first
            centre = centre_of(spacing[D - 1], face[D - 1], face[D], rows8(h_state, D - 1))
            hk[2] = centre - face[D - 1] * last
        hs = spacing[k] * rows8(h_before, k)
        h_source[k * 8 : (k + 1) * 8, :] = hs
        hf[0] = hf[0] + first * hs
        hf[1] = hf[1] + last * hs
        h_first[k * 8 : (k + 1) * 8, :] = (coef_x * spacing[k]) * first
        h_last[k * 8 : (k + 1) * 8, :] = (coef_x * spacing[k]) * last
        partner = (pltpu.roll(first, 4, 0), pltpu.roll(last, 4, 0))
        for a, mine in enumerate((first, last)):
            mine = (weight * spacing[k]) * mine
            for b in range(2):
                hw[2 * a + b] = hw[2 * a + b] + mine * partner[b]
    hk[0] = face[0] * first

    columns = transposed(
        jnp.concatenate(
            [v[YH : YH + 1] for v in hk + hf] + [v[YOWN : YOWN + 1] for v in hw], 0
        )
    )
    columns_corr = transposed(jnp.concatenate([yh_corr, yh_colour], 0))

    mine = colour[...]
    colour_lo, colour_hi = got_lo[4 * D : 4 * D + 1, :], got_hi[4 * D : 4 * D + 1, :]
    tint = mine.astype(jnp.float32)
    tint_y = columns_corr[:X, D : D + 1]
    at_left, at_right = (lane == 0), (lane == Y - 1)

    def beside_of(value, lo, hi, y_column):
        return (
            jnp.where(row == 0, lo, pltpu.roll(value, 1, 0)),
            jnp.where(row == X - 1, hi, pltpu.roll(value, X - 1, 0)),
            jnp.where(at_left, jnp.where(left_core, 0.0, y_column), pltpu.roll(value, 1, 1)),
            jnp.where(at_right, jnp.where(left_core, y_column, 0.0), pltpu.roll(value, Y - 1, 1)),
        )

    weights = [
        jnp.where((tint == 1.0) & (other == 0.0), 0.0, jnp.float32(amount))
        for other, amount in zip(
            beside_of(tint, colour_lo, colour_hi, tint_y), (coef_x, coef_x, coef_y, coef_y)
        )
    ]
    for k in range(D):
        value = corr[k * X : (k + 1) * X, :]
        around = beside_of(
            value, beside_corr[0][k : k + 1], beside_corr[1][k : k + 1], columns_corr[:X, k : k + 1]
        )
        total = res[k * X : (k + 1) * X, :]
        for w, v in zip(weights, around):
            total = total + w * v
        source[at(k), :] = spacing[k] * total

    beside_after_first(face, h_source, h_inv, zero, zero, h_line)
    still = jnp.zeros((X, Y), jnp.float32)
    own_after_first(face, source, inv, mine, still, still, v_first)
    columns_first = transposed(h_line[pl.ds(YH, D, stride=8), :])
    f_first = f_last = still
    for k in range(D):
        added = beside_sum(v_first, h_line, columns_first[:X, k : k + 1], k, left_core)
        total = source[at(k), :] + jnp.where(mine == 1, spacing[k] * added, 0.0)
        f_first = f_first + e_first[at(k), :] * total
        f_last = f_last + e_last[at(k), :] * total

    def put(r, half, value):
        message[pl.ds(half * R + r, X, stride=2 * R), :] = value

    def put_both(r, value):
        put(r, 0, value[:, :L])
        put(r, 1, value[:, L:])

    short_lane = iota((X, L), 1)
    own_values = [k_own[i * X : (i + 1) * X, :] for i in range(3)] + [f_first, f_last]
    seen_values = own_values[:3] + [jnp.where(tint == 0.0, f, still) for f in own_values[3:]]
    inner_link = [w_y[i * X : (i + 1) * X, :][:, L - 1 : L] for i in (0, 2, 1, 3)]
    for q in range(5):
        own, seen = own_values[q], seen_values[q]
        side = (hk + hf)[q]
        put_both(4 * q, own)
        low = jnp.concatenate([side[XLO0 : XLO0 + 1], side[XLO1 : XLO1 + 1]], 1)
        high = jnp.concatenate([side[XHI : XHI + 1], side[XHI + 1 : XHI + 2]], 1)
        put_both(4 * q + 1, jnp.where(row == 0, low, pltpu.roll(seen, 1, 0)))
        put_both(4 * q + 2, jnp.where(row == X - 1, high, pltpu.roll(seen, X - 1, 0)))
        outer = columns[:X, q : q + 1]
        left_end, right_end = seen[:, L:], seen[:, :L]
        left_none, right_none = (0.0, 0.0) if q >= 3 else (left_end, right_end)
        left_end = jnp.where(
            short_lane == L - 1, jnp.where(left_core, left_none, outer), left_end
        )
        right_end = jnp.where(short_lane == 0, jnp.where(left_core, outer, right_none), right_end)
        if q < 4:
            link = columns[:X, 5 + q : 6 + q]
            left_end = jnp.where(short_lane == L // 2, jnp.where(left_core, 0.0, link), left_end)
            right_end = jnp.where(short_lane == L // 2, inner_link[q], right_end)
        put(4 * q + 3, 0, left_end)
        put(4 * q + 3, 1, right_end)

    edge_first, edge_last = (
        jnp.concatenate([e[k * X : k * X + 1, :] for k in range(D)], 0) for e in (e_first, e_last)
    )
    low_first = jnp.concatenate([h_first[pl.ds(p, D, stride=8), :] for p in (XLO0, XLO1)], 1)
    low_last = jnp.concatenate([h_last[pl.ds(p, D, stride=8), :] for p in (XLO0, XLO1)], 1)
    for a, mine_e in enumerate((edge_first, edge_last)):
        for b, other_e in enumerate((low_first, low_last)):
            i, j = 2 * a + b, 2 * b + a
            edge = jnp.sum(mine_e * other_e, axis=0, keepdims=True)
            put_both(WXM + i, jnp.where(row == 0, edge, w_x[i * X : (i + 1) * X, :]))
            high = jnp.concatenate([hw[i][OWN15 : OWN15 + 1], hw[i][OWN15 + 1 : OWN15 + 2]], 1)
            turned = pltpu.roll(w_x[j * X : (j + 1) * X, :], X - 1, 0)
            put_both(WXP + i, jnp.where(row == X - 1, high, turned))
            link = jnp.where(left_core, columns[:X, 5 + i : 6 + i], 0.0)
            put_both(WYP + i, jnp.where(at_right, link, w_y[i * X : (i + 1) * X, :]))


def separator_kernel(got, colour, out, v_scratch, line_scratch):
    patch = lax.axis_index("gz")
    tint = colour[pl.ds(patch // 2, 1), :]
    tint = jnp.where(patch % 2 == 0, tint[:, :L], tint[:, L:])

    def quantity(q, d):
        return got[d * R + 4 * q : d * R + 4 * q + 4, :]

    off = [quantity(1, d) for d in range(B)]
    diag = [
        quantity(2, d) - quantity(0, d + 1) if d < B - 1 else quantity(2, d) for d in range(B)
    ]
    right = [
        quantity(4, d) + quantity(3, d + 1) if d < B - 1 else quantity(4, d) for d in range(B)
    ]
    middle = B // 2
    up, down = {}, {}
    for n in range(middle):
        d = n
        pivot = diag[d] - off[d] * up[d - 1][1] if n else diag[d]
        inverse = 1.0 / pivot
        up[d] = (inverse, off[d + 1] * inverse)
        d = B - 1 - n
        if d > middle:
            pivot = diag[d] - off[d + 1] * down[d + 1][1] if n else diag[d]
            inverse = 1.0 / pivot
            down[d] = (inverse, off[d] * inverse)
    centre = diag[middle] - off[middle] * up[middle - 1][1] - off[middle + 1] * down[middle + 1][1]
    centre = 1.0 / centre

    def solved(right, sets):
        def cut(value):
            return value[:sets]

        ahead, behind, values = {}, {}, [None] * B
        for n in range(middle):
            d = n
            total = right[d] + cut(off[d]) * ahead[d - 1] if n else right[d]
            ahead[d] = total * cut(up[d][0])
            d = B - 1 - n
            if d > middle:
                total = right[d] + cut(off[d + 1]) * behind[d + 1] if n else right[d]
                behind[d] = total * cut(down[d][0])
        total = (
            right[middle]
            + cut(off[middle]) * ahead[middle - 1]
            + cut(off[middle + 1]) * behind[middle + 1]
        )
        values[middle] = total * cut(centre)
        for n in range(middle):
            d = middle - 1 - n
            values[d] = ahead[d] + cut(up[d][1]) * values[d + 1]
            d = middle + 1 + n
            if d < B:
                values[d] = behind[d] + cut(down[d][1]) * values[d - 1]
        return values

    v_scratch[0:4, :] = jnp.zeros((4, L), jnp.float32)
    for d, value in enumerate(solved(right, 4)):
        v_scratch[4 + d * 4 : 8 + d * 4, :] = value

    lane = iota((B, L), 1)

    def of_set(s):
        return v_scratch[pl.ds(s, B, stride=4), :], v_scratch[pl.ds(4 + s, B, stride=4), :]

    def lines(r):
        return got[pl.ds(r, B, stride=R), :]

    own_pair, lo_pair, hi_pair, end_pair = (of_set(s) for s in range(4))
    first_pair = [jnp.where(tint == 0, v, 0.0) for v in own_pair]
    left_pair = [
        jnp.where(lane == 0, pltpu.roll(e, 1, 1), pltpu.roll(v, 1, 1))
        for e, v in zip(end_pair, first_pair)
    ]
    right_pair = [
        jnp.where(lane == L - 1, pltpu.roll(e, L - 1, 1), pltpu.roll(v, L - 1, 1))
        for e, v in zip(end_pair, first_pair)
    ]
    added = []
    for a in range(2):
        total = jnp.zeros((B, L), jnp.float32)
        for b in range(2):
            i, j = 2 * a + b, 2 * b + a
            total = total + lines(WXM + i) * lo_pair[b]
            total = total + lines(WXP + i) * hi_pair[b]
            total = total + lines(WYP + i) * right_pair[b]
            back = jnp.where(
                lane == 0, pltpu.roll(lines(4 * i + 3), L // 2, 1), pltpu.roll(lines(WYP + j), 1, 1)
            )
            total = total + back * left_pair[b]
        added.append(jnp.where(tint == 1, total, 0.0) + lines(12 + 4 * a))
    line_scratch[0:B, :] = added[0]
    line_scratch[B : B + 8, :] = jnp.zeros((8, L), jnp.float32)
    line_scratch[0:B, :] = added[1] + line_scratch[1 : B + 1, :]
    second = [line_scratch[d : d + 1, :] for d in range(B)]
    values = solved(second, 1)
    line_scratch[0:1, :] = jnp.zeros((1, L), jnp.float32)
    for d in range(B):
        line_scratch[d + 1 : d + 2, :] = values[d]
    results = [line_scratch[0:B, :], line_scratch[1 : B + 1, :]]
    results += [*lo_pair, *hi_pair, *end_pair]
    for i, value in enumerate(results):
        out[pl.ds(i, B, stride=8), :] = value


def finish_kernel(level, source, inv, h_source, h_inv, colour, got, out, v_first, h_line):
    spacing, face = row_coefficients(level)
    left_core = lax.axis_index("gy") == 0
    mine = colour[...]

    def own(i):
        return jnp.concatenate([got[pl.ds(h * 8 + i, X, stride=16), :] for h in range(2)], 1)

    low, high = own(0), own(1)
    ends = []
    for i in (6, 7):
        near = got[pl.ds(8 + i, X, stride=16), :]
        far = pltpu.roll(got[pl.ds(i, X, stride=16), :], 1, 1)
        ends.append(jnp.where(left_core, near, far)[:, 0:1])
    short_lane = iota((X, L), 1)
    pair = jnp.where(short_lane == 0, ends[0], ends[1])
    turned = transposed(pair)
    nothing = jnp.zeros((1, L), jnp.float32)

    def beside(b):
        at = {XHI: 30 * 8 + 4, XHI + 1: 31 * 8 + 4, XLO0: 2, XLO1: 8 + 2}
        rows = [
            turned[b : b + 1]
            if p == YH
            else got[at[p] + b : at[p] + b + 1, :]
            if p in at
            else nothing
            for p in range(8)
        ]
        return jnp.concatenate(rows, 0)

    beside_after_first(face, h_source, h_inv, beside(0), beside(1), h_line)
    columns = transposed(h_line[pl.ds(YH, D, stride=8), :])
    own_after_first(face, source, inv, mine, low, high, v_first)
    value = low
    for k in range(D - 1):
        added = beside_sum(v_first, h_line, columns[:X, k : k + 1], k, left_core)
        value = (source[at(k), :] + spacing[k] * added + face[k] * value) * inv[at(k), :]
        out[at(k), :] = value
    value = high
    for k in range(D - 1, -1, -1):
        if k < D - 1:
            value = out[at(k), :] + (face[k + 1] * inv[at(k), :]) * value
        out[at(k), :] = jnp.where(mine == 0, v_first[at(k), :], value)


VMEM = pl.BlockSpec(memory_space=pltpu.VMEM)
SMEM = pl.BlockSpec(memory_space=pltpu.SMEM)


def f32(*shape):
    return jax.ShapeDtypeStruct(shape, jnp.float32)


def call(kernel, outs, specs, scratch, cost, *args):
    return pl.pallas_call(
        kernel,
        out_shape=outs,
        in_specs=specs,
        out_specs=jax.tree.map(lambda _: VMEM, outs),
        scratch_shapes=[pltpu.VMEM(shape, jnp.float32) for shape in scratch],
        compiler_params=pltpu.CompilerParams(vmem_limit_bytes=32 * 1024 * 1024),
        cost_estimate=pl.CostEstimate(flops=cost, bytes_accessed=cost, transcendentals=0),
    )(*args)


def on_device(correction, residual, state, level, colour):
    corr, res, st = (v.reshape(D * X, Y) for v in (correction, residual, state))
    own_lo, own_hi = call(
        pack_x_kernel, (f32(72, Y), f32(72, Y)), [VMEM] * 4, [], 1 << 20, corr, res, st, colour
    )
    xs = lax.axis_size("gx")
    ring = [(i, (i + 1) % xs) for i in range(xs)]
    got_lo = lax.ppermute(own_hi, "gx", ring)
    got_hi = lax.ppermute(own_lo, "gx", [(b, a) for a, b in ring])
    own_y = call(
        pack_y_kernel, f32(8, Y), [VMEM] * 4 + [pl.BlockSpec(memory_space=pl.ANY)], [],
        1 << 20, corr, res, st, colour, own_lo,
    )
    swap = [(0, 1), (1, 0)]
    got_y = lax.ppermute(own_y, "gy", swap)
    field = f32(D * X, Y)
    inv, e_first, e_last, k_own, w_x, w_y = call(
        factor_kernel, (field, field, field, f32(3 * X, Y), f32(4 * X, Y), f32(4 * X, Y)),
        [SMEM, VMEM], [], 1 << 22, level, st,
    )
    cross_lo = lax.ppermute(got_lo[:D], "gy", swap)
    cross_hi = lax.ppermute(got_hi[:D], "gy", swap)
    message, source, h_source, h_inv = call(
        interface_kernel, (f32(B * R, L), field, f32(8 * D, L), f32(8 * D, L)),
        [SMEM] + [VMEM] * 17, [(8 * D, L)] * 6 + [(D * X, Y)], 1 << 22,
        level, corr, res, colour, inv, e_first, e_last, k_own, w_x, w_y,
        own_lo, own_hi, got_lo, got_hi, own_y, got_y, cross_lo, cross_hi,
    )

    def exchanged(value, rows):
        blocks = value.reshape(B, rows, L)
        return lax.all_to_all(blocks, "gz", 0, 0, tiled=True).reshape(B * rows, L)

    separators = call(
        separator_kernel, f32(B * 8, L), [VMEM] * 2, [(4 * B + 8, L), (B + 8, L)],
        1 << 21, exchanged(message, R), colour,
    )
    out = call(
        finish_kernel, field, [SMEM] + [VMEM] * 6, [(D * X, Y), (8 * D, L)], 1 << 21,
        level, source, inv, h_source, h_inv, colour, exchanged(separators, 8),
    )
    return out.reshape(D, X, Y)


def solution(mesh):
    block = P("gz", "gx", "gy")
    return jax.shard_map(
        on_device,
        mesh=mesh,
        in_specs=(block, block, block, P(), P("gx", "gy")),
        out_specs=block,
        check_vma=False,
    )
```

time: 191 us -> 60.9 us (0.32); the launches traced: 188 us -> 60.6 us
  waiting for transfers between devices: 52.1 us -> 5.56 us
  starting transfers between devices: 27.7 us -> 2.86 us
  other arithmetic: 24.4 us -> 0 us
  local copies, waits for them, and re-layouts: 20 us -> 3.73 us
  between operations: 14.5 us -> 0.11 us
  blocking collectives: 49.8 us -> 42.5 us
  Pallas kernels: 0 us -> 5.88 us
    all_to_all x1 -> x0, waiting for transfers between devices: 35.3 us -> none  [from_everyone(): return lax.all_to_all(copies, axis, split_axis=0, concat_axis=0, tiled=True)]
    slice x62 -> x2, local copies, waits for them, and re-layouts: 14.9 us -> 0.01 us  [the longest x1 0.01 us: on_device(): cross_lo = lax.ppermute(got_lo[:D], 'gy', swap)]
    ppermute x8 -> x5, starting transfers between devices: 17.1 us -> 2.86 us  [the longest x1 2.29 us: on_device(): got_lo = lax.ppermute(own_hi, 'gx', ring)]
    all_gather x1 -> x0, waiting for transfers between devices: 14.2 us -> none  [gathered_by_axis(): value = lax.all_gather(value, axis, axis=dim, tiled=True)]
    all_gather x1 -> x0, blocking collectives: 14.1 us -> none  [gathered_by_axis(): value = lax.all_gather(value, axis, axis=dim, tiled=True)]
    add x24 -> x0, other arithmetic: 13.8 us -> none  [the longest x16 9.15 us: apply_local(): source + weight_low * move_rows(source, stride, 0.0)]
    all_to_all x1 -> x0, starting transfers between devices: 10.6 us -> none  [from_everyone(): return lax.all_to_all(copies, axis, split_axis=0, concat_axis=0, tiled=True)]
    all_to_all x1 -> x2, blocking collectives: 35.6 us -> 42.5 us  [exchanged(): return lax.all_to_all(blocks, 'gz', 0, 0, tiled=True).reshape(B * rows, L)]
  transfers between devices with their start and end apart: 10 -> 5, of which waited for: 4 -> 2; matrix products, arithmetic and copies ran while one was open for 5% -> 0% of each run, Pallas kernels for 0% -> 2%
where the time goes in v1:
time: 60.9 us; the launch traced here: 60.6 us
  blocking collectives  42.5 us (70%)
  Pallas kernels  5.88 us (10%)
  waiting for transfers between devices  5.56 us (9%)
  local copies, waits for them, and re-layouts  3.73 us (6%)
  starting transfers between devices  2.86 us (5%)
    all_to_all x2, blocking collectives, exchanged(): return lax.all_to_all(blocks, 'gz', 0, 0, tiled=True).reshape(B * rows, L)  42.5 us
    pallas_call x6, Pallas kernels, call(): pl.pallas_call(kernel, out_shape=outs, in_specs=specs, out_specs=jax.tree...  5.88 us
    unnamed x18, local copies, waits for them, and re-layouts  3.73 us
    ppermute x1, waiting for transfers between devices, on_device(): got_hi = lax.ppermute(own_lo, 'gx', [(b, a) for a, b in ring])  3.42 us
    ppermute x1, starting transfers between devices, on_device(): got_lo = lax.ppermute(own_hi, 'gx', ring)  2.29 us
    ppermute x1, waiting for transfers between devices, on_device(): got_lo = lax.ppermute(own_hi, 'gx', ring)  2.14 us
  transfers between devices with their start and end apart: 5, of which 2 were waited for; matrix products, arithmetic and copies ran while one was open for 0% of the time, Pallas kernels for 2%

profile of v1, /device:TPU:6, one launch (start us, length us, event | category | flops | bytes accessed | tf_op | source)
XLA Modules:
  0.0 60.6 jit_solution(7147440506914719268)
XLA Ops:
  0.0 0.0 copy-start
  0.0 0.9 %copy-done = f32[16,16,256]{2,1,0:T(8,128)S(1)} copy-done((f32[16,16,256]{2,1,0:T(8,128)S(1)}, f32[16,16,256]{2,1,0:T(8,128)}, u32[]{:S(2)}) %copy-start) | copy-done | bytes 262168
  1.0 0.0 copy-start.2
  1.0 0.9 %copy-done.2 = f32[16,16,256]{2,1,0:T(8,128)S(1)} copy-done((f32[16,16,256]{2,1,0:T(8,128)S(1)}, f32[16,16,256]{2,1,0:T(8,128)}, u32[]{:S(2)}) %copy-start.2) | copy-done | bytes 262168
  1.9 0.9 %copy-done.4 = f32[16,16,256]{2,1,0:T(8,128)S(1)} copy-done((f32[16,16,256]{2,1,0:T(8,128)S(1)}, f32[16,16,256]{2,1,0:T(8,128)}, u32[]{:S(2)}) %copy-start.4) | copy-done | bytes 262168
  2.9 0.7 %copy-done.6 = s32[16,256]{1,0:T(8,128)S(1)} copy-done((s32[16,256]{1,0:T(8,128)S(1)}, s32[16,256]{1,0:T(8,128)}, u32[]{:S(2)}) %copy-start.6) | copy-done | bytes 16408
  3.6 0.1 shard_map.56
  3.6 2.3 %collective-permute-start = (f32[72,256]{1,0:T(8,128)S(1)}, f32[72,256]{1,0:T(8,128)S(1)}, u32[]{:S(2)}, u32[]{:S(2)}) collective-permute-start(f32[72,256]{1,0:T(8,128)S(1)} %get-tuple-element.24.own_hi), channel_id=1, source_target_pairs={{0,64},{64,128},{128,192},{192,0},{1,65},{65,129},{129,193},{193,1... | collective-permute-start | bytes 221192 | tf_op jit(solution)/shard_map/ppermute | solution.py:574
  5.9 0.0 collective-permute-start.1
  5.9 2.1 %collective-permute-done.got_lo = f32[72,256]{1,0:T(8,128)S(1)} collective-permute-done((f32[72,256]{1,0:T(8,128)S(1)}, f32[72,256]{1,0:T(8,128)S(1)}, u32[]{:S(2)}, u32[]{:S(2)}) %collective-permute-start) | collective-permute-done | bytes 73760 | tf_op jit(solution)/shard_map/ppermute | solution.py:574
  8.1 0.0 collective-permute-start.3
  8.1 3.4 %collective-permute-done.1.got_hi = f32[72,256]{1,0:T(8,128)S(1)} collective-permute-done((f32[72,256]{1,0:T(8,128)S(1)}, f32[72,256]{1,0:T(8,128)S(1)}, u32[]{:S(2)}, u32[]{:S(2)}) %collective-permute-start.1) | collective-permute-done | bytes 73760 | tf_op jit(solution)/shard_map/ppermute | solution.py:575
  11.5 0.0 collective-permute-start.4
  11.5 0.0 copy-start.5
  11.5 0.0 copy-start.7
  11.5 0.2 shard_map.57.own_y
  11.7 0.0 copy-start.3
  11.8 0.6 collective-permute-start.2
  12.3 0.1 copy-done.1
  12.5 0.0 copy-done.8
  12.5 1.1 %shard_map.55 = (f32[256,256]{1,0:T(8,128)S(1)}, f32[256,256]{1,0:T(8,128)S(1)}, f32[256,256]{1,0:T(8,128)S(1)}, f32[48,256]{1,0:T(8,128)S(1)}, f32[64,256]{1,0:T(8,128)S(1)}, /*index=5*/f32[64,256]{1,0:T(8,128)S(1)}) custom-call(s32[512]{0:T(512)S(1)} %copy-done.8, f32[256,256]{1,0:T(8,128)S(1)} %bitcast.10), custom_call_target="tpu_custom_call" | custom-call | flops 4194304 | bytes 4194304 | tf_op jit(solution)/shard_map/pallas_call | solution.py:556
  13.5 0.0 collective-permute-done.2.got_y
  13.5 0.0 collective-permute-done.3.cross_lo
  13.6 0.0 collective-permute-done.4.cross_hi
  13.6 0.0 copy-done.5
  13.6 0.0 copy-done.7
  13.6 0.0 copy-done.3
  13.6 2.1 %shard_map.58 = (f32[1024,128]{1,0:T(8,128)S(1)}, f32[256,256]{1,0:T(8,128)S(1)}, f32[128,128]{1,0:T(8,128)S(1)}, f32[128,128]{1,0:T(8,128)S(1)}) custom-call(s32[512]{0:T(512)S(1)} %copy-done.8, f32[256,256]{1,0:T(8,128)S(1)} %bitcast.13, f32[256,256]{1,0:T(8,128)S(1)} %bitcast.16, s32[16,256]{1,0:T(8,128)S(1)} %copy-done.7, ...), custom_call_target="tpu_custom_call" | custom-call | flops 4194304 | bytes 4194304 | tf_op jit(solution)/shard_map/pallas_call | solution.py:556
  15.7 27.4 %all_to_all.10 = f32[32,32,128]{2,1,0:T(8,128)S(1)} all-to-all(f32[32,32,128]{2,1,0:T(8,128)S(1)} %bitcast.18), channel_id=1, replica_groups=mesh['gx'=4,'gy'=2,'gz'=32] {'gz'}, dimensions={0} | all-to-all | bytes 1048576 | tf_op jit(solution)/shard_map/all_to_all | solution.py:598
  43.1 0.5 shard_map.59
  43.5 15.1 %all_to_all.11 = f32[32,8,128]{2,1,0:T(8,128)S(1)} all-to-all(f32[32,8,128]{2,1,0:T(8,128)S(1)} %bitcast.19), channel_id=1, replica_groups=mesh['gx'=4,'gy'=2,'gz'=32] {'gz'}, dimensions={0} | all-to-all | bytes 262144 | tf_op jit(solution)/shard_map/all_to_all | solution.py:598
  58.6 2.0 %shard_map.60 = f32[256,256]{1,0:T(8,128)} custom-call(s32[512]{0:T(512)S(1)} %copy-done.8, f32[256,256]{1,0:T(8,128)S(1)} %get-tuple-element.25.source, f32[256,256]{1,0:T(8,128)S(1)} %get-tuple-element.17.inv, f32[128,128]{1,0:T(8,128)S(1)} %get-tuple-element.26.h_source, f32[128,128]{1,0:T(8,128)S(1)} %get-tuple-element.27.h_inv, ...), custom_call_target="tpu_custom_call" | custom-call | flops 2097152 | bytes 2097152 | tf_op jit(solution)/shard_map/pallas_call | solution.py:556
  (6 shorter events, 0.0 us)
Async XLA Ops:
  0.0 0.9 %copy-start = (f32[16,16,256]{2,1,0:T(8,128)S(1)}, f32[16,16,256]{2,1,0:T(8,128)}, u32[]{:S(2)}) copy-start(f32[16,16,256]{2,1,0:T(8,128)} %param.7) | copy-start | bytes 786436
  1.0 0.9 %copy-start.2 = (f32[16,16,256]{2,1,0:T(8,128)S(1)}, f32[16,16,256]{2,1,0:T(8,128)}, u32[]{:S(2)}) copy-start(f32[16,16,256]{2,1,0:T(8,128)} %param.5) | copy-start | bytes 786436
  1.9 0.9 %copy-start.4 = (f32[16,16,256]{2,1,0:T(8,128)S(1)}, f32[16,16,256]{2,1,0:T(8,128)}, u32[]{:S(2)}) copy-start(f32[16,16,256]{2,1,0:T(8,128)} %param.6) | copy-start | bytes 786436
  2.9 0.7 %copy-start.6 = (s32[16,256]{1,0:T(8,128)S(1)}, s32[16,256]{1,0:T(8,128)}, u32[]{:S(2)}) copy-start(s32[16,256]{1,0:T(8,128)} %colour.9) | copy-start | bytes 49156
  3.6 4.4 %collective-permute-start = (f32[72,256]{1,0:T(8,128)S(1)}, f32[72,256]{1,0:T(8,128)S(1)}, u32[]{:S(2)}, u32[]{:S(2)}) collective-permute-start(f32[72,256]{1,0:T(8,128)S(1)} %get-tuple-element.24.own_hi), channel_id=1, source_target_pairs={{0,64},{64,128},{128,192},{192,0},{1,65},{65,129},{129,193},{193,1... | collective-permute-start | bytes 221192 | tf_op jit(solution)/shard_map/ppermute | solution.py:574
  5.9 5.6 %collective-permute-start.1 = (f32[72,256]{1,0:T(8,128)S(1)}, f32[72,256]{1,0:T(8,128)S(1)}, u32[]{:S(2)}, u32[]{:S(2)}) collective-permute-start(f32[72,256]{1,0:T(8,128)S(1)} %get-tuple-element.23.after.own_lo), channel_id=1, source_target_pairs={{64,0},{128,64},{192,128},{0,192},{65,1},{129,65},{193,129},{1,193... | collective-permute-start | bytes 221192 | tf_op jit(solution)/shard_map/ppermute | solution.py:575
  8.1 5.5 %collective-permute-start.3 = (f32[16,256]{1,0:T(8,128)S(1)}, f32[16,256]{1,0:T(8,128)S(1)}, u32[]{:S(2)}, u32[]{:S(2)}) collective-permute-start(f32[16,256]{1,0:T(8,128)S(1)} %slice.8), channel_id=1, source_target_pairs={{0,32},{32,0},{1,33},{33,1},{2,34},{34,2},{3,35},{35,3},{4,36},{36... | collective-permute-start | bytes 49160 | tf_op jit(solution)/shard_map/ppermute | solution.py:587
  11.5 1.0 %copy-start.1 = (f32[16,16,256]{2,1,0:T(8,128)S(1)}, f32[16,16,256]{2,1,0:T(8,128)}, u32[]{:S(2)}) copy-start(f32[16,16,256]{2,1,0:T(8,128)} %param.7) | copy-start | bytes 786436
  11.5 1.0 %copy-start.8 = (s32[512]{0:T(512)S(1)}, s32[512]{0:T(512)}, u32[]{:S(2)}) copy-start(s32[512]{0:T(512)} %level.5) | copy-start | bytes 6148
  11.5 2.0 %collective-permute-start.4 = (f32[16,256]{1,0:T(8,128)S(1)}, f32[16,256]{1,0:T(8,128)S(1)}, u32[]{:S(2)}, u32[]{:S(2)}) collective-permute-start(f32[16,256]{1,0:T(8,128)S(1)} %slice.9), channel_id=1, source_target_pairs={{0,32},{32,0},{1,33},{33,1},{2,34},{34,2},{3,35},{35,3},{4,36},{36... | collective-permute-start | bytes 49160 | tf_op jit(solution)/shard_map/ppermute | solution.py:588
  11.5 2.0 %copy-start.5 = (f32[16,16,256]{2,1,0:T(8,128)S(1)}, f32[16,16,256]{2,1,0:T(8,128)}, u32[]{:S(2)}) copy-start(f32[16,16,256]{2,1,0:T(8,128)} %param.6) | copy-start | bytes 786436
  11.5 2.0 %copy-start.7 = (s32[16,256]{1,0:T(8,128)S(1)}, s32[16,256]{1,0:T(8,128)}, u32[]{:S(2)}) copy-start(s32[16,256]{1,0:T(8,128)} %colour.9) | copy-start | bytes 49156
  11.7 1.8 %copy-start.3 = (f32[16,16,256]{2,1,0:T(8,128)S(1)}, f32[16,16,256]{2,1,0:T(8,128)}, u32[]{:S(2)}) copy-start(f32[16,16,256]{2,1,0:T(8,128)} %param.5) | copy-start | bytes 786436
  11.8 1.8 %collective-permute-start.2 = (f32[8,256]{1,0:T(8,128)S(1)}, f32[8,256]{1,0:T(8,128)S(1)}, u32[]{:S(2)}, u32[]{:S(2)}) collective-permute-start(f32[8,256]{1,0:T(8,128)S(1)} %shard_map.57.own_y), channel_id=1, source_target_pairs={{0,32},{32,0},{1,33},{33,1},{2,34},{34,2},{3,35},{35,3},{4,36},{36... | collective-permute-start | bytes 24584 | tf_op jit(solution)/shard_map/ppermute | solution.py:581

commit v2 on v1

--- a/solution.py
+++ b/solution.py
@@ -103,16 +103,23 @@
     return coef_x * in_x + coef_y * (left + right)
 
 
-def pack_x_kernel(corr, res, state, colour, lo, hi):
+def pack_x_kernel(corr, res, state, colour, lo, hi, tint, arrived):
+    copies = []
     for out, edge, inner in ((lo, 0, 1), (hi, X - 1, X - 2)):
         for i, (ref, x) in enumerate(((corr, edge), (corr, inner), (res, edge), (state, edge))):
-            for k in range(D):
-                out[i * D + k : i * D + k + 1, :] = ref[k * X + x : k * X + x + 1, :]
-        row = colour[edge : edge + 1, :].astype(jnp.float32)
+            rows = out.at[pl.ds(i * D, D), :]
+            copies.append(pltpu.make_async_copy(ref.at[:, x, :], rows, arrived.at[len(copies)]))
+    copies.append(pltpu.make_async_copy(colour, tint, arrived.at[len(copies)]))
+    for copy in copies:
+        copy.start()
+    for copy in copies:
+        copy.wait()
+    for out, edge in ((lo, 0), (hi, X - 1)):
+        row = tint[edge : edge + 1, :].astype(jnp.float32)
         out[4 * D : 4 * D + 8, :] = jnp.broadcast_to(row, (8, Y))
 
 
-def pack_y_kernel(corr, res, state, colour, after, out):
+def pack_y_kernel(corr, res, state, colour, out):
     left_core = lax.axis_index("gy") == 0
 
     def columns(value):
@@ -545,6 +552,7 @@
 
 
 VMEM = pl.BlockSpec(memory_space=pltpu.VMEM)
+ANY = pl.BlockSpec(memory_space=pl.ANY)
 SMEM = pl.BlockSpec(memory_space=pltpu.SMEM)
 
 
@@ -552,14 +560,16 @@
     return jax.ShapeDtypeStruct(shape, jnp.float32)
 
 
-def call(kernel, outs, specs, scratch, cost, *args):
+def call(kernel, outs, specs, scratch, cost, *args, vmem=32):
     return pl.pallas_call(
         kernel,
         out_shape=outs,
         in_specs=specs,
         out_specs=jax.tree.map(lambda _: VMEM, outs),
-        scratch_shapes=[pltpu.VMEM(shape, jnp.float32) for shape in scratch],
-        compiler_params=pltpu.CompilerParams(vmem_limit_bytes=32 * 1024 * 1024),
+        scratch_shapes=[
+            pltpu.VMEM(s, jnp.float32) if isinstance(s, tuple) else s for s in scratch
+        ],
+        compiler_params=pltpu.CompilerParams(vmem_limit_bytes=vmem * 1024 * 1024),
         cost_estimate=pl.CostEstimate(flops=cost, bytes_accessed=cost, transcendentals=0),
     )(*args)
 
@@ -567,15 +577,16 @@
 def on_device(correction, residual, state, level, colour):
     corr, res, st = (v.reshape(D * X, Y) for v in (correction, residual, state))
     own_lo, own_hi = call(
-        pack_x_kernel, (f32(72, Y), f32(72, Y)), [VMEM] * 4, [], 1 << 20, corr, res, st, colour
+        pack_x_kernel, (f32(72, Y), f32(72, Y)), [ANY] * 4,
+        [pltpu.VMEM((X, Y), jnp.int32), pltpu.SemaphoreType.DMA((9,))],
+        1 << 20, correction, residual, state, colour, vmem=60,
     )
     xs = lax.axis_size("gx")
     ring = [(i, (i + 1) % xs) for i in range(xs)]
     got_lo = lax.ppermute(own_hi, "gx", ring)
     got_hi = lax.ppermute(own_lo, "gx", [(b, a) for a, b in ring])
     own_y = call(
-        pack_y_kernel, f32(8, Y), [VMEM] * 4 + [pl.BlockSpec(memory_space=pl.ANY)], [],
-        1 << 20, corr, res, st, colour, own_lo,
+        pack_y_kernel, f32(8, Y), [VMEM] * 4, [], 1 << 20, corr, res, st, colour
     )
     swap = [(0, 1), (1, 0)]
     got_y = lax.ppermute(own_y, "gy", swap)
@@ -584,6 +595,7 @@
         factor_kernel, (field, field, field, f32(3 * X, Y), f32(4 * X, Y), f32(4 * X, Y)),
         [SMEM, VMEM], [], 1 << 22, level, st,
     )
+    got_lo, got_hi, inv, own_y = lax.optimization_barrier((got_lo, got_hi, inv, own_y))
     cross_lo = lax.ppermute(got_lo[:D], "gy", swap)
     cross_hi = lax.ppermute(got_hi[:D], "gy", swap)
     message, source, h_source, h_inv = call(

time: 60.9 us -> 58.9 us (0.967)
  local copies, waits for them, and re-layouts: 3.73 us -> 0.51 us
  Pallas kernels: 5.88 us -> 7.41 us
    unnamed x18 -> x14, local copies, waits for them, and re-layouts: 3.73 us -> 0.5 us
    ppermute x1, waiting for transfers between devices: 2.14 us -> 0.55 us  [on_device(): got_lo = lax.ppermute(own_hi, 'gx', ring)]
    pallas_call x6, Pallas kernels: 5.88 us -> 7.41 us  [call(): pl.pallas_call(kernel, out_shape=outs, in_specs=specs, out_specs=jax.tree...]
    ppermute x1, waiting for transfers between devices: 0.01 us -> 1.08 us  [on_device(): got_y = lax.ppermute(own_y, 'gy', swap)]
  transfers between devices with their start and end apart: 5 -> 5, of which waited for: 2 -> 3; matrix products, arithmetic and copies ran while one was open for 0% -> 0% of each run, Pallas kernels for 2% -> 2%
where the time goes in v2:
time: 58.9 us; the launch traced here: 58.7 us
  blocking collectives  42.7 us (72%)
  Pallas kernels  7.41 us (13%)
  waiting for transfers between devices  5.05 us (9%)
  starting transfers between devices  2.88 us (5%)
    all_to_all x2, blocking collectives, exchanged(): return lax.all_to_all(blocks, 'gz', 0, 0, tiled=True).reshape(B * rows, L)  42.7 us
    pallas_call x6, Pallas kernels, call(): pl.pallas_call(kernel, out_shape=outs, in_specs=specs, out_specs=jax.tree...  7.41 us
    ppermute x1, waiting for transfers between devices, on_device(): got_hi = lax.ppermute(own_lo, 'gx', [(b, a) for a, b in ring])  3.41 us
    ppermute x1, starting transfers between devices, on_device(): got_lo = lax.ppermute(own_hi, 'gx', ring)  2.28 us
  transfers between devices with their start and end apart: 5, of which 3 were waited for; matrix products, arithmetic and copies ran while one was open for 0% of the time, Pallas kernels for 2%

profile of v2, /device:TPU:6, one launch (start us, length us, event | category | flops | bytes accessed | tf_op | source)
XLA Modules:
  0.0 58.7 jit_solution(10328543645818647122)
XLA Ops:
  0.0 0.0 copy-start
  0.0 0.0 copy-start.2
  0.0 0.0 copy-start.1
  0.0 0.0 copy-start.3
  0.0 1.6 %shard_map.55 = (f32[72,256]{1,0:T(8,128)}, f32[72,256]{1,0:T(8,128)}) custom-call(f32[16,16,256]{2,1,0:T(8,128)} %corr.1, f32[16,16,256]{2,1,0:T(8,128)} %res.1, f32[16,16,256]{2,1,0:T(8,128)} %state.1, s32[16,256]{1,0:T(8,128)} %colour.9), custom_call_target="tpu_custom_call" | custom-call | flops 1048576 | bytes 1048576 | tf_op jit(solution)/shard_map/pallas_call | solution.py:564
  1.6 2.3 %collective-permute-start = (f32[72,256]{1,0:T(8,128)}, f32[72,256]{1,0:T(8,128)S(1)}, u32[]{:S(2)}, u32[]{:S(2)}) collective-permute-start(f32[72,256]{1,0:T(8,128)} %get-tuple-element.21.own_hi), channel_id=1, source_target_pairs={{0,64},{64,128},{128,192},{192,0},{1,65},{65,129},{129,193},{193,1... | collective-permute-start | bytes 221192 | tf_op jit(solution)/shard_map/ppermute | solution.py:586
  3.9 0.0 collective-permute-start.1
  3.9 0.0 copy-done
  3.9 0.0 copy-done.2
  3.9 0.0 copy-done.1
  3.9 0.0 copy-done.3
  4.0 0.0 copy-start.6
  4.0 0.2 shard_map.57.own_y
  4.2 0.5 copy-done.6
  4.6 0.0 copy-start.5
  4.6 1.1 %shard_map.56 = (f32[256,256]{1,0:T(8,128)S(1)}, f32[256,256]{1,0:T(8,128)S(1)}, f32[256,256]{1,0:T(8,128)S(1)}, f32[48,256]{1,0:T(8,128)S(1)}, f32[64,256]{1,0:T(8,128)S(1)}, /*index=5*/f32[64,256]{1,0:T(8,128)S(1)}) custom-call(s32[512]{0:T(512)S(1)} %copy-done.6, f32[256,256]{1,0:T(8,128)S(1)} %bitcast.9), custom_call_target="tpu_custom_call" | custom-call | flops 4194304 | bytes 4194304 | tf_op jit(solution)/shard_map/pallas_call | solution.py:564
  5.7 0.0 copy-start.4
  5.7 0.6 collective-permute-done.got_lo
  6.3 3.4 %collective-permute-done.1.got_hi = f32[72,256]{1,0:T(8,128)S(1)} collective-permute-done((f32[72,256]{1,0:T(8,128)}, f32[72,256]{1,0:T(8,128)S(1)}, u32[]{:S(2)}, u32[]{:S(2)}) %collective-permute-start.1) | collective-permute-done | bytes 73760 | tf_op jit(solution)/shard_map/ppermute | solution.py:587
  9.7 0.0 collective-permute-start.4
  9.7 0.5 collective-permute-start.3
  10.2 0.1 collective-permute-start.2
  10.3 1.1 %collective-permute-done.2.got_y = f32[8,256]{1,0:T(8,128)S(1)} collective-permute-done((f32[8,256]{1,0:T(8,128)S(1)}, f32[8,256]{1,0:T(8,128)S(1)}, u32[]{:S(2)}, u32[]{:S(2)}) %collective-permute-start.2) | collective-permute-done | bytes 8224 | tf_op jit(solution)/shard_map/ppermute | solution.py:592
  11.4 0.0 collective-permute-done.4.cross_hi
  11.4 0.0 collective-permute-done.3.cross_lo
  11.4 0.0 copy-done.5
  11.4 0.0 copy-done.4
  11.4 2.1 %shard_map.58 = (f32[1024,128]{1,0:T(8,128)S(1)}, f32[256,256]{1,0:T(8,128)S(1)}, f32[128,128]{1,0:T(8,128)S(1)}, f32[128,128]{1,0:T(8,128)S(1)}) custom-call(s32[512]{0:T(512)S(1)} %copy-done.6, f32[256,256]{1,0:T(8,128)S(1)} %bitcast.11, f32[256,256]{1,0:T(8,128)S(1)} %bitcast.13, s32[16,256]{1,0:T(8,128)S(1)} %copy-done.3, ...), custom_call_target="tpu_custom_call" | custom-call | flops 4194304 | bytes 4194304 | tf_op jit(solution)/shard_map/pallas_call | solution.py:564
  13.5 27.7 %all_to_all.10 = f32[32,32,128]{2,1,0:T(8,128)S(1)} all-to-all(f32[32,32,128]{2,1,0:T(8,128)S(1)} %bitcast.15), channel_id=1, replica_groups=mesh['gx'=4,'gy'=2,'gz'=32] {'gz'}, dimensions={0} | all-to-all | bytes 1048576 | tf_op jit(solution)/shard_map/all_to_all | solution.py:610
  41.2 0.5 shard_map.59
  41.7 15.0 %all_to_all.11 = f32[32,8,128]{2,1,0:T(8,128)S(1)} all-to-all(f32[32,8,128]{2,1,0:T(8,128)S(1)} %bitcast.16), channel_id=1, replica_groups=mesh['gx'=4,'gy'=2,'gz'=32] {'gz'}, dimensions={0} | all-to-all | bytes 262144 | tf_op jit(solution)/shard_map/all_to_all | solution.py:610
  56.7 2.0 %shard_map.60 = f32[256,256]{1,0:T(8,128)} custom-call(s32[512]{0:T(512)S(1)} %copy-done.6, f32[256,256]{1,0:T(8,128)S(1)} %get-tuple-element.33.source, f32[256,256]{1,0:T(8,128)S(1)} %get-tuple-element.24.inv, f32[128,128]{1,0:T(8,128)S(1)} %get-tuple-element.34.h_source, f32[128,128]{1,0:T(8,128)S(1)} %get-tuple-element.35.h_inv, ...), custom_call_target="tpu_custom_call" | custom-call | flops 2097152 | bytes 2097152 | tf_op jit(solution)/shard_map/pallas_call | solution.py:564
  (2 shorter events, 0.0 us)
Async XLA Ops:
  0.0 3.9 %copy-start = (f32[16,16,256]{2,1,0:T(8,128)S(1)}, f32[16,16,256]{2,1,0:T(8,128)}, u32[]{:S(2)}) copy-start(f32[16,16,256]{2,1,0:T(8,128)} %state.1) | copy-start | bytes 786436
  0.0 3.9 %copy-start.2 = (f32[16,16,256]{2,1,0:T(8,128)S(1)}, f32[16,16,256]{2,1,0:T(8,128)}, u32[]{:S(2)}) copy-start(f32[16,16,256]{2,1,0:T(8,128)} %res.1) | copy-start | bytes 786436
  0.0 3.9 %copy-start.1 = (f32[16,16,256]{2,1,0:T(8,128)S(1)}, f32[16,16,256]{2,1,0:T(8,128)}, u32[]{:S(2)}) copy-start(f32[16,16,256]{2,1,0:T(8,128)} %corr.1) | copy-start | bytes 786436
  0.0 3.9 %copy-start.3 = (s32[16,256]{1,0:T(8,128)S(1)}, s32[16,256]{1,0:T(8,128)}, u32[]{:S(2)}) copy-start(s32[16,256]{1,0:T(8,128)} %colour.9) | copy-start | bytes 49156
  1.6 4.6 %collective-permute-start = (f32[72,256]{1,0:T(8,128)}, f32[72,256]{1,0:T(8,128)S(1)}, u32[]{:S(2)}, u32[]{:S(2)}) collective-permute-start(f32[72,256]{1,0:T(8,128)} %get-tuple-element.21.own_hi), channel_id=1, source_target_pairs={{0,64},{64,128},{128,192},{192,0},{1,65},{65,129},{129,193},{193,1... | collective-permute-start | bytes 221192 | tf_op jit(solution)/shard_map/ppermute | solution.py:586
  3.9 5.8 %collective-permute-start.1 = (f32[72,256]{1,0:T(8,128)}, f32[72,256]{1,0:T(8,128)S(1)}, u32[]{:S(2)}, u32[]{:S(2)}) collective-permute-start(f32[72,256]{1,0:T(8,128)} %get-tuple-element.22.own_lo), channel_id=1, source_target_pairs={{64,0},{128,64},{192,128},{0,192},{65,1},{129,65},{193,129},{1,193... | collective-permute-start | bytes 221192 | tf_op jit(solution)/shard_map/ppermute | solution.py:587
  4.0 0.7 %copy-start.6 = (s32[512]{0:T(512)S(1)}, s32[512]{0:T(512)}, u32[]{:S(2)}) copy-start(s32[512]{0:T(512)} %level.5) | copy-start | bytes 6148
  4.6 6.8 %copy-start.5 = (f32[72,256]{1,0:T(8,128)S(1)}, f32[72,256]{1,0:T(8,128)}, u32[]{:S(2)}) copy-start(f32[72,256]{1,0:T(8,128)} %get-tuple-element.21.own_hi) | copy-start | bytes 221188
  5.7 5.7 %copy-start.4 = (f32[72,256]{1,0:T(8,128)S(1)}, f32[72,256]{1,0:T(8,128)}, u32[]{:S(2)}) copy-start(f32[72,256]{1,0:T(8,128)} %get-tuple-element.22.own_lo) | copy-start | bytes 221188
  9.7 1.7 %collective-permute-start.4 = (f32[16,256]{1,0:T(8,128)S(1)}, f32[16,256]{1,0:T(8,128)S(1)}, u32[]{:S(2)}, u32[]{:S(2)}) collective-permute-start(f32[16,256]{1,0:T(8,128)S(1)} %slice.7), channel_id=1, source_target_pairs={{0,32},{32,0},{1,33},{33,1},{2,34},{34,2},{3,35},{35,3},{4,36},{36... | collective-permute-start | bytes 49160 | tf_op jit(solution)/shard_map/ppermute | solution.py:600
  9.7 1.7 %collective-permute-start.3 = (f32[16,256]{1,0:T(8,128)S(1)}, f32[16,256]{1,0:T(8,128)S(1)}, u32[]{:S(2)}, u32[]{:S(2)}) collective-permute-start(f32[16,256]{1,0:T(8,128)S(1)} %slice.6), channel_id=1, source_target_pairs={{0,32},{32,0},{1,33},{33,1},{2,34},{34,2},{3,35},{35,3},{4,36},{36... | collective-permute-start | bytes 49160 | tf_op jit(solution)/shard_map/ppermute | solution.py:599
  10.2 1.2 %collective-permute-start.2 = (f32[8,256]{1,0:T(8,128)S(1)}, f32[8,256]{1,0:T(8,128)S(1)}, u32[]{:S(2)}, u32[]{:S(2)}) collective-permute-start(f32[8,256]{1,0:T(8,128)S(1)} %shard_map.57.own_y), channel_id=1, source_target_pairs={{0,32},{32,0},{1,33},{33,1},{2,34},{34,2},{3,35},{35,3},{4,36},{36... | collective-permute-start | bytes 24584 | tf_op jit(solution)/shard_map/ppermute | solution.py:592

commit v3 on v2

--- a/solution.py
+++ b/solution.py
@@ -15,10 +15,11 @@
 Y = 256
 L = 128
 B = 32
-R = 32
+R = 16
 
 XHI, YH, XLO0, OWN15, YOWN, XLO1 = 0, 2, 3, 4, 6, 7
-WXM, WXP, WYP = 20, 24, 28
+PER, HIGH_LINK, LEFT, RIGHT = 18, 90, 96, 112
+TURNED = (0, 2, 1, 3)
 
 
 def iota(shape, dim):
@@ -119,7 +120,7 @@
         out[4 * D : 4 * D + 8, :] = jnp.broadcast_to(row, (8, Y))
 
 
-def pack_y_kernel(corr, res, state, colour, out):
+def pack_y_kernel(corr, res, state, colour, out, tint):
     left_core = lax.axis_index("gy") == 0
 
     def columns(value):
@@ -136,6 +137,9 @@
     out[3:4, :] = picked(columns(state[...]), 0)
     row = picked(columns(colour[...].astype(jnp.float32)), 0)
     out[4:8, :] = jnp.broadcast_to(jnp.concatenate([row, row], 1), (4, Y))
+    shifted = jnp.concatenate([jnp.zeros((1, Y), jnp.float32), colour[...].astype(jnp.float32)], 0)
+    for c in range(2):
+        tint[c * L : (c + 1) * L, :] = transposed(shifted[:, c * L : (c + 1) * L])
 
 
 def factor_kernel(level, state, inv, e_first, e_last, k_own, w_x, w_y):
@@ -190,7 +194,7 @@
     level, corr, res, colour, inv, e_first, e_last, k_own, w_x, w_y,
     own_lo, own_hi, got_lo, got_hi, own_y, got_y, cross_lo, cross_hi,
     message, source, h_source, h_inv,
-    y_scratch, h_state, h_before, h_first, h_last, h_line, v_first,
+    y_scratch, h_state, h_before, h_first, h_last, h_line, v_first, laid,
 ):
     spacing, face = row_coefficients(level)
     left_core = lax.axis_index("gy") == 0
@@ -349,38 +353,40 @@
         f_first = f_first + e_first[at(k), :] * total
         f_last = f_last + e_last[at(k), :] * total
 
-    def put(r, half, value):
-        message[pl.ds(half * R + r, X, stride=2 * R), :] = value
-
-    def put_both(r, value):
-        put(r, 0, value[:, :L])
-        put(r, 1, value[:, L:])
-
-    short_lane = iota((X, L), 1)
     own_values = [k_own[i * X : (i + 1) * X, :] for i in range(3)] + [f_first, f_last]
     seen_values = own_values[:3] + [jnp.where(tint == 0.0, f, still) for f in own_values[3:]]
-    inner_link = [w_y[i * X : (i + 1) * X, :][:, L - 1 : L] for i in (0, 2, 1, 3)]
+    slot = lane & 7
+    left_slots = right_slots = still
     for q in range(5):
-        own, seen = own_values[q], seen_values[q]
-        side = (hk + hf)[q]
-        put_both(4 * q, own)
+        side, seen, at_q = (hk + hf)[q], seen_values[q], L + PER * q
         low = jnp.concatenate([side[XLO0 : XLO0 + 1], side[XLO1 : XLO1 + 1]], 1)
         high = jnp.concatenate([side[XHI : XHI + 1], side[XHI + 1 : XHI + 2]], 1)
-        put_both(4 * q + 1, jnp.where(row == 0, low, pltpu.roll(seen, 1, 0)))
-        put_both(4 * q + 2, jnp.where(row == X - 1, high, pltpu.roll(seen, X - 1, 0)))
+        laid[at_q : at_q + 1, :] = low
+        laid[at_q + 1 : at_q + 1 + X, :] = own_values[q]
+        laid[at_q + 1 + X : at_q + 2 + X, :] = high
         outer = columns[:X, q : q + 1]
-        left_end, right_end = seen[:, L:], seen[:, :L]
-        left_none, right_none = (0.0, 0.0) if q >= 3 else (left_end, right_end)
-        left_end = jnp.where(
-            short_lane == L - 1, jnp.where(left_core, left_none, outer), left_end
-        )
-        right_end = jnp.where(short_lane == 0, jnp.where(left_core, outer, right_none), right_end)
-        if q < 4:
-            link = columns[:X, 5 + q : 6 + q]
-            left_end = jnp.where(short_lane == L // 2, jnp.where(left_core, 0.0, link), left_end)
-            right_end = jnp.where(short_lane == L // 2, inner_link[q], right_end)
-        put(4 * q + 3, 0, left_end)
-        put(4 * q + 3, 1, right_end)
+        nothing = still if q >= 3 else seen
+        before = jnp.where(at_right, jnp.where(left_core, nothing, outer), seen)
+        behind = jnp.where(at_left, jnp.where(left_core, outer, nothing), seen)
+        left_slots = jnp.where(slot == q, pltpu.roll(before, 1 + q, 1), left_slots)
+        right_slots = jnp.where(slot == q, pltpu.roll(behind, Y - 8 + q, 1), right_slots)
+    for i, j in enumerate(TURNED):
+        link = columns[:X, 5 + i : 6 + i]
+        along = w_y[i * X : (i + 1) * X, :]
+        laid[i * X : (i + 1) * X, :] = jnp.where(
+            at_right, jnp.where(left_core, link, along), along
+        )
+        along = w_y[j * X : (j + 1) * X, :]
+        along = jnp.where(at_right, jnp.where(left_core, along, link), along)
+        if i < 3:
+            left_slots = jnp.where(slot == 5 + i, pltpu.roll(along, 6 + i, 1), left_slots)
+        else:
+            right_slots = jnp.where(slot == 5, pltpu.roll(along, 6, 1), right_slots)
+        high = jnp.concatenate([hw[i][OWN15 : OWN15 + 1], hw[i][OWN15 + 1 : OWN15 + 2]], 1)
+        laid[L + HIGH_LINK + i : L + HIGH_LINK + i + 1, :] = high
+    laid[L + HIGH_LINK + 4 : L + LEFT, :] = jnp.zeros((LEFT - HIGH_LINK - 4, Y), jnp.float32)
+    laid[L + LEFT : L + RIGHT, :] = left_slots
+    laid[L + RIGHT :, :] = right_slots
 
     edge_first, edge_last = (
         jnp.concatenate([e[k * X : k * X + 1, :] for k in range(D)], 0) for e in (e_first, e_last)
@@ -389,31 +395,50 @@
     low_last = jnp.concatenate([h_last[pl.ds(p, D, stride=8), :] for p in (XLO0, XLO1)], 1)
     for a, mine_e in enumerate((edge_first, edge_last)):
         for b, other_e in enumerate((low_first, low_last)):
-            i, j = 2 * a + b, 2 * b + a
+            i = 2 * a + b
             edge = jnp.sum(mine_e * other_e, axis=0, keepdims=True)
-            put_both(WXM + i, jnp.where(row == 0, edge, w_x[i * X : (i + 1) * X, :]))
-            high = jnp.concatenate([hw[i][OWN15 : OWN15 + 1], hw[i][OWN15 + 1 : OWN15 + 2]], 1)
-            turned = pltpu.roll(w_x[j * X : (j + 1) * X, :], X - 1, 0)
-            put_both(WXP + i, jnp.where(row == X - 1, high, turned))
-            link = jnp.where(left_core, columns[:X, 5 + i : 6 + i], 0.0)
-            put_both(WYP + i, jnp.where(at_right, link, w_y[i * X : (i + 1) * X, :]))
-
-
-def separator_kernel(got, colour, out, v_scratch, line_scratch):
+            along = w_x[i * X : (i + 1) * X, :]
+            laid[(4 + i) * X : (5 + i) * X, :] = jnp.where(row == 0, edge, along)
+
+    for tile in range(2):
+        for c in range(2):
+            turned = jnp.transpose(laid[tile * L : (tile + 1) * L, c * L : (c + 1) * L])
+            for n in range(L // 8):
+                first_row = (c * (L // 8) + n) * R + 8 * tile
+                message[first_row : first_row + 8, :] = turned[8 * n : 8 * n + 8]
+
+
+def separator_kernel(got, tints, out):
     patch = lax.axis_index("gz")
-    tint = colour[pl.ds(patch // 2, 1), :]
-    tint = jnp.where(patch % 2 == 0, tint[:, :L], tint[:, L:])
-
-    def quantity(q, d):
-        return got[d * R + 4 * q : d * R + 4 * q + 4, :]
-
-    off = [quantity(1, d) for d in range(B)]
-    diag = [
-        quantity(2, d) - quantity(0, d + 1) if d < B - 1 else quantity(2, d) for d in range(B)
-    ]
-    right = [
-        quantity(4, d) + quantity(3, d + 1) if d < B - 1 else quantity(4, d) for d in range(B)
-    ]
+    tint = tints[pl.ds(pl.multiple_of(patch * 8, 8), 8), :]
+    line, lane = iota((8, L), 0), iota((8, L), 1)
+
+    def rolled(value, amount):
+        amount = amount % L
+        return pltpu.roll(value, amount, 1) if amount else value
+
+    def couplings(d):
+        return got[d * R : d * R + 8, :]
+
+    def values_of(d):
+        return got[d * R + 8 : d * R + 16, :]
+
+    quantities = []
+    for d in range(B):
+        tile = values_of(d)
+        ends = [jnp.broadcast_to(got[d * R + 8 + q : d * R + 9 + q, :], (8, L)) for q in range(5)]
+        quantities.append(
+            [jnp.where(lane >= LEFT, ends[q], rolled(tile, -PER * q)) for q in range(5)]
+        )
+    off = [quantities[d][1] for d in range(B)]
+
+    def joined(here, above, sign):
+        return [
+            here[d] + sign * above[d + 1] if d < B - 1 else here[d] for d in range(B)
+        ]
+
+    diag = joined([v[2] for v in quantities], [v[0] for v in quantities], -1.0)
+    right = joined([v[4] for v in quantities], [v[3] for v in quantities], 1.0)
     middle = B // 2
     up, down = {}, {}
     for n in range(middle):
@@ -429,80 +454,73 @@
     centre = diag[middle] - off[middle] * up[middle - 1][1] - off[middle + 1] * down[middle + 1][1]
     centre = 1.0 / centre
 
-    def solved(right, sets):
-        def cut(value):
-            return value[:sets]
-
+    def solved(right):
         ahead, behind, values = {}, {}, [None] * B
         for n in range(middle):
             d = n
-            total = right[d] + cut(off[d]) * ahead[d - 1] if n else right[d]
-            ahead[d] = total * cut(up[d][0])
+            total = right[d] + off[d] * ahead[d - 1] if n else right[d]
+            ahead[d] = total * up[d][0]
             d = B - 1 - n
             if d > middle:
-                total = right[d] + cut(off[d + 1]) * behind[d + 1] if n else right[d]
-                behind[d] = total * cut(down[d][0])
-        total = (
-            right[middle]
-            + cut(off[middle]) * ahead[middle - 1]
-            + cut(off[middle + 1]) * behind[middle + 1]
-        )
-        values[middle] = total * cut(centre)
+                total = right[d] + off[d + 1] * behind[d + 1] if n else right[d]
+                behind[d] = total * down[d][0]
+        total = right[middle] + off[middle] * ahead[middle - 1] + off[middle + 1] * behind[middle + 1]
+        values[middle] = total * centre
         for n in range(middle):
             d = middle - 1 - n
-            values[d] = ahead[d] + cut(up[d][1]) * values[d + 1]
+            values[d] = ahead[d] + up[d][1] * values[d + 1]
             d = middle + 1 + n
             if d < B:
-                values[d] = behind[d] + cut(down[d][1]) * values[d - 1]
+                values[d] = behind[d] + down[d][1] * values[d - 1]
         return values
 
-    v_scratch[0:4, :] = jnp.zeros((4, L), jnp.float32)
-    for d, value in enumerate(solved(right, 4)):
-        v_scratch[4 + d * 4 : 8 + d * 4, :] = value
-
-    lane = iota((B, L), 1)
-
-    def of_set(s):
-        return v_scratch[pl.ds(s, B, stride=4), :], v_scratch[pl.ds(4 + s, B, stride=4), :]
-
-    def lines(r):
-        return got[pl.ds(r, B, stride=R), :]
-
-    own_pair, lo_pair, hi_pair, end_pair = (of_set(s) for s in range(4))
-    first_pair = [jnp.where(tint == 0, v, 0.0) for v in own_pair]
-    left_pair = [
-        jnp.where(lane == 0, pltpu.roll(e, 1, 1), pltpu.roll(v, 1, 1))
-        for e, v in zip(end_pair, first_pair)
-    ]
-    right_pair = [
-        jnp.where(lane == L - 1, pltpu.roll(e, L - 1, 1), pltpu.roll(v, L - 1, 1))
-        for e, v in zip(end_pair, first_pair)
-    ]
+    around = []
+    for value in solved(right):
+        first = jnp.where(tint == 1.0, 0.0, value)
+        around.append(
+            (
+                rolled(first, 1),
+                rolled(first, -1),
+                jnp.where(line == 0, rolled(value, 1 - LEFT), pltpu.roll(first, 1, 0)),
+                jnp.where(line == 7, rolled(value, 1 - RIGHT), pltpu.roll(first, 7, 0)),
+            )
+        )
+    still = jnp.zeros((8, L), jnp.float32)
     added = []
-    for a in range(2):
-        total = jnp.zeros((B, L), jnp.float32)
-        for b in range(2):
-            i, j = 2 * a + b, 2 * b + a
-            total = total + lines(WXM + i) * lo_pair[b]
-            total = total + lines(WXP + i) * hi_pair[b]
-            total = total + lines(WYP + i) * right_pair[b]
-            back = jnp.where(
-                lane == 0, pltpu.roll(lines(4 * i + 3), L // 2, 1), pltpu.roll(lines(WYP + j), 1, 1)
-            )
-            total = total + back * left_pair[b]
-        added.append(jnp.where(tint == 1, total, 0.0) + lines(12 + 4 * a))
-    line_scratch[0:B, :] = added[0]
-    line_scratch[B : B + 8, :] = jnp.zeros((8, L), jnp.float32)
-    line_scratch[0:B, :] = added[1] + line_scratch[1 : B + 1, :]
-    second = [line_scratch[d : d + 1, :] for d in range(B)]
-    values = solved(second, 1)
-    line_scratch[0:1, :] = jnp.zeros((1, L), jnp.float32)
     for d in range(B):
-        line_scratch[d + 1 : d + 2, :] = values[d]
-    results = [line_scratch[0:B, :], line_scratch[1 : B + 1, :]]
-    results += [*lo_pair, *hi_pair, *end_pair]
-    for i, value in enumerate(results):
-        out[pl.ds(i, B, stride=8), :] = value
+        tile, extra = couplings(d), values_of(d)
+        totals = []
+        for a in range(2):
+            total = still
+            for b in range(2):
+                i, j = 2 * a + b, 2 * b + a
+                here = around[d - 1 + b] if d - 1 + b >= 0 else None
+                if here is None:
+                    continue
+                total = total + rolled(tile, 1 - 64 - 16 * i) * here[0]
+                after = jnp.where(
+                    lane == X, rolled(extra, X - HIGH_LINK - i), rolled(tile, -64 - 16 * j)
+                )
+                total = total + after * here[1]
+                link = got[d * R + 8 + (5 + i if i < 3 else 5) :, :][:1]
+                link = rolled(link, 1 - LEFT if i < 3 else 1 - RIGHT)
+                back = jnp.where(line == 0, link, pltpu.roll(rolled(tile, 1 - 16 * j), 1, 0))
+                total = total + back * here[2]
+                total = total + rolled(tile, 1 - 16 * i) * here[3]
+            totals.append(jnp.where(tint == 1.0, total, 0.0))
+        added.append(totals)
+    second = joined(
+        [quantities[d][4] + added[d][1] for d in range(B)],
+        [quantities[d][3] + added[d][0] for d in range(B)],
+        1.0,
+    )
+    before = still
+    for d, value in enumerate(solved(second)):
+        ends = jnp.where(line < 4, value, before)
+        out[8 * d : 8 * d + 8, :] = jnp.where(
+            lane < 32, value, jnp.where(lane < 64, pltpu.roll(before, 32, 1), ends)
+        )
+        before = value
 
 
 def finish_kernel(level, source, inv, h_source, h_inv, colour, got, out, v_first, h_line):
@@ -510,31 +528,18 @@
     left_core = lax.axis_index("gy") == 0
     mine = colour[...]
 
-    def own(i):
-        return jnp.concatenate([got[pl.ds(h * 8 + i, X, stride=16), :] for h in range(2)], 1)
-
-    low, high = own(0), own(1)
-    ends = []
-    for i in (6, 7):
-        near = got[pl.ds(8 + i, X, stride=16), :]
-        far = pltpu.roll(got[pl.ds(i, X, stride=16), :], 1, 1)
-        ends.append(jnp.where(left_core, near, far)[:, 0:1])
-    short_lane = iota((X, L), 1)
-    pair = jnp.where(short_lane == 0, ends[0], ends[1])
-    turned = transposed(pair)
+    turned = jnp.concatenate([jnp.transpose(got[c * L : (c + 1) * L, :]) for c in range(2)], 1)
+    low, high = turned[33 : 33 + X], turned[1 : 1 + X]
     nothing = jnp.zeros((1, L), jnp.float32)
 
     def beside(b):
-        at = {XHI: 30 * 8 + 4, XHI + 1: 31 * 8 + 4, XLO0: 2, XLO1: 8 + 2}
-        rows = [
-            turned[b : b + 1]
-            if p == YH
-            else got[at[p] + b : at[p] + b + 1, :]
-            if p in at
-            else nothing
-            for p in range(8)
-        ]
-        return jnp.concatenate(rows, 0)
+        at_b = 0 if b else 32
+        near = got[Y - 8 + at_b // 8 : Y - 7 + at_b // 8, :]
+        far = got[at_b // 8 : at_b // 8 + 1, :]
+        end = jnp.where(left_core, pltpu.roll(near, L - RIGHT, 1), pltpu.roll(far, L - LEFT, 1))
+        lo, hi = turned[at_b : at_b + 1], turned[at_b + 1 + X : at_b + 2 + X]
+        places = {XHI: hi[:, :L], XHI + 1: hi[:, L:], XLO0: lo[:, :L], XLO1: lo[:, L:], YH: end}
+        return jnp.concatenate([places.get(p, nothing) for p in range(8)], 0)
 
     beside_after_first(face, h_source, h_inv, beside(0), beside(1), h_line)
     columns = transposed(h_line[pl.ds(YH, D, stride=8), :])
@@ -585,8 +590,8 @@
     ring = [(i, (i + 1) % xs) for i in range(xs)]
     got_lo = lax.ppermute(own_hi, "gx", ring)
     got_hi = lax.ppermute(own_lo, "gx", [(b, a) for a, b in ring])
-    own_y = call(
-        pack_y_kernel, f32(8, Y), [VMEM] * 4, [], 1 << 20, corr, res, st, colour
+    own_y, tints = call(
+        pack_y_kernel, (f32(8, Y), f32(Y, L)), [VMEM] * 4, [], 1 << 20, corr, res, st, colour
     )
     swap = [(0, 1), (1, 0)]
     got_y = lax.ppermute(own_y, "gy", swap)
@@ -600,7 +605,7 @@
     cross_hi = lax.ppermute(got_hi[:D], "gy", swap)
     message, source, h_source, h_inv = call(
         interface_kernel, (f32(B * R, L), field, f32(8 * D, L), f32(8 * D, L)),
-        [SMEM] + [VMEM] * 17, [(8 * D, L)] * 6 + [(D * X, Y)], 1 << 22,
+        [SMEM] + [VMEM] * 17, [(8 * D, L)] * 6 + [(D * X, Y), (2 * L, Y)], 1 << 22,
         level, corr, res, colour, inv, e_first, e_last, k_own, w_x, w_y,
         own_lo, own_hi, got_lo, got_hi, own_y, got_y, cross_lo, cross_hi,
     )
@@ -610,8 +615,7 @@
         return lax.all_to_all(blocks, "gz", 0, 0, tiled=True).reshape(B * rows, L)
 
     separators = call(
-        separator_kernel, f32(B * 8, L), [VMEM] * 2, [(4 * B + 8, L), (B + 8, L)],
-        1 << 21, exchanged(message, R), colour,
+        separator_kernel, f32(B * 8, L), [VMEM] * 2, [], 1 << 21, exchanged(message, R), tints
     )
     out = call(
         finish_kernel, field, [SMEM] + [VMEM] * 6, [(D * X, Y), (8 * D, L)], 1 << 21,

time: 58.9 us -> 54.2 us (0.920)
  blocking collectives: 42.7 us -> 37 us
  Pallas kernels: 7.41 us -> 8.38 us
    all_to_all x2, blocking collectives: 42.7 us -> 37 us  [exchanged(): return lax.all_to_all(blocks, 'gz', 0, 0, tiled=True).reshape(B * rows, L)]
    pallas_call x6, Pallas kernels: 7.41 us -> 8.38 us  [call(): pl.pallas_call(kernel, out_shape=outs, in_specs=specs, out_specs=jax.tree...]
where the time goes in v3:
time: 54.2 us; the launch traced here: 53.9 us
  blocking collectives  37 us (68%)
  Pallas kernels  8.38 us (15%)
  waiting for transfers between devices  5.05 us (9%)
  starting transfers between devices  2.88 us (5%)
    all_to_all x2, blocking collectives, exchanged(): return lax.all_to_all(blocks, 'gz', 0, 0, tiled=True).reshape(B * rows, L)  37 us
    pallas_call x6, Pallas kernels, call(): pl.pallas_call(kernel, out_shape=outs, in_specs=specs, out_specs=jax.tree...  8.38 us
    ppermute x1, waiting for transfers between devices, on_device(): got_hi = lax.ppermute(own_lo, 'gx', [(b, a) for a, b in ring])  3.41 us
    ppermute x1, starting transfers between devices, on_device(): got_lo = lax.ppermute(own_hi, 'gx', ring)  2.28 us
  transfers between devices with their start and end apart: 5, of which 3 were waited for; matrix products, arithmetic and copies ran while one was open for 0% of the time, Pallas kernels for 2%

profile of v3, /device:TPU:6, one launch (start us, length us, event | category | flops | bytes accessed | tf_op | source)
XLA Modules:
  0.0 53.9 jit_solution(8079777554305202651)
XLA Ops:
  0.0 0.0 copy-start
  0.0 0.0 copy-start.2
  0.0 0.0 copy-start.1
  0.0 0.0 copy-start.3
  0.0 1.6 %shard_map.55 = (f32[72,256]{1,0:T(8,128)}, f32[72,256]{1,0:T(8,128)}) custom-call(f32[16,16,256]{2,1,0:T(8,128)} %corr.1, f32[16,16,256]{2,1,0:T(8,128)} %res.1, f32[16,16,256]{2,1,0:T(8,128)} %state.1, s32[16,256]{1,0:T(8,128)} %colour.7), custom_call_target="tpu_custom_call" | custom-call | flops 1048576 | bytes 1048576 | tf_op jit(solution)/shard_map/pallas_call | solution.py:569
  1.6 2.3 %collective-permute-start = (f32[72,256]{1,0:T(8,128)}, f32[72,256]{1,0:T(8,128)S(1)}, u32[]{:S(2)}, u32[]{:S(2)}) collective-permute-start(f32[72,256]{1,0:T(8,128)} %get-tuple-element.23.own_hi), channel_id=1, source_target_pairs={{0,64},{64,128},{128,192},{192,0},{1,65},{65,129},{129,193},{193,1... | collective-permute-start | bytes 221192 | tf_op jit(solution)/shard_map/ppermute | solution.py:591
  3.9 0.0 collective-permute-start.1
  3.9 0.0 copy-done
  3.9 0.0 copy-done.2
  3.9 0.0 copy-done.1
  3.9 0.0 copy-done.3
  4.0 0.0 copy-start.6
  4.0 0.2 shard_map.57
  4.2 0.4 copy-done.6
  4.6 0.0 copy-start.5
  4.6 1.1 %shard_map.56 = (f32[256,256]{1,0:T(8,128)S(1)}, f32[256,256]{1,0:T(8,128)S(1)}, f32[256,256]{1,0:T(8,128)S(1)}, f32[48,256]{1,0:T(8,128)S(1)}, f32[64,256]{1,0:T(8,128)S(1)}, /*index=5*/f32[64,256]{1,0:T(8,128)S(1)}) custom-call(s32[512]{0:T(512)S(1)} %copy-done.6, f32[256,256]{1,0:T(8,128)S(1)} %bitcast.9), custom_call_target="tpu_custom_call" | custom-call | flops 4194304 | bytes 4194304 | tf_op jit(solution)/shard_map/pallas_call | solution.py:569
  5.7 0.0 copy-start.4
  5.7 0.6 %collective-permute-done.got_lo = f32[72,256]{1,0:T(8,128)S(1)} collective-permute-done((f32[72,256]{1,0:T(8,128)}, f32[72,256]{1,0:T(8,128)S(1)}, u32[]{:S(2)}, u32[]{:S(2)}) %collective-permute-start) | collective-permute-done | bytes 73760 | tf_op jit(solution)/shard_map/ppermute | solution.py:591
  6.3 3.4 %collective-permute-done.1.got_hi = f32[72,256]{1,0:T(8,128)S(1)} collective-permute-done((f32[72,256]{1,0:T(8,128)}, f32[72,256]{1,0:T(8,128)S(1)}, u32[]{:S(2)}, u32[]{:S(2)}) %collective-permute-start.1) | collective-permute-done | bytes 73760 | tf_op jit(solution)/shard_map/ppermute | solution.py:592
  9.7 0.0 collective-permute-start.4
  9.7 0.5 collective-permute-start.3
  10.2 0.1 collective-permute-start.2
  10.3 1.1 %collective-permute-done.2.got_y = f32[8,256]{1,0:T(8,128)S(1)} collective-permute-done((f32[8,256]{1,0:T(8,128)S(1)}, f32[8,256]{1,0:T(8,128)S(1)}, u32[]{:S(2)}, u32[]{:S(2)}) %collective-permute-start.2) | collective-permute-done | bytes 8224 | tf_op jit(solution)/shard_map/ppermute | solution.py:597
  11.4 0.0 collective-permute-done.4.cross_hi
  11.4 0.0 collective-permute-done.3.cross_lo
  11.4 0.0 copy-done.5
  11.4 0.0 copy-done.4
  11.4 2.2 %shard_map.58 = (f32[512,128]{1,0:T(8,128)S(1)}, f32[256,256]{1,0:T(8,128)S(1)}, f32[128,128]{1,0:T(8,128)S(1)}, f32[128,128]{1,0:T(8,128)S(1)}) custom-call(s32[512]{0:T(512)S(1)} %copy-done.6, f32[256,256]{1,0:T(8,128)S(1)} %bitcast.11, f32[256,256]{1,0:T(8,128)S(1)} %bitcast.13, s32[16,256]{1,0:T(8,128)S(1)} %copy-done.3, ...), custom_call_target="tpu_custom_call" | custom-call | flops 4194304 | bytes 4194304 | tf_op jit(solution)/shard_map/pallas_call | solution.py:569
  13.6 22.8 %all_to_all.10 = f32[32,16,128]{2,1,0:T(8,128)S(1)} all-to-all(f32[32,16,128]{2,1,0:T(8,128)S(1)} %bitcast.17), channel_id=1, replica_groups=mesh['gx'=4,'gy'=2,'gz'=32] {'gz'}, dimensions={0} | all-to-all | bytes 524288 | tf_op jit(solution)/shard_map/all_to_all | solution.py:615
  36.4 1.4 %shard_map.59 = f32[256,128]{1,0:T(8,128)S(1)} custom-call(f32[512,128]{1,0:T(8,128)S(1)} %bitcast.14, f32[256,128]{1,0:T(8,128)S(1)} %get-tuple-element.40.tints), custom_call_target="tpu_custom_call" | custom-call | flops 2097152 | bytes 2097152 | tf_op jit(solution)/shard_map/pallas_call | solution.py:569
  37.8 14.2 %all_to_all.11 = f32[32,8,128]{2,1,0:T(8,128)S(1)} all-to-all(f32[32,8,128]{2,1,0:T(8,128)S(1)} %bitcast.15), channel_id=1, replica_groups=mesh['gx'=4,'gy'=2,'gz'=32] {'gz'}, dimensions={0} | all-to-all | bytes 262144 | tf_op jit(solution)/shard_map/all_to_all | solution.py:615
  52.0 1.9 %shard_map.60 = f32[256,256]{1,0:T(8,128)} custom-call(s32[512]{0:T(512)S(1)} %copy-done.6, f32[256,256]{1,0:T(8,128)S(1)} %get-tuple-element.36.source, f32[256,256]{1,0:T(8,128)S(1)} %get-tuple-element.27.inv, f32[128,128]{1,0:T(8,128)S(1)} %get-tuple-element.37.h_source, f32[128,128]{1,0:T(8,128)S(1)} %get-tuple-element.38.h_inv, ...), custom_call_target="tpu_custom_call" | custom-call | flops 2097152 | bytes 2097152 | tf_op jit(solution)/shard_map/pallas_call | solution.py:569
  (2 shorter events, 0.0 us)
Async XLA Ops:
  0.0 3.9 %copy-start = (f32[16,16,256]{2,1,0:T(8,128)S(1)}, f32[16,16,256]{2,1,0:T(8,128)}, u32[]{:S(2)}) copy-start(f32[16,16,256]{2,1,0:T(8,128)} %state.1) | copy-start | bytes 786436
  0.0 3.9 %copy-start.2 = (f32[16,16,256]{2,1,0:T(8,128)S(1)}, f32[16,16,256]{2,1,0:T(8,128)}, u32[]{:S(2)}) copy-start(f32[16,16,256]{2,1,0:T(8,128)} %res.1) | copy-start | bytes 786436
  0.0 3.9 %copy-start.1 = (f32[16,16,256]{2,1,0:T(8,128)S(1)}, f32[16,16,256]{2,1,0:T(8,128)}, u32[]{:S(2)}) copy-start(f32[16,16,256]{2,1,0:T(8,128)} %corr.1) | copy-start | bytes 786436
  0.0 3.9 %copy-start.3 = (s32[16,256]{1,0:T(8,128)S(1)}, s32[16,256]{1,0:T(8,128)}, u32[]{:S(2)}) copy-start(s32[16,256]{1,0:T(8,128)} %colour.7) | copy-start | bytes 49156
  1.6 4.6 %collective-permute-start = (f32[72,256]{1,0:T(8,128)}, f32[72,256]{1,0:T(8,128)S(1)}, u32[]{:S(2)}, u32[]{:S(2)}) collective-permute-start(f32[72,256]{1,0:T(8,128)} %get-tuple-element.23.own_hi), channel_id=1, source_target_pairs={{0,64},{64,128},{128,192},{192,0},{1,65},{65,129},{129,193},{193,1... | collective-permute-start | bytes 221192 | tf_op jit(solution)/shard_map/ppermute | solution.py:591
  3.9 5.8 %collective-permute-start.1 = (f32[72,256]{1,0:T(8,128)}, f32[72,256]{1,0:T(8,128)S(1)}, u32[]{:S(2)}, u32[]{:S(2)}) collective-permute-start(f32[72,256]{1,0:T(8,128)} %get-tuple-element.24.own_lo), channel_id=1, source_target_pairs={{64,0},{128,64},{192,128},{0,192},{65,1},{129,65},{193,129},{1,193... | collective-permute-start | bytes 221192 | tf_op jit(solution)/shard_map/ppermute | solution.py:592
  4.0 0.7 %copy-start.6 = (s32[512]{0:T(512)S(1)}, s32[512]{0:T(512)}, u32[]{:S(2)}) copy-start(s32[512]{0:T(512)} %level.5) | copy-start | bytes 6148
  4.6 6.8 %copy-start.5 = (f32[72,256]{1,0:T(8,128)S(1)}, f32[72,256]{1,0:T(8,128)}, u32[]{:S(2)}) copy-start(f32[72,256]{1,0:T(8,128)} %get-tuple-element.23.own_hi) | copy-start | bytes 221188
  5.7 5.7 %copy-start.4 = (f32[72,256]{1,0:T(8,128)S(1)}, f32[72,256]{1,0:T(8,128)}, u32[]{:S(2)}) copy-start(f32[72,256]{1,0:T(8,128)} %get-tuple-element.24.own_lo) | copy-start | bytes 221188
  9.7 1.7 %collective-permute-start.4 = (f32[16,256]{1,0:T(8,128)S(1)}, f32[16,256]{1,0:T(8,128)S(1)}, u32[]{:S(2)}, u32[]{:S(2)}) collective-permute-start(f32[16,256]{1,0:T(8,128)S(1)} %slice.7), channel_id=1, source_target_pairs={{0,32},{32,0},{1,33},{33,1},{2,34},{34,2},{3,35},{35,3},{4,36},{36... | collective-permute-start | bytes 49160 | tf_op jit(solution)/shard_map/ppermute | solution.py:605
  9.7 1.7 %collective-permute-start.3 = (f32[16,256]{1,0:T(8,128)S(1)}, f32[16,256]{1,0:T(8,128)S(1)}, u32[]{:S(2)}, u32[]{:S(2)}) collective-permute-start(f32[16,256]{1,0:T(8,128)S(1)} %slice.6), channel_id=1, source_target_pairs={{0,32},{32,0},{1,33},{33,1},{2,34},{34,2},{3,35},{35,3},{4,36},{36... | collective-permute-start | bytes 49160 | tf_op jit(solution)/shard_map/ppermute | solution.py:604
  10.2 1.2 %collective-permute-start.2 = (f32[8,256]{1,0:T(8,128)S(1)}, f32[8,256]{1,0:T(8,128)S(1)}, u32[]{:S(2)}, u32[]{:S(2)}) collective-permute-start(f32[8,256]{1,0:T(8,128)S(1)} %get-tuple-element.35.own_y), channel_id=1, source_target_pairs={{0,32},{32,0},{1,33},{33,1},{2,34},{34,2},{3,35},{35,3},{4,36},{36... | collective-permute-start | bytes 24584 | tf_op jit(solution)/shard_map/ppermute | solution.py:597

commit v4 on v3

--- a/solution.py
+++ b/solution.py
@@ -43,6 +43,13 @@
         face = jnp.float32(coef_z * 2.0) / (around[i] + around[i + 1])
         faces.append(jnp.where(inside, face, jnp.float32(0.0)))
     return around[1 : D + 1], faces
+
+
+def coefficient_rows(coef, width):
+    return (
+        [coef[k : k + 1, :width] for k in range(D)],
+        [coef[D + k : D + k + 1, :width] for k in range(D + 1)],
+    )
 
 
 def centre_of(spacing, low, high, state):
@@ -87,17 +94,21 @@
         v_first[at(k), :] = jnp.where(tint == 0, value, 0.0)
 
 
-def beside_sum(v_first, h_line, column, k, left_core):
+def sided(columns):
+    left = jnp.full(columns.shape, lax.axis_index("gy"), jnp.int32) == 0
+    return jnp.where(left, 0.0, columns), jnp.where(left, columns, 0.0)
+
+
+def beside_sum(v_first, h_line, columns, k):
     row, lane = iota((X, Y), 0), iota((X, Y), 1)
     lines = v_first[at(k), :]
     sides = h_line[k * 8 : (k + 1) * 8, :]
     lo = jnp.concatenate([sides[XLO0 : XLO0 + 1], sides[XLO1 : XLO1 + 1]], 1)
     hi = jnp.concatenate([sides[XHI : XHI + 1], sides[XHI + 1 : XHI + 2]], 1)
 
-    left = jnp.where(lane == 0, jnp.where(left_core, 0.0, column), pltpu.roll(lines, 1, 1))
-    right = jnp.where(
-        lane == Y - 1, jnp.where(left_core, column, 0.0), pltpu.roll(lines, Y - 1, 1)
-    )
+    left_column, right_column = (c[:X, k : k + 1] for c in columns)
+    left = jnp.where(lane == 0, left_column, pltpu.roll(lines, 1, 1))
+    right = jnp.where(lane == Y - 1, right_column, pltpu.roll(lines, Y - 1, 1))
     in_x = jnp.where(row == 0, lo, pltpu.roll(lines, 1, 0)) + jnp.where(
         row == X - 1, hi, pltpu.roll(lines, X - 1, 0)
     )
@@ -142,8 +153,12 @@
         tint[c * L : (c + 1) * L, :] = transposed(shifted[:, c * L : (c + 1) * L])
 
 
-def factor_kernel(level, state, inv, e_first, e_last, k_own, w_x, w_y):
+def factor_kernel(level, state, inv, e_first, e_last, k_own, w_x, w_y, coef):
     spacing, face = row_coefficients(level)
+    for i, value in enumerate(spacing + face):
+        coef[i : i + 1, :] = jnp.full((1, Y), value, jnp.float32)
+    for i in range(2 * D + 1, coef.shape[0]):
+        coef[i : i + 1, :] = jnp.zeros((1, Y), jnp.float32)
 
     def rows(ref, k):
         return ref[k * X : (k + 1) * X, :]
@@ -190,14 +205,14 @@
         w_y[i * X : (i + 1) * X, :] = wy[i]
 
 
-def interface_kernel(
-    level, corr, res, colour, inv, e_first, e_last, k_own, w_x, w_y,
-    own_lo, own_hi, got_lo, got_hi, own_y, got_y, cross_lo, cross_hi,
-    message, source, h_source, h_inv,
-    y_scratch, h_state, h_before, h_first, h_last, h_line, v_first, laid,
+def local_kernel(
+    coef, corr, res, colour, inv, e_first, e_last, k_own, w_x, w_y,
+    own_lo, own_hi, got_lo, got_hi, own_y, got_y,
+    source, v_first, h_source, h_inv, h_first, h_last, h_mask, coupled, laid,
+    y_scratch, h_state, pairs,
 ):
-    spacing, face = row_coefficients(level)
-    left_core = lax.axis_index("gy") == 0
+    spacing, face = coefficient_rows(coef, Y)
+    h_spacing, h_face = coefficient_rows(coef, L)
     has_lo, has_hi = lax.axis_index("gx") > 0, lax.axis_index("gx") < lax.axis_size("gx") - 1
     row = iota((X, Y), 0)
     lane = iota((X, Y), 1)
@@ -207,50 +222,44 @@
 
     def spread(ref):
         for k in range(D):
-            at = k % 8 * X
+            first = k % 8 * X
             tile = ref[:, k // 8 * L : (k // 8 + 1) * L]
-            y_scratch[k * 8 : (k + 1) * 8, :] = pltpu.roll(tile, L - at, 1) if at else tile
+            y_scratch[k * 8 : (k + 1) * 8, :] = pltpu.roll(tile, L - first, 1) if first else tile
         return [y_scratch[pl.ds(q, D, stride=8), :] for q in range(5)]
 
     yh_corr, yh_next, yh_res, yh_state, yh_colour = spread(got_y)
     yo_corr, unused, unused, yo_state, unused = spread(own_y)
     yh_colour = yh_colour[0:1]
 
+    h_state[...] = jnp.zeros_like(h_state)
+    h_source[...] = jnp.zeros_like(h_source)
+    h_mask[...] = jnp.zeros_like(h_mask)
+
     small_lane = iota((D, L), 1)
-
-    def corner(ref, there):
-        value = jnp.where(left_core, ref[:, 0:1], ref[:, Y - 1 : Y])
-        return jnp.where(there, value, 0.0)
-
-    corner_lo, corner_hi = corner(cross_lo, has_lo), corner(cross_hi, has_hi)
-
-    h_state[...] = jnp.zeros_like(h_state)
-    h_before[...] = jnp.zeros_like(h_before)
-
-    below = jnp.where(small_lane == 0, corner_lo, pltpu.roll(yh_corr, 1, 1))
-    above = jnp.where(small_lane == X - 1, corner_hi, pltpu.roll(yh_corr, L - 1, 1))
+    below = jnp.where(small_lane == 0, 0.0, pltpu.roll(yh_corr, 1, 1))
+    above = jnp.where(small_lane == X - 1, 0.0, pltpu.roll(yh_corr, L - 1, 1))
     yh_source = yh_res + (coef_x * (below + above) + coef_y * (yo_corr + yh_next))
-    h_before[pl.ds(YH, D, stride=8), :] = jnp.where(yh_colour == 0.0, yh_source, 0.0)
+    h_source[pl.ds(YH, D, stride=8), :] = jnp.where(yh_colour == 0.0, yh_source, 0.0)
+    h_mask[YH : YH + 1, :] = jnp.where(yh_colour == 0.0, 1.0, 0.0)
     h_state[pl.ds(YH, D, stride=8), :] = yh_state
     h_state[pl.ds(YOWN, D, stride=8), :] = yo_state
     beside_corr = []
-    row_k = iota((D, Y), 0)
     lane_k = iota((D, Y), 1)
-    for got, own, there, at_corner, places in (
-        (got_lo, own_lo, has_lo, corner_lo, (XLO0, XLO1)),
-        (got_hi, own_hi, has_hi, corner_hi, (XHI, XHI + 1)),
+    for got, own, there, places in (
+        (got_lo, own_lo, has_lo, (XLO0, XLO1)),
+        (got_hi, own_hi, has_hi, (XHI, XHI + 1)),
     ):
         near = jnp.where(there, plane(got, 0), 0.0)
         beside_corr.append(near)
-        left = jnp.where(lane_k == 0, jnp.where(left_core, 0.0, at_corner), pltpu.roll(near, 1, 1))
-        right = jnp.where(
-            lane_k == Y - 1, jnp.where(left_core, at_corner, 0.0), pltpu.roll(near, Y - 1, 1)
-        )
+        left = jnp.where(lane_k == 0, 0.0, pltpu.roll(near, 1, 1))
+        right = jnp.where(lane_k == Y - 1, 0.0, pltpu.roll(near, Y - 1, 1))
         value = plane(got, 2) + (coef_x * (plane(got, 1) + plane(own, 0)) + coef_y * (left + right))
-        value = jnp.where(there & (got[4 * D : 4 * D + 1, :] == 0.0), value, 0.0)
+        mask = jnp.where(there & (got[4 * D : 4 * D + 1, :] == 0.0), 1.0, 0.0)
+        value = jnp.where(mask == 1.0, value, 0.0)
         states = plane(got, 3)
         for c, place in enumerate(places):
-            h_before[pl.ds(place, D, stride=8), :] = value[:, c * L : (c + 1) * L]
+            h_source[pl.ds(place, D, stride=8), :] = value[:, c * L : (c + 1) * L]
+            h_mask[place : place + 1, :] = mask[:, c * L : (c + 1) * L]
             h_state[pl.ds(place, D, stride=8), :] = states[:, c * L : (c + 1) * L]
     edge_state = plane(own_hi, 3)
     for c in range(2):
@@ -262,13 +271,13 @@
     ratio = running = None
     inverses, forwards = [], []
     for k in range(D - 1):
-        pivot = centre_of(spacing[k], face[k], face[k + 1], rows8(h_state, k))
+        pivot = centre_of(h_spacing[k], h_face[k], h_face[k + 1], rows8(h_state, k))
         if k:
-            pivot = pivot - face[k] * ratio
+            pivot = pivot - h_face[k] * ratio
         inverse = 1.0 / pivot
-        scaled = face[k] * inverse
+        scaled = h_face[k] * inverse
         running = scaled * running if k else scaled
-        ratio = face[k + 1] * inverse
+        ratio = h_face[k + 1] * inverse
         inverses.append(inverse)
         forwards.append(running)
         h_inv[k * 8 : (k + 1) * 8, :] = inverse
@@ -277,135 +286,197 @@
     place8 = iota((8, L), 0)
     weight = jnp.where((place8 == YOWN) | (place8 == YH), jnp.float32(coef_y), jnp.float32(coef_x))
     first, last = zero, one
-    hw = [zero, zero, zero, weight * spacing[D - 1]]
-    hs = spacing[D - 1] * rows8(h_before, D - 1)
-    h_source[(D - 1) * 8 :, :] = hs
-    hf = [zero, hs]
+    hw = [zero, zero, zero, weight * h_spacing[D - 1]]
+    h_source[(D - 1) * 8 :, :] = h_spacing[D - 1] * rows8(h_source, D - 1)
     hk = [None, None, None]
     h_first[(D - 1) * 8 :, :] = zero
-    h_last[(D - 1) * 8 :, :] = one * (coef_x * spacing[D - 1])
+    h_last[(D - 1) * 8 :, :] = one
     for k in range(D - 2, -1, -1):
-        ratio = face[k + 1] * inverses[k]
+        ratio = h_face[k + 1] * inverses[k]
         first = forwards[k] + ratio * first
         last = ratio * last
         if k == D - 2:
-            hk[1] = face[D - 1] * first
-            centre = centre_of(spacing[D - 1], face[D - 1], face[D], rows8(h_state, D - 1))
-            hk[2] = centre - face[D - 1] * last
-        hs = spacing[k] * rows8(h_before, k)
-        h_source[k * 8 : (k + 1) * 8, :] = hs
-        hf[0] = hf[0] + first * hs
-        hf[1] = hf[1] + last * hs
-        h_first[k * 8 : (k + 1) * 8, :] = (coef_x * spacing[k]) * first
-        h_last[k * 8 : (k + 1) * 8, :] = (coef_x * spacing[k]) * last
+            hk[1] = h_face[D - 1] * first
+            centre = centre_of(h_spacing[D - 1], h_face[D - 1], h_face[D], rows8(h_state, D - 1))
+            hk[2] = centre - h_face[D - 1] * last
+        h_source[k * 8 : (k + 1) * 8, :] = h_spacing[k] * rows8(h_source, k)
+        h_first[k * 8 : (k + 1) * 8, :] = first
+        h_last[k * 8 : (k + 1) * 8, :] = last
         partner = (pltpu.roll(first, 4, 0), pltpu.roll(last, 4, 0))
         for a, mine in enumerate((first, last)):
-            mine = (weight * spacing[k]) * mine
+            mine = (weight * h_spacing[k]) * mine
             for b in range(2):
                 hw[2 * a + b] = hw[2 * a + b] + mine * partner[b]
-    hk[0] = face[0] * first
+    hk[0] = h_face[0] * first
 
     columns = transposed(
-        jnp.concatenate(
-            [v[YH : YH + 1] for v in hk + hf] + [v[YOWN : YOWN + 1] for v in hw], 0
-        )
-    )
-    columns_corr = transposed(jnp.concatenate([yh_corr, yh_colour], 0))
+        jnp.concatenate([v[YH : YH + 1] for v in hk] + [v[YOWN : YOWN + 1] for v in hw], 0)
+    )
+    columns_corr = sided(transposed(jnp.concatenate([yh_corr, yh_colour], 0)))
 
     mine = colour[...]
     colour_lo, colour_hi = got_lo[4 * D : 4 * D + 1, :], got_hi[4 * D : 4 * D + 1, :]
     tint = mine.astype(jnp.float32)
-    tint_y = columns_corr[:X, D : D + 1]
     at_left, at_right = (lane == 0), (lane == Y - 1)
 
-    def beside_of(value, lo, hi, y_column):
+    def beside_of(value, lo, hi, k):
         return (
             jnp.where(row == 0, lo, pltpu.roll(value, 1, 0)),
             jnp.where(row == X - 1, hi, pltpu.roll(value, X - 1, 0)),
-            jnp.where(at_left, jnp.where(left_core, 0.0, y_column), pltpu.roll(value, 1, 1)),
-            jnp.where(at_right, jnp.where(left_core, y_column, 0.0), pltpu.roll(value, Y - 1, 1)),
+            jnp.where(at_left, columns_corr[0][:X, k : k + 1], pltpu.roll(value, 1, 1)),
+            jnp.where(at_right, columns_corr[1][:X, k : k + 1], pltpu.roll(value, Y - 1, 1)),
         )
 
     weights = [
         jnp.where((tint == 1.0) & (other == 0.0), 0.0, jnp.float32(amount))
         for other, amount in zip(
-            beside_of(tint, colour_lo, colour_hi, tint_y), (coef_x, coef_x, coef_y, coef_y)
+            beside_of(tint, colour_lo, colour_hi, D), (coef_x, coef_x, coef_y, coef_y)
         )
     ]
     for k in range(D):
-        value = corr[k * X : (k + 1) * X, :]
         around = beside_of(
-            value, beside_corr[0][k : k + 1], beside_corr[1][k : k + 1], columns_corr[:X, k : k + 1]
+            corr[at(k), :], beside_corr[0][k : k + 1], beside_corr[1][k : k + 1], k
         )
-        total = res[k * X : (k + 1) * X, :]
+        total = res[at(k), :]
         for w, v in zip(weights, around):
             total = total + w * v
         source[at(k), :] = spacing[k] * total
-
-    beside_after_first(face, h_source, h_inv, zero, zero, h_line)
     still = jnp.zeros((X, Y), jnp.float32)
     own_after_first(face, source, inv, mine, still, still, v_first)
-    columns_first = transposed(h_line[pl.ds(YH, D, stride=8), :])
-    f_first = f_last = still
-    for k in range(D):
-        added = beside_sum(v_first, h_line, columns_first[:X, k : k + 1], k, left_core)
-        total = source[at(k), :] + jnp.where(mine == 1, spacing[k] * added, 0.0)
-        f_first = f_first + e_first[at(k), :] * total
-        f_last = f_last + e_last[at(k), :] * total
-
-    own_values = [k_own[i * X : (i + 1) * X, :] for i in range(3)] + [f_first, f_last]
-    seen_values = own_values[:3] + [jnp.where(tint == 0.0, f, still) for f in own_values[3:]]
+
+    masks = end_masks()
     slot = lane & 7
     left_slots = right_slots = still
-    for q in range(5):
-        side, seen, at_q = (hk + hf)[q], seen_values[q], L + PER * q
-        low = jnp.concatenate([side[XLO0 : XLO0 + 1], side[XLO1 : XLO1 + 1]], 1)
-        high = jnp.concatenate([side[XHI : XHI + 1], side[XHI + 1 : XHI + 2]], 1)
-        laid[at_q : at_q + 1, :] = low
-        laid[at_q + 1 : at_q + 1 + X, :] = own_values[q]
-        laid[at_q + 1 + X : at_q + 2 + X, :] = high
-        outer = columns[:X, q : q + 1]
-        nothing = still if q >= 3 else seen
-        before = jnp.where(at_right, jnp.where(left_core, nothing, outer), seen)
-        behind = jnp.where(at_left, jnp.where(left_core, outer, nothing), seen)
-        left_slots = jnp.where(slot == q, pltpu.roll(before, 1 + q, 1), left_slots)
-        right_slots = jnp.where(slot == q, pltpu.roll(behind, Y - 8 + q, 1), right_slots)
+    for q in range(3):
+        own = k_own[q * X : (q + 1) * X, :]
+        put_lines(laid, q, hk[q], own)
+        left, right = end_slots(masks, q, columns[:X, q : q + 1], own, own)
+        left_slots = jnp.where(slot == q, left, left_slots)
+        right_slots = jnp.where(slot == q, right, right_slots)
     for i, j in enumerate(TURNED):
-        link = columns[:X, 5 + i : 6 + i]
+        link = columns[:X, 3 + i : 4 + i]
         along = w_y[i * X : (i + 1) * X, :]
-        laid[i * X : (i + 1) * X, :] = jnp.where(
-            at_right, jnp.where(left_core, link, along), along
-        )
-        along = w_y[j * X : (j + 1) * X, :]
-        along = jnp.where(at_right, jnp.where(left_core, along, link), along)
+        pairs[i * X : (i + 1) * X, :] = jnp.where(masks[2], link, along)
+        along = jnp.where(masks[1], link, w_y[j * X : (j + 1) * X, :])
         if i < 3:
             left_slots = jnp.where(slot == 5 + i, pltpu.roll(along, 6 + i, 1), left_slots)
         else:
             right_slots = jnp.where(slot == 5, pltpu.roll(along, 6, 1), right_slots)
         high = jnp.concatenate([hw[i][OWN15 : OWN15 + 1], hw[i][OWN15 + 1 : OWN15 + 2]], 1)
-        laid[L + HIGH_LINK + i : L + HIGH_LINK + i + 1, :] = high
-    laid[L + HIGH_LINK + 4 : L + LEFT, :] = jnp.zeros((LEFT - HIGH_LINK - 4, Y), jnp.float32)
-    laid[L + LEFT : L + RIGHT, :] = left_slots
-    laid[L + RIGHT :, :] = right_slots
-
-    edge_first, edge_last = (
-        jnp.concatenate([e[k * X : k * X + 1, :] for k in range(D)], 0) for e in (e_first, e_last)
-    )
-    low_first = jnp.concatenate([h_first[pl.ds(p, D, stride=8), :] for p in (XLO0, XLO1)], 1)
-    low_last = jnp.concatenate([h_last[pl.ds(p, D, stride=8), :] for p in (XLO0, XLO1)], 1)
-    for a, mine_e in enumerate((edge_first, edge_last)):
-        for b, other_e in enumerate((low_first, low_last)):
+        laid[HIGH_LINK + i : HIGH_LINK + i + 1, :] = high
+    laid[PER * 3 : PER * 5, :] = jnp.zeros((PER * 2, Y), jnp.float32)
+    laid[HIGH_LINK + 4 : LEFT, :] = jnp.zeros((LEFT - HIGH_LINK - 4, Y), jnp.float32)
+    laid[LEFT:RIGHT, :] = left_slots
+    laid[RIGHT:, :] = right_slots
+
+    amounts = coef_x * coef[0:D, 0:1]
+    edges = [
+        amounts * jnp.concatenate([e[k * X : k * X + 1, :] for k in range(D)], 0)
+        for e in (e_first, e_last)
+    ]
+    lows = [
+        jnp.concatenate([h[pl.ds(p, D, stride=8), :] for p in (XLO0, XLO1)], 1)
+        for h in (h_first, h_last)
+    ]
+    for a in range(2):
+        for b in range(2):
             i = 2 * a + b
-            edge = jnp.sum(mine_e * other_e, axis=0, keepdims=True)
+            edge = jnp.sum(edges[a] * lows[b], axis=0, keepdims=True)
             along = w_x[i * X : (i + 1) * X, :]
-            laid[(4 + i) * X : (5 + i) * X, :] = jnp.where(row == 0, edge, along)
-
-    for tile in range(2):
-        for c in range(2):
-            turned = jnp.transpose(laid[tile * L : (tile + 1) * L, c * L : (c + 1) * L])
-            for n in range(L // 8):
-                first_row = (c * (L // 8) + n) * R + 8 * tile
-                message[first_row : first_row + 8, :] = turned[8 * n : 8 * n + 8]
+            pairs[(4 + i) * X : (5 + i) * X, :] = jnp.where(row == 0, edge, along)
+    for c in range(2):
+        coupled[c * L : (c + 1) * L, :] = jnp.transpose(pairs[:, c * L : (c + 1) * L])
+
+
+def end_masks():
+    lane = iota((X, Y), 1)
+    is_left = jnp.full((X, Y), lax.axis_index("gy"), jnp.int32) == 0
+    at_left, at_right = (lane == 0), (lane == Y - 1)
+    return at_left & is_left, at_right & ~is_left, at_right & is_left, at_left & ~is_left
+
+
+def end_slots(masks, q, outer, seen, nothing):
+    outer_left, outer_right, none_left, none_right = masks
+    before = jnp.where(outer_right, outer, jnp.where(none_left, nothing, seen))
+    behind = jnp.where(outer_left, outer, jnp.where(none_right, nothing, seen))
+    return pltpu.roll(before, 1 + q, 1), pltpu.roll(behind, Y - 8 + q, 1)
+
+
+def put_lines(laid, q, side, own):
+    low = jnp.concatenate([side[XLO0 : XLO0 + 1], side[XLO1 : XLO1 + 1]], 1)
+    high = jnp.concatenate([side[XHI : XHI + 1], side[XHI + 1 : XHI + 2]], 1)
+    laid[PER * q : PER * q + 1, :] = low
+    laid[PER * q + 1 : PER * q + 1 + X, :] = own
+    laid[PER * q + 1 + X : PER * q + 2 + X, :] = high
+
+
+def message_kernel(
+    coef, colour, source, v_first, h_local, h_inv, h_first, h_last, h_mask, coupled, local,
+    e_first, e_last, cross_lo, cross_hi,
+    message, h_source, h_line, laid,
+):
+    spacing, face = coefficient_rows(coef, Y)
+    h_face = coefficient_rows(coef, L)[1]
+    on_left = jnp.where(lax.axis_index("gy") == 0, jnp.float32(1.0), jnp.float32(0.0))
+    lane = iota((X, Y), 1)
+    small_lane = iota((D, L), 1)
+    amounts = coef[0:D, 0:1]
+    h_source[...] = h_local[...]
+    laid[...] = local[...]
+
+    def add(place, lane_at, value):
+        rows = h_source[pl.ds(place, D, stride=8), :]
+        rows = rows + jnp.where(small_lane == lane_at, value, 0.0) * h_mask[place : place + 1, :]
+        h_source[pl.ds(place, D, stride=8), :] = rows
+
+    xs = lax.axis_size("gx") - 1
+    for cross, there, places, lane_at in (
+        (cross_lo, lax.axis_index("gx") > 0, (XLO0, XLO1), 0),
+        (cross_hi, lax.axis_index("gx") < xs, (XHI, XHI + 1), X - 1),
+    ):
+        value = on_left * cross[:, 0:1] + (1.0 - on_left) * cross[:, Y - 1 : Y]
+        value = amounts * jnp.where(there, value, 0.0)
+        add(YH, lane_at, coef_x * value)
+        add(places[0], 0, (coef_y * (1.0 - on_left)) * value)
+        add(places[1], L - 1, (coef_y * on_left) * value)
+
+    zero = jnp.zeros((8, L), jnp.float32)
+    hf = [zero, zero]
+    for k in range(D):
+        rows = slice(k * 8, (k + 1) * 8)
+        hf[0] = hf[0] + h_first[rows, :] * h_source[rows, :]
+        hf[1] = hf[1] + h_last[rows, :] * h_source[rows, :]
+    columns = transposed(jnp.concatenate([v[YH : YH + 1] for v in hf], 0))
+
+    beside_after_first(h_face, h_source, h_inv, zero, zero, h_line)
+    columns_first = sided(transposed(h_line[pl.ds(YH, D, stride=8), :]))
+    mine = colour[...]
+    still = jnp.zeros((X, Y), jnp.float32)
+    f_own = [still, still]
+    for k in range(D):
+        added = beside_sum(v_first, h_line, columns_first, k)
+        total = source[at(k), :] + jnp.where(mine == 1, spacing[k] * added, 0.0)
+        f_own[0] = f_own[0] + e_first[at(k), :] * total
+        f_own[1] = f_own[1] + e_last[at(k), :] * total
+
+    masks = end_masks()
+    slot = lane & 7
+    left_slots, right_slots = laid[LEFT:RIGHT, :], laid[RIGHT:, :]
+    for i in range(2):
+        q = 3 + i
+        put_lines(laid, q, hf[i], f_own[i])
+        seen = jnp.where(mine == 0, f_own[i], 0.0)
+        left, right = end_slots(masks, q, columns[:X, i : i + 1], seen, still)
+        left_slots = jnp.where(slot == q, left, left_slots)
+        right_slots = jnp.where(slot == q, right, right_slots)
+    laid[LEFT:RIGHT, :] = left_slots
+    laid[RIGHT:, :] = right_slots
+    for c in range(2):
+        turned = jnp.transpose(laid[:, c * L : (c + 1) * L])
+        for n in range(L // 8):
+            p = c * (L // 8) + n
+            message[p * R : p * R + 8, :] = coupled[8 * p : 8 * p + 8, :]
+            message[p * R + 8 : p * R + 16, :] = turned[8 * n : 8 * n + 8]
 
 
 def separator_kernel(got, tints, out):
@@ -523,8 +594,9 @@
         before = value
 
 
-def finish_kernel(level, source, inv, h_source, h_inv, colour, got, out, v_first, h_line):
-    spacing, face = row_coefficients(level)
+def finish_kernel(coef, source, inv, h_source, h_inv, colour, got, out, v_first, h_line):
+    spacing, face = coefficient_rows(coef, Y)
+    h_face = coefficient_rows(coef, L)[1]
     left_core = lax.axis_index("gy") == 0
     mine = colour[...]
 
@@ -541,12 +613,12 @@
         places = {XHI: hi[:, :L], XHI + 1: hi[:, L:], XLO0: lo[:, :L], XLO1: lo[:, L:], YH: end}
         return jnp.concatenate([places.get(p, nothing) for p in range(8)], 0)
 
-    beside_after_first(face, h_source, h_inv, beside(0), beside(1), h_line)
-    columns = transposed(h_line[pl.ds(YH, D, stride=8), :])
+    beside_after_first(h_face, h_source, h_inv, beside(0), beside(1), h_line)
+    columns = sided(transposed(h_line[pl.ds(YH, D, stride=8), :]))
     own_after_first(face, source, inv, mine, low, high, v_first)
     value = low
     for k in range(D - 1):
-        added = beside_sum(v_first, h_line, columns[:X, k : k + 1], k, left_core)
+        added = beside_sum(v_first, h_line, columns, k)
         value = (source[at(k), :] + spacing[k] * added + face[k] * value) * inv[at(k), :]
         out[at(k), :] = value
     value = high
@@ -596,18 +668,25 @@
     swap = [(0, 1), (1, 0)]
     got_y = lax.ppermute(own_y, "gy", swap)
     field = f32(D * X, Y)
-    inv, e_first, e_last, k_own, w_x, w_y = call(
-        factor_kernel, (field, field, field, f32(3 * X, Y), f32(4 * X, Y), f32(4 * X, Y)),
+    inv, e_first, e_last, k_own, w_x, w_y, coef = call(
+        factor_kernel,
+        (field, field, field, f32(3 * X, Y), f32(4 * X, Y), f32(4 * X, Y), f32(40, Y)),
         [SMEM, VMEM], [], 1 << 22, level, st,
     )
-    got_lo, got_hi, inv, own_y = lax.optimization_barrier((got_lo, got_hi, inv, own_y))
+    got_lo, got_hi, got_y, inv = lax.optimization_barrier((got_lo, got_hi, got_y, inv))
     cross_lo = lax.ppermute(got_lo[:D], "gy", swap)
     cross_hi = lax.ppermute(got_hi[:D], "gy", swap)
-    message, source, h_source, h_inv = call(
-        interface_kernel, (f32(B * R, L), field, f32(8 * D, L), f32(8 * D, L)),
-        [SMEM] + [VMEM] * 17, [(8 * D, L)] * 6 + [(D * X, Y), (2 * L, Y)], 1 << 22,
-        level, corr, res, colour, inv, e_first, e_last, k_own, w_x, w_y,
-        own_lo, own_hi, got_lo, got_hi, own_y, got_y, cross_lo, cross_hi,
+    small = f32(8 * D, L)
+    source, v_first, h_local, h_inv, h_first, h_last, h_mask, coupled, laid = call(
+        local_kernel, (field, field, small, small, small, small, f32(8, L), f32(Y, L), f32(L, Y)),
+        [VMEM] * 16, [(8 * D, L), (8 * D, L), (L, Y)], 1 << 22,
+        coef, corr, res, colour, inv, e_first, e_last, k_own, w_x, w_y,
+        own_lo, own_hi, got_lo, got_hi, own_y, got_y,
+    )
+    message, h_source = call(
+        message_kernel, (f32(B * R, L), small), [VMEM] * 15, [(8 * D, L), (L, Y)], 1 << 22,
+        coef, colour, source, v_first, h_local, h_inv, h_first, h_last, h_mask, coupled, laid,
+        e_first, e_last, cross_lo, cross_hi,
     )
 
     def exchanged(value, rows):
@@ -618,8 +697,8 @@
         separator_kernel, f32(B * 8, L), [VMEM] * 2, [], 1 << 21, exchanged(message, R), tints
     )
     out = call(
-        finish_kernel, field, [SMEM] + [VMEM] * 6, [(D * X, Y), (8 * D, L)], 1 << 21,
-        level, source, inv, h_source, h_inv, colour, exchanged(separators, 8),
+        finish_kernel, field, [VMEM] * 7, [(D * X, Y), (8 * D, L)], 1 << 21,
+        coef, source, inv, h_source, h_inv, colour, exchanged(separators, 8),
     )
     return out.reshape(D, X, Y)
 

time: 54.2 us -> 51.9 us (0.958)
  Pallas kernels: 8.38 us -> 7.08 us
  waiting for transfers between devices: 5.05 us -> 4.06 us
    pallas_call x6 -> x7, Pallas kernels: 8.38 us -> 7.08 us  [call(): pl.pallas_call(kernel, out_shape=outs, in_specs=specs, out_specs=jax.tree...]
    ppermute x1, waiting for transfers between devices: 1.08 us -> 0.01 us  [on_device(): got_y = lax.ppermute(own_y, 'gy', swap)]
  transfers between devices with their start and end apart: 5 -> 5, of which waited for: 3 -> 3; matrix products, arithmetic and copies ran while one was open for 0% -> 0% of each run, Pallas kernels for 2% -> 4%
where the time goes in v4:
time: 51.9 us; the launch traced here: 51.7 us
  blocking collectives  37.2 us (72%)
  Pallas kernels  7.08 us (14%)
  waiting for transfers between devices  4.06 us (8%)
  starting transfers between devices  2.88 us (6%)
    all_to_all x2, blocking collectives, exchanged(): return lax.all_to_all(blocks, 'gz', 0, 0, tiled=True).reshape(B * rows, L)  37.2 us
    pallas_call x7, Pallas kernels, call(): pl.pallas_call(kernel, out_shape=outs, in_specs=specs, out_specs=jax.tree...  7.08 us
    ppermute x1, waiting for transfers between devices, on_device(): got_hi = lax.ppermute(own_lo, 'gx', [(b, a) for a, b in ring])  3.41 us
    ppermute x1, starting transfers between devices, on_device(): got_lo = lax.ppermute(own_hi, 'gx', ring)  2.28 us
  transfers between devices with their start and end apart: 5, of which 3 were waited for; matrix products, arithmetic and copies ran while one was open for 0% of the time, Pallas kernels for 4%

profile of v4, /device:TPU:6, one launch (start us, length us, event | category | flops | bytes accessed | tf_op | source)
XLA Modules:
  0.0 51.7 jit_solution(2214522787992359476)
XLA Ops:
  0.0 0.0 copy-start.2
  0.0 0.0 copy-start
  0.0 0.0 copy-start.1
  0.0 0.0 copy-start.3
  0.0 1.6 %shard_map.56 = (f32[72,256]{1,0:T(8,128)}, f32[72,256]{1,0:T(8,128)}) custom-call(f32[16,16,256]{2,1,0:T(8,128)} %corr.1, f32[16,16,256]{2,1,0:T(8,128)} %res.1, f32[16,16,256]{2,1,0:T(8,128)} %state.1, s32[16,256]{1,0:T(8,128)} %colour.9), custom_call_target="tpu_custom_call" | custom-call | flops 1048576 | bytes 1048576 | tf_op jit(solution)/shard_map/pallas_call | solution.py:641
  1.7 2.3 %collective-permute-start = (f32[72,256]{1,0:T(8,128)}, f32[72,256]{1,0:T(8,128)S(1)}, u32[]{:S(2)}, u32[]{:S(2)}) collective-permute-start(f32[72,256]{1,0:T(8,128)} %get-tuple-element.32.own_hi), channel_id=1, source_target_pairs={{0,64},{64,128},{128,192},{192,0},{1,65},{65,129},{129,193},{193,1... | collective-permute-start | bytes 221192 | tf_op jit(solution)/shard_map/ppermute | solution.py:663
  3.9 0.0 collective-permute-start.1
  3.9 0.0 copy-done.2
  3.9 0.0 copy-done
  4.0 0.0 copy-done.1
  4.0 0.0 copy-done.3
  4.0 0.0 copy-start.6
  4.0 0.2 shard_map.57
  4.2 0.1 collective-permute-start.2
  4.3 0.3 copy-done.6
  4.7 1.1 %shard_map.55 = (f32[256,256]{1,0:T(8,128)S(1)}, f32[256,256]{1,0:T(8,128)S(1)}, f32[256,256]{1,0:T(8,128)S(1)}, f32[48,256]{1,0:T(8,128)S(1)}, f32[64,256]{1,0:...) custom-call(s32[512]{0:T(512)S(1)} %copy-done.6, f32[256,256]{1,0:T(8,128)S(1)} %bitcast.13), custom_call_target="tpu_custom_call" | custom-call | flops 4194304 | bytes 4194304 | tf_op jit(solution)/shard_map/pallas_call | solution.py:641
  5.7 0.0 copy-start.4
  5.7 0.0 collective-permute-done.2.got_y
  5.8 0.6 %collective-permute-done.got_lo = f32[72,256]{1,0:T(8,128)S(1)} collective-permute-done((f32[72,256]{1,0:T(8,128)}, f32[72,256]{1,0:T(8,128)S(1)}, u32[]{:S(2)}, u32[]{:S(2)}) %collective-permute-start) | collective-permute-done | bytes 73760 | tf_op jit(solution)/shard_map/ppermute | solution.py:663
  6.3 3.4 %collective-permute-done.1.got_hi = f32[72,256]{1,0:T(8,128)S(1)} collective-permute-done((f32[72,256]{1,0:T(8,128)}, f32[72,256]{1,0:T(8,128)S(1)}, u32[]{:S(2)}, u32[]{:S(2)}) %collective-permute-start.1) | collective-permute-done | bytes 73760 | tf_op jit(solution)/shard_map/ppermute | solution.py:664
  9.7 0.0 collective-permute-start.3
  9.7 0.5 collective-permute-start.4
  10.2 0.0 copy-done.5
  10.2 0.0 copy-done.4
  10.2 0.7 %shard_map.58 = (f32[256,256]{1,0:T(8,128)S(1)}, f32[256,256]{1,0:T(8,128)S(1)}, f32[128,128]{1,0:T(8,128)S(1)}, f32[128,128]{1,0:T(8,128)S(1)}, f32[128,128]{1,...) custom-call(f32[40,256]{1,0:T(8,128)S(1)} %get-tuple-element.31.coef, ...), custom_call_target="tpu_custom_call" | custom-call | flops 4194304 | bytes 4194304 | tf_op jit(solution)/shard_map/pallas_call | solution.py:641
  11.0 0.0 collective-permute-done.3.cross_lo
  11.0 0.1 collective-permute-done.4.cross_hi
  11.1 0.7 %shard_map.59 = (f32[512,128]{1,0:T(8,128)S(1)}, f32[128,128]{1,0:T(8,128)S(1)}) custom-call(f32[40,256]{1,0:T(8,128)S(1)} %get-tuple-element.31.coef, s32[16,256]{1,0:T(8,128)S(1)} %copy-done.3, f32[256,256]{1,0:T(8,128)S(1)} %get-tuple-element.45.source, f32[256,256]{1,0:T(8,128)S(1)} %get-tuple-element.46.v_first, ...), custom_call_target="tpu_custom_call" | custom-call | flops 4194304 | bytes 4194304 | tf_op jit(solution)/shard_map/pallas_call | solution.py:641
  11.8 23.1 %all_to_all.10 = f32[32,16,128]{2,1,0:T(8,128)S(1)} all-to-all(f32[32,16,128]{2,1,0:T(8,128)S(1)} %bitcast.17), channel_id=1, replica_groups=mesh['gx'=4,'gy'=2,'gz'=32] {'gz'}, dimensions={0} | all-to-all | bytes 524288 | tf_op jit(solution)/shard_map/all_to_all | solution.py:694
  34.9 1.4 %shard_map.60 = f32[256,128]{1,0:T(8,128)S(1)} custom-call(f32[512,128]{1,0:T(8,128)S(1)} %bitcast.14, f32[256,128]{1,0:T(8,128)S(1)} %get-tuple-element.56.tints), custom_call_target="tpu_custom_call" | custom-call | flops 2097152 | bytes 2097152 | tf_op jit(solution)/shard_map/pallas_call | solution.py:641
  36.3 14.1 %all_to_all.11 = f32[32,8,128]{2,1,0:T(8,128)S(1)} all-to-all(f32[32,8,128]{2,1,0:T(8,128)S(1)} %bitcast.16), channel_id=1, replica_groups=mesh['gx'=4,'gy'=2,'gz'=32] {'gz'}, dimensions={0} | all-to-all | bytes 262144 | tf_op jit(solution)/shard_map/all_to_all | solution.py:694
  50.4 1.3 %shard_map.61 = f32[256,256]{1,0:T(8,128)} custom-call(f32[40,256]{1,0:T(8,128)S(1)} %get-tuple-element.31.coef, f32[256,256]{1,0:T(8,128)S(1)} %get-tuple-element.45.source, f32[256,256]{1,0:T(8,128)S(1)} %get-tuple-element.36.inv, f32[128,128]{1,0:T(8,128)S(1)} %get-tuple-element.54.h_source, f32[128,128]{1,0:T(8,128)S(1)} %get-tuple-element.48.h_inv, ...), custom_call_target="tpu_custom_call" | custom-call | flops 2097152 | bytes 2097152 | tf_op jit(solution)/shard_map/pallas_call | solution.py:641
  (3 shorter events, 0.0 us)
Async XLA Ops:
  0.0 3.9 %copy-start.2 = (f32[16,16,256]{2,1,0:T(8,128)S(1)}, f32[16,16,256]{2,1,0:T(8,128)}, u32[]{:S(2)}) copy-start(f32[16,16,256]{2,1,0:T(8,128)} %state.1) | copy-start | bytes 786436
  0.0 3.9 %copy-start = (f32[16,16,256]{2,1,0:T(8,128)S(1)}, f32[16,16,256]{2,1,0:T(8,128)}, u32[]{:S(2)}) copy-start(f32[16,16,256]{2,1,0:T(8,128)} %corr.1) | copy-start | bytes 786436
  0.0 3.9 %copy-start.1 = (f32[16,16,256]{2,1,0:T(8,128)S(1)}, f32[16,16,256]{2,1,0:T(8,128)}, u32[]{:S(2)}) copy-start(f32[16,16,256]{2,1,0:T(8,128)} %res.1) | copy-start | bytes 786436
  0.0 4.0 %copy-start.3 = (s32[16,256]{1,0:T(8,128)S(1)}, s32[16,256]{1,0:T(8,128)}, u32[]{:S(2)}) copy-start(s32[16,256]{1,0:T(8,128)} %colour.9) | copy-start | bytes 49156
  1.7 4.6 %collective-permute-start = (f32[72,256]{1,0:T(8,128)}, f32[72,256]{1,0:T(8,128)S(1)}, u32[]{:S(2)}, u32[]{:S(2)}) collective-permute-start(f32[72,256]{1,0:T(8,128)} %get-tuple-element.32.own_hi), channel_id=1, source_target_pairs={{0,64},{64,128},{128,192},{192,0},{1,65},{65,129},{129,193},{193,1... | collective-permute-start | bytes 221192 | tf_op jit(solution)/shard_map/ppermute | solution.py:663
  3.9 5.8 %collective-permute-start.1 = (f32[72,256]{1,0:T(8,128)}, f32[72,256]{1,0:T(8,128)S(1)}, u32[]{:S(2)}, u32[]{:S(2)}) collective-permute-start(f32[72,256]{1,0:T(8,128)} %get-tuple-element.33.own_lo), channel_id=1, source_target_pairs={{64,0},{128,64},{192,128},{0,192},{65,1},{129,65},{193,129},{1,193... | collective-permute-start | bytes 221192 | tf_op jit(solution)/shard_map/ppermute | solution.py:664
  4.0 0.7 %copy-start.6 = (s32[512]{0:T(512)S(1)}, s32[512]{0:T(512)}, u32[]{:S(2)}) copy-start(s32[512]{0:T(512)} %level.1) | copy-start | bytes 6148
  4.2 1.5 %collective-permute-start.2 = (f32[8,256]{1,0:T(8,128)S(1)}, f32[8,256]{1,0:T(8,128)S(1)}, u32[]{:S(2)}, u32[]{:S(2)}) collective-permute-start(f32[8,256]{1,0:T(8,128)S(1)} %get-tuple-element.34.own_y), channel_id=1, source_target_pairs={{0,32},{32,0},{1,33},{33,1},{2,34},{34,2},{3,35},{35,3},{4,36},{36... | collective-permute-start | bytes 24584 | tf_op jit(solution)/shard_map/ppermute | solution.py:669
  4.7 5.6 %copy-start.5 = (f32[72,256]{1,0:T(8,128)S(1)}, f32[72,256]{1,0:T(8,128)}, u32[]{:S(2)}) copy-start(f32[72,256]{1,0:T(8,128)} %get-tuple-element.32.own_hi) | copy-start | bytes 221188
  5.7 4.5 %copy-start.4 = (f32[72,256]{1,0:T(8,128)S(1)}, f32[72,256]{1,0:T(8,128)}, u32[]{:S(2)}) copy-start(f32[72,256]{1,0:T(8,128)} %get-tuple-element.33.own_lo) | copy-start | bytes 221188
  9.7 1.3 %collective-permute-start.3 = (f32[16,256]{1,0:T(8,128)S(1)}, f32[16,256]{1,0:T(8,128)S(1)}, u32[]{:S(2)}, u32[]{:S(2)}) collective-permute-start(f32[16,256]{1,0:T(8,128)S(1)} %slice.6), channel_id=1, source_target_pairs={{0,32},{32,0},{1,33},{33,1},{2,34},{34,2},{3,35},{35,3},{4,36},{36... | collective-permute-start | bytes 49160 | tf_op jit(solution)/shard_map/ppermute | solution.py:677
  9.7 1.3 %collective-permute-start.4 = (f32[16,256]{1,0:T(8,128)S(1)}, f32[16,256]{1,0:T(8,128)S(1)}, u32[]{:S(2)}, u32[]{:S(2)}) collective-permute-start(f32[16,256]{1,0:T(8,128)S(1)} %slice.7), channel_id=1, source_target_pairs={{0,32},{32,0},{1,33},{33,1},{2,34},{34,2},{3,35},{35,3},{4,36},{36... | collective-permute-start | bytes 49160 | tf_op jit(solution)/shard_map/ppermute | solution.py:678

commit v5 on v4

--- a/solution.py
+++ b/solution.py
@@ -479,7 +479,7 @@
             message[p * R + 8 : p * R + 16, :] = turned[8 * n : 8 * n + 8]
 
 
-def separator_kernel(got, tints, out):
+def separator_kernel(got, tints, out, ends):
     patch = lax.axis_index("gz")
     tint = tints[pl.ds(pl.multiple_of(patch * 8, 8), 8), :]
     line, lane = iota((8, L), 0), iota((8, L), 1)
@@ -497,9 +497,9 @@
     quantities = []
     for d in range(B):
         tile = values_of(d)
-        ends = [jnp.broadcast_to(got[d * R + 8 + q : d * R + 9 + q, :], (8, L)) for q in range(5)]
+        edge = [jnp.broadcast_to(got[d * R + 8 + q : d * R + 9 + q, :], (8, L)) for q in range(5)]
         quantities.append(
-            [jnp.where(lane >= LEFT, ends[q], rolled(tile, -PER * q)) for q in range(5)]
+            [jnp.where(lane >= LEFT, edge[q], rolled(tile, -PER * q)) for q in range(5)]
         )
     off = [quantities[d][1] for d in range(B)]
 
@@ -586,36 +586,63 @@
         1.0,
     )
     before = still
+    ends[0:8, :] = still
     for d, value in enumerate(solved(second)):
-        ends = jnp.where(line < 4, value, before)
-        out[8 * d : 8 * d + 8, :] = jnp.where(
-            lane < 32, value, jnp.where(lane < 64, pltpu.roll(before, 32, 1), ends)
+        pair = jnp.where(lane < 32, value, pltpu.roll(pltpu.roll(value, 32, 1), 4, 0))
+        both = jnp.where(lane < 64, pair, pltpu.roll(before, 64, 1))
+        out[4 * d : 4 * d + 4, :] = both[:4]
+        ends[8 + d : 9 + d, :] = value[0:1]
+        before = pair
+
+    shift = jnp.where(patch == 0, PER - LEFT + L, PER - RIGHT + L)
+    here, below = ends[8 : 8 + B, :], ends[7 : 7 + B, :]
+    lanes = iota((B, L), 1)
+    for i in range(2):
+        rows = out[pl.ds(i, B, stride=4), :]
+        rows = jnp.where(
+            (lanes >= PER) & (lanes < PER + 8), pltpu.roll(here, shift - 8 * i, 1), rows
         )
-        before = value
-
-
-def finish_kernel(coef, source, inv, h_source, h_inv, colour, got, out, v_first, h_line):
+        rows = jnp.where(
+            (lanes >= PER + 64) & (lanes < PER + 72), pltpu.roll(below, shift + 64 - 8 * i, 1), rows
+        )
+        out[pl.ds(i, B, stride=4), :] = rows
+
+
+def finish_kernel(
+    coef, source, inv, h_source, h_inv, colour, known, e_first, e_last, got, out, v_first, h_line
+):
     spacing, face = coefficient_rows(coef, Y)
     h_face = coefficient_rows(coef, L)[1]
     left_core = lax.axis_index("gy") == 0
     mine = colour[...]
 
-    turned = jnp.concatenate([jnp.transpose(got[c * L : (c + 1) * L, :]) for c in range(2)], 1)
-    low, high = turned[33 : 33 + X], turned[1 : 1 + X]
+    upper = iota((8, L), 0) < 4
+    tiles = []
+    for n in range(B // 2):
+        near = got[8 * n : 8 * n + 8, :]
+        far = pltpu.roll(near, L - 32, 1)
+        tiles.append(jnp.where(upper, near, pltpu.roll(far, 4, 0)))
+        tiles.append(jnp.where(upper, pltpu.roll(near, 4, 0), far))
+    halves = [jnp.concatenate(tiles[c * L // 8 : (c + 1) * L // 8], 0) for c in range(2)]
+    turned = jnp.concatenate([jnp.transpose(half) for half in halves], 1)
+    low, high = turned[65 : 65 + X], turned[1 : 1 + X]
     nothing = jnp.zeros((1, L), jnp.float32)
+    outer = jnp.where(left_core, tiles[-1], tiles[0])
 
     def beside(b):
-        at_b = 0 if b else 32
-        near = got[Y - 8 + at_b // 8 : Y - 7 + at_b // 8, :]
-        far = got[at_b // 8 : at_b // 8 + 1, :]
-        end = jnp.where(left_core, pltpu.roll(near, L - RIGHT, 1), pltpu.roll(far, L - LEFT, 1))
+        at_b = 0 if b else 64
+        moved = pltpu.roll(outer, L - PER - at_b, 1)
+        end = jnp.where(iota((1, L), 1) < 8, moved[0:1], pltpu.roll(moved[1:2], 8, 1))
         lo, hi = turned[at_b : at_b + 1], turned[at_b + 1 + X : at_b + 2 + X]
         places = {XHI: hi[:, :L], XHI + 1: hi[:, L:], XLO0: lo[:, :L], XLO1: lo[:, L:], YH: end}
         return jnp.concatenate([places.get(p, nothing) for p in range(8)], 0)
 
     beside_after_first(h_face, h_source, h_inv, beside(0), beside(1), h_line)
     columns = sided(transposed(h_line[pl.ds(YH, D, stride=8), :]))
-    own_after_first(face, source, inv, mine, low, high, v_first)
+    low_first, high_first = jnp.where(mine == 0, low, 0.0), jnp.where(mine == 0, high, 0.0)
+    for k in range(D):
+        value = known[at(k), :] + e_first[at(k), :] * low_first
+        v_first[at(k), :] = value + e_last[at(k), :] * high_first
     value = low
     for k in range(D - 1):
         added = beside_sum(v_first, h_line, columns, k)
@@ -694,11 +721,13 @@
         return lax.all_to_all(blocks, "gz", 0, 0, tiled=True).reshape(B * rows, L)
 
     separators = call(
-        separator_kernel, f32(B * 8, L), [VMEM] * 2, [], 1 << 21, exchanged(message, R), tints
+        separator_kernel, f32(B * 4, L), [VMEM] * 2, [(B + 8, L)],
+        1 << 21, exchanged(message, R), tints,
     )
     out = call(
-        finish_kernel, field, [VMEM] * 7, [(D * X, Y), (8 * D, L)], 1 << 21,
-        coef, source, inv, h_source, h_inv, colour, exchanged(separators, 8),
+        finish_kernel, field, [VMEM] * 10, [(D * X, Y), (8 * D, L)], 1 << 21,
+        coef, source, inv, h_source, h_inv, colour, v_first, e_first, e_last,
+        exchanged(separators, 4),
     )
     return out.reshape(D, X, Y)
 

time: 51.9 us -> 51.6 us (level)
  blocking collectives: 37.2 us -> 36.6 us
    all_to_all x2, blocking collectives: 37.2 us -> 36.6 us  [exchanged(): return lax.all_to_all(blocks, 'gz', 0, 0, tiled=True).reshape(B * rows, L)]
where the time goes in v5:
time: 51.6 us; the launch traced here: 51.3 us
  blocking collectives  36.6 us (71%)
  Pallas kernels  7.27 us (14%)
  waiting for transfers between devices  4.07 us (8%)
  starting transfers between devices  2.88 us (6%)
    all_to_all x2, blocking collectives, exchanged(): return lax.all_to_all(blocks, 'gz', 0, 0, tiled=True).reshape(B * rows, L)  36.6 us
    pallas_call x7, Pallas kernels, call(): pl.pallas_call(kernel, out_shape=outs, in_specs=specs, out_specs=jax.tree...  7.27 us
    ppermute x1, waiting for transfers between devices, on_device(): got_hi = lax.ppermute(own_lo, 'gx', [(b, a) for a, b in ring])  3.41 us
    ppermute x1, starting transfers between devices, on_device(): got_lo = lax.ppermute(own_hi, 'gx', ring)  2.28 us
  transfers between devices with their start and end apart: 5, of which 3 were waited for; matrix products, arithmetic and copies ran while one was open for 0% of the time, Pallas kernels for 4%

profile of v5, /device:TPU:6, one launch (start us, length us, event | category | flops | bytes accessed | tf_op | source)
XLA Modules:
  0.0 51.3 jit_solution(3932225062969476910)
XLA Ops:
  0.0 0.0 copy-start.2
  0.0 0.0 copy-start
  0.0 0.0 copy-start.1
  0.0 0.0 copy-start.3
  0.0 1.6 %shard_map.56 = (f32[72,256]{1,0:T(8,128)}, f32[72,256]{1,0:T(8,128)}) custom-call(f32[16,16,256]{2,1,0:T(8,128)} %corr.1, f32[16,16,256]{2,1,0:T(8,128)} %res.1, f32[16,16,256]{2,1,0:T(8,128)} %state.1, s32[16,256]{1,0:T(8,128)} %colour.9), custom_call_target="tpu_custom_call" | custom-call | flops 1048576 | bytes 1048576 | tf_op jit(solution)/shard_map/pallas_call | solution.py:668
  1.7 2.3 %collective-permute-start = (f32[72,256]{1,0:T(8,128)}, f32[72,256]{1,0:T(8,128)S(1)}, u32[]{:S(2)}, u32[]{:S(2)}) collective-permute-start(f32[72,256]{1,0:T(8,128)} %get-tuple-element.32.own_hi), channel_id=1, source_target_pairs={{0,64},{64,128},{128,192},{192,0},{1,65},{65,129},{129,193},{193,1... | collective-permute-start | bytes 221192 | tf_op jit(solution)/shard_map/ppermute | solution.py:690
  3.9 0.0 collective-permute-start.1
  3.9 0.0 copy-done.2
  3.9 0.0 copy-done
  4.0 0.0 copy-done.1
  4.0 0.0 copy-done.3
  4.0 0.0 copy-start.6
  4.0 0.2 shard_map.57
  4.2 0.1 collective-permute-start.2
  4.3 0.3 copy-done.6
  4.7 1.1 %shard_map.55 = (f32[256,256]{1,0:T(8,128)S(1)}, f32[256,256]{1,0:T(8,128)S(1)}, f32[256,256]{1,0:T(8,128)S(1)}, f32[48,256]{1,0:T(8,128)S(1)}, f32[64,256]{1,0:...) custom-call(s32[512]{0:T(512)S(1)} %copy-done.6, f32[256,256]{1,0:T(8,128)S(1)} %bitcast.13), custom_call_target="tpu_custom_call" | custom-call | flops 4194304 | bytes 4194304 | tf_op jit(solution)/shard_map/pallas_call | solution.py:668
  5.7 0.0 copy-start.4
  5.7 0.0 collective-permute-done.2.got_y
  5.8 0.6 %collective-permute-done.got_lo = f32[72,256]{1,0:T(8,128)S(1)} collective-permute-done((f32[72,256]{1,0:T(8,128)}, f32[72,256]{1,0:T(8,128)S(1)}, u32[]{:S(2)}, u32[]{:S(2)}) %collective-permute-start) | collective-permute-done | bytes 73760 | tf_op jit(solution)/shard_map/ppermute | solution.py:690
  6.3 3.4 %collective-permute-done.1.got_hi = f32[72,256]{1,0:T(8,128)S(1)} collective-permute-done((f32[72,256]{1,0:T(8,128)}, f32[72,256]{1,0:T(8,128)S(1)}, u32[]{:S(2)}, u32[]{:S(2)}) %collective-permute-start.1) | collective-permute-done | bytes 73760 | tf_op jit(solution)/shard_map/ppermute | solution.py:691
  9.7 0.0 collective-permute-start.3
  9.7 0.5 collective-permute-start.4
  10.2 0.0 copy-done.5
  10.2 0.0 copy-done.4
  10.2 0.7 %shard_map.58 = (f32[256,256]{1,0:T(8,128)S(1)}, f32[256,256]{1,0:T(8,128)S(1)}, f32[128,128]{1,0:T(8,128)S(1)}, f32[128,128]{1,0:T(8,128)S(1)}, f32[128,128]{1,...) custom-call(f32[40,256]{1,0:T(8,128)S(1)} %get-tuple-element.31.coef, ...), custom_call_target="tpu_custom_call" | custom-call | flops 4194304 | bytes 4194304 | tf_op jit(solution)/shard_map/pallas_call | solution.py:668
  11.0 0.0 collective-permute-done.3.cross_lo
  11.0 0.1 collective-permute-done.4.cross_hi
  11.1 0.7 %shard_map.59 = (f32[512,128]{1,0:T(8,128)S(1)}, f32[128,128]{1,0:T(8,128)S(1)}) custom-call(f32[40,256]{1,0:T(8,128)S(1)} %get-tuple-element.31.coef, s32[16,256]{1,0:T(8,128)S(1)} %copy-done.3, f32[256,256]{1,0:T(8,128)S(1)} %get-tuple-element.45.source, f32[256,256]{1,0:T(8,128)S(1)} %get-tuple-element.46.v_first.known, ...), custom_call_target="tpu_custom_call" | custom-call | flops 4194304 | bytes 4194304 | tf_op jit(solution)/shard_map/pallas_call | solution.py:668
  11.8 23.1 %all_to_all.10 = f32[32,16,128]{2,1,0:T(8,128)S(1)} all-to-all(f32[32,16,128]{2,1,0:T(8,128)S(1)} %bitcast.17), channel_id=1, replica_groups=mesh['gx'=4,'gy'=2,'gz'=32] {'gz'}, dimensions={0} | all-to-all | bytes 524288 | tf_op jit(solution)/shard_map/all_to_all | solution.py:721
  34.9 1.5 %shard_map.60 = f32[128,128]{1,0:T(8,128)S(1)} custom-call(f32[512,128]{1,0:T(8,128)S(1)} %bitcast.14, f32[256,128]{1,0:T(8,128)S(1)} %get-tuple-element.56.tints), custom_call_target="tpu_custom_call" | custom-call | flops 2097152 | bytes 2097152 | tf_op jit(solution)/shard_map/pallas_call | solution.py:668
  36.4 13.5 %all_to_all.11 = f32[32,4,128]{2,1,0:T(4,128)S(1)} all-to-all(f32[32,4,128]{2,1,0:T(4,128)S(1)} %bitcast.16), channel_id=1, replica_groups=mesh['gx'=4,'gy'=2,'gz'=32] {'gz'}, dimensions={0} | all-to-all | bytes 131072 | tf_op jit(solution)/shard_map/all_to_all | solution.py:721
  50.0 1.4 %shard_map.61 = f32[256,256]{1,0:T(8,128)} custom-call(f32[40,256]{1,0:T(8,128)S(1)} %get-tuple-element.31.coef, f32[256,256]{1,0:T(8,128)S(1)} %get-tuple-element.45.source, f32[256,256]{1,0:T(8,128)S(1)} %get-tuple-element.36.inv, f32[128,128]{1,0:T(8,128)S(1)} %get-tuple-element.54.h_source, f32[128,128]{1,0:T(8,128)S(1)} %get-tuple-element.48.h_inv, ...), custom_call_target="tpu_custom_call" | custom-call | flops 2097152 | bytes 2097152 | tf_op jit(solution)/shard_map/pallas_call | solution.py:668
  (3 shorter events, 0.0 us)
Async XLA Ops:
  0.0 3.9 %copy-start.2 = (f32[16,16,256]{2,1,0:T(8,128)S(1)}, f32[16,16,256]{2,1,0:T(8,128)}, u32[]{:S(2)}) copy-start(f32[16,16,256]{2,1,0:T(8,128)} %state.1) | copy-start | bytes 786436
  0.0 3.9 %copy-start = (f32[16,16,256]{2,1,0:T(8,128)S(1)}, f32[16,16,256]{2,1,0:T(8,128)}, u32[]{:S(2)}) copy-start(f32[16,16,256]{2,1,0:T(8,128)} %corr.1) | copy-start | bytes 786436
  0.0 3.9 %copy-start.1 = (f32[16,16,256]{2,1,0:T(8,128)S(1)}, f32[16,16,256]{2,1,0:T(8,128)}, u32[]{:S(2)}) copy-start(f32[16,16,256]{2,1,0:T(8,128)} %res.1) | copy-start | bytes 786436
  0.0 4.0 %copy-start.3 = (s32[16,256]{1,0:T(8,128)S(1)}, s32[16,256]{1,0:T(8,128)}, u32[]{:S(2)}) copy-start(s32[16,256]{1,0:T(8,128)} %colour.9) | copy-start | bytes 49156
  1.7 4.6 %collective-permute-start = (f32[72,256]{1,0:T(8,128)}, f32[72,256]{1,0:T(8,128)S(1)}, u32[]{:S(2)}, u32[]{:S(2)}) collective-permute-start(f32[72,256]{1,0:T(8,128)} %get-tuple-element.32.own_hi), channel_id=1, source_target_pairs={{0,64},{64,128},{128,192},{192,0},{1,65},{65,129},{129,193},{193,1... | collective-permute-start | bytes 221192 | tf_op jit(solution)/shard_map/ppermute | solution.py:690
  3.9 5.8 %collective-permute-start.1 = (f32[72,256]{1,0:T(8,128)}, f32[72,256]{1,0:T(8,128)S(1)}, u32[]{:S(2)}, u32[]{:S(2)}) collective-permute-start(f32[72,256]{1,0:T(8,128)} %get-tuple-element.33.own_lo), channel_id=1, source_target_pairs={{64,0},{128,64},{192,128},{0,192},{65,1},{129,65},{193,129},{1,193... | collective-permute-start | bytes 221192 | tf_op jit(solution)/shard_map/ppermute | solution.py:691
  4.0 0.7 %copy-start.6 = (s32[512]{0:T(512)S(1)}, s32[512]{0:T(512)}, u32[]{:S(2)}) copy-start(s32[512]{0:T(512)} %level.1) | copy-start | bytes 6148
  4.2 1.5 %collective-permute-start.2 = (f32[8,256]{1,0:T(8,128)S(1)}, f32[8,256]{1,0:T(8,128)S(1)}, u32[]{:S(2)}, u32[]{:S(2)}) collective-permute-start(f32[8,256]{1,0:T(8,128)S(1)} %get-tuple-element.34.own_y), channel_id=1, source_target_pairs={{0,32},{32,0},{1,33},{33,1},{2,34},{34,2},{3,35},{35,3},{4,36},{36... | collective-permute-start | bytes 24584 | tf_op jit(solution)/shard_map/ppermute | solution.py:696
  4.7 5.6 %copy-start.5 = (f32[72,256]{1,0:T(8,128)S(1)}, f32[72,256]{1,0:T(8,128)}, u32[]{:S(2)}) copy-start(f32[72,256]{1,0:T(8,128)} %get-tuple-element.32.own_hi) | copy-start | bytes 221188
  5.7 4.5 %copy-start.4 = (f32[72,256]{1,0:T(8,128)S(1)}, f32[72,256]{1,0:T(8,128)}, u32[]{:S(2)}) copy-start(f32[72,256]{1,0:T(8,128)} %get-tuple-element.33.own_lo) | copy-start | bytes 221188
  9.7 1.2 %collective-permute-start.3 = (f32[16,256]{1,0:T(8,128)S(1)}, f32[16,256]{1,0:T(8,128)S(1)}, u32[]{:S(2)}, u32[]{:S(2)}) collective-permute-start(f32[16,256]{1,0:T(8,128)S(1)} %slice.6), channel_id=1, source_target_pairs={{0,32},{32,0},{1,33},{33,1},{2,34},{34,2},{3,35},{35,3},{4,36},{36... | collective-permute-start | bytes 49160 | tf_op jit(solution)/shard_map/ppermute | solution.py:704
  9.7 1.3 %collective-permute-start.4 = (f32[16,256]{1,0:T(8,128)S(1)}, f32[16,256]{1,0:T(8,128)S(1)}, u32[]{:S(2)}, u32[]{:S(2)}) collective-permute-start(f32[16,256]{1,0:T(8,128)S(1)} %slice.7), channel_id=1, source_target_pairs={{0,32},{32,0},{1,33},{33,1},{2,34},{34,2},{3,35},{35,3},{4,36},{36... | collective-permute-start | bytes 49160 | tf_op jit(solution)/shard_map/ppermute | solution.py:705

commit v6 on v5

--- a/solution.py
+++ b/solution.py
@@ -412,7 +412,7 @@
 
 def message_kernel(
     coef, colour, source, v_first, h_local, h_inv, h_first, h_last, h_mask, coupled, local,
-    e_first, e_last, cross_lo, cross_hi,
+    e_first, e_last, crossed,
     message, h_source, h_line, laid,
 ):
     spacing, face = coefficient_rows(coef, Y)
@@ -430,6 +430,7 @@
         h_source[pl.ds(place, D, stride=8), :] = rows
 
     xs = lax.axis_size("gx") - 1
+    cross_lo, cross_hi = crossed[0:D, :], crossed[D:, :]
     for cross, there, places, lane_at in (
         (cross_lo, lax.axis_index("gx") > 0, (XLO0, XLO1), 0),
         (cross_hi, lax.axis_index("gx") < xs, (XHI, XHI + 1), X - 1),
@@ -701,8 +702,7 @@
         [SMEM, VMEM], [], 1 << 22, level, st,
     )
     got_lo, got_hi, got_y, inv = lax.optimization_barrier((got_lo, got_hi, got_y, inv))
-    cross_lo = lax.ppermute(got_lo[:D], "gy", swap)
-    cross_hi = lax.ppermute(got_hi[:D], "gy", swap)
+    crossed = lax.ppermute(jnp.concatenate([got_lo[:D], got_hi[:D]], 0), "gy", swap)
     small = f32(8 * D, L)
     source, v_first, h_local, h_inv, h_first, h_last, h_mask, coupled, laid = call(
         local_kernel, (field, field, small, small, small, small, f32(8, L), f32(Y, L), f32(L, Y)),
@@ -711,9 +711,9 @@
         own_lo, own_hi, got_lo, got_hi, own_y, got_y,
     )
     message, h_source = call(
-        message_kernel, (f32(B * R, L), small), [VMEM] * 15, [(8 * D, L), (L, Y)], 1 << 22,
+        message_kernel, (f32(B * R, L), small), [VMEM] * 14, [(8 * D, L), (L, Y)], 1 << 22,
         coef, colour, source, v_first, h_local, h_inv, h_first, h_last, h_mask, coupled, laid,
-        e_first, e_last, cross_lo, cross_hi,
+        e_first, e_last, crossed,
     )
 
     def exchanged(value, rows):

time: 51.6 us -> 51.4 us (level)
  transfers between devices with their start and end apart: 5 -> 4, of which waited for: 3 -> 3; matrix products, arithmetic and copies ran while one was open for 0% -> 0% of each run, Pallas kernels for 4% -> 4%
where the time goes in v6:
time: 51.4 us; the launch traced here: 51.1 us
  blocking collectives  36.5 us (71%)
  Pallas kernels  7.26 us (14%)
  waiting for transfers between devices  4.41 us (9%)
  starting transfers between devices  2.47 us (5%)
    all_to_all x2, blocking collectives, exchanged(): return lax.all_to_all(blocks, 'gz', 0, 0, tiled=True).reshape(B * rows, L)  36.5 us
    pallas_call x7, Pallas kernels, call(): pl.pallas_call(kernel, out_shape=outs, in_specs=specs, out_specs=jax.tree...  7.26 us
    ppermute x1, waiting for transfers between devices, on_device(): got_hi = lax.ppermute(own_lo, 'gx', [(b, a) for a, b in ring])  3.41 us
    ppermute x1, starting transfers between devices, on_device(): got_lo = lax.ppermute(own_hi, 'gx', ring)  2.28 us
  transfers between devices with their start and end apart: 4, of which 3 were waited for; matrix products, arithmetic and copies ran while one was open for 0% of the time, Pallas kernels for 4%

profile of v6, /device:TPU:6, one launch (start us, length us, event | category | flops | bytes accessed | tf_op | source)
XLA Modules:
  0.0 51.1 jit_solution(85050656341158941)
XLA Ops:
  0.0 0.0 copy-start.2
  0.0 0.0 copy-start
  0.0 0.0 copy-start.1
  0.0 0.0 copy-start.3
  0.0 1.6 %shard_map.56 = (f32[72,256]{1,0:T(8,128)}, f32[72,256]{1,0:T(8,128)}) custom-call(f32[16,16,256]{2,1,0:T(8,128)} %corr.1, f32[16,16,256]{2,1,0:T(8,128)} %res.1, f32[16,16,256]{2,1,0:T(8,128)} %state.1, s32[16,256]{1,0:T(8,128)} %colour.9), custom_call_target="tpu_custom_call" | custom-call | flops 1048576 | bytes 1048576 | tf_op jit(solution)/shard_map/pallas_call | solution.py:669
  1.6 2.3 %collective-permute-start = (f32[72,256]{1,0:T(8,128)}, f32[72,256]{1,0:T(8,128)S(1)}, u32[]{:S(2)}, u32[]{:S(2)}) collective-permute-start(f32[72,256]{1,0:T(8,128)} %get-tuple-element.32.own_hi), channel_id=1, source_target_pairs={{0,64},{64,128},{128,192},{192,0},{1,65},{65,129},{129,193},{193,1... | collective-permute-start | bytes 221192 | tf_op jit(solution)/shard_map/ppermute | solution.py:691
  3.9 0.0 collective-permute-start.1
  3.9 0.0 copy-done.2
  3.9 0.0 copy-done
  3.9 0.0 copy-done.1
  3.9 0.0 copy-done.3
  4.0 0.0 copy-start.6
  4.0 0.2 shard_map.57
  4.2 0.1 collective-permute-start.2
  4.3 0.3 copy-done.6
  4.6 0.0 copy-start.5
  4.6 1.1 %shard_map.55 = (f32[256,256]{1,0:T(8,128)S(1)}, f32[256,256]{1,0:T(8,128)S(1)}, f32[256,256]{1,0:T(8,128)S(1)}, f32[48,256]{1,0:T(8,128)S(1)}, f32[64,256]{1,0:...) custom-call(s32[512]{0:T(512)S(1)} %copy-done.6, f32[256,256]{1,0:T(8,128)S(1)} %bitcast.13), custom_call_target="tpu_custom_call" | custom-call | flops 4194304 | bytes 4194304 | tf_op jit(solution)/shard_map/pallas_call | solution.py:669
  5.7 0.0 copy-start.4
  5.7 0.0 collective-permute-done.2.got_y
  5.7 0.6 %collective-permute-done.got_lo = f32[72,256]{1,0:T(8,128)S(1)} collective-permute-done((f32[72,256]{1,0:T(8,128)}, f32[72,256]{1,0:T(8,128)S(1)}, u32[]{:S(2)}, u32[]{:S(2)}) %collective-permute-start) | collective-permute-done | bytes 73760 | tf_op jit(solution)/shard_map/ppermute | solution.py:691
  6.3 3.4 %collective-permute-done.1.got_hi = f32[72,256]{1,0:T(8,128)S(1)} collective-permute-done((f32[72,256]{1,0:T(8,128)}, f32[72,256]{1,0:T(8,128)S(1)}, u32[]{:S(2)}, u32[]{:S(2)}) %collective-permute-start.1) | collective-permute-done | bytes 73760 | tf_op jit(solution)/shard_map/ppermute | solution.py:692
  9.7 0.1 collective-permute-start.3
  9.8 0.0 copy-done.5
  9.8 0.0 copy-done.4
  9.8 0.7 %shard_map.58 = (f32[256,256]{1,0:T(8,128)S(1)}, f32[256,256]{1,0:T(8,128)S(1)}, f32[128,128]{1,0:T(8,128)S(1)}, f32[128,128]{1,0:T(8,128)S(1)}, f32[128,128]{1,...) custom-call(f32[40,256]{1,0:T(8,128)S(1)} %get-tuple-element.31.coef, ...), custom_call_target="tpu_custom_call" | custom-call | flops 4194304 | bytes 4194304 | tf_op jit(solution)/shard_map/pallas_call | solution.py:669
  10.6 0.4 collective-permute-done.3.crossed
  11.0 0.7 %shard_map.59 = (f32[512,128]{1,0:T(8,128)S(1)}, f32[128,128]{1,0:T(8,128)S(1)}) custom-call(f32[40,256]{1,0:T(8,128)S(1)} %get-tuple-element.31.coef, s32[16,256]{1,0:T(8,128)S(1)} %copy-done.3, f32[256,256]{1,0:T(8,128)S(1)} %get-tuple-element.45.source, f32[256,256]{1,0:T(8,128)S(1)} %get-tuple-element.46.v_first.known, ...), custom_call_target="tpu_custom_call" | custom-call | flops 4194304 | bytes 4194304 | tf_op jit(solution)/shard_map/pallas_call | solution.py:669
  11.7 22.8 %all_to_all.10 = f32[32,16,128]{2,1,0:T(8,128)S(1)} all-to-all(f32[32,16,128]{2,1,0:T(8,128)S(1)} %bitcast.17), channel_id=1, replica_groups=mesh['gx'=4,'gy'=2,'gz'=32] {'gz'}, dimensions={0} | all-to-all | bytes 524288 | tf_op jit(solution)/shard_map/all_to_all | solution.py:721
  34.6 1.5 %shard_map.60 = f32[128,128]{1,0:T(8,128)S(1)} custom-call(f32[512,128]{1,0:T(8,128)S(1)} %bitcast.14, f32[256,128]{1,0:T(8,128)S(1)} %get-tuple-element.56.tints), custom_call_target="tpu_custom_call" | custom-call | flops 2097152 | bytes 2097152 | tf_op jit(solution)/shard_map/pallas_call | solution.py:669
  36.1 13.6 %all_to_all.11 = f32[32,4,128]{2,1,0:T(4,128)S(1)} all-to-all(f32[32,4,128]{2,1,0:T(4,128)S(1)} %bitcast.16), channel_id=1, replica_groups=mesh['gx'=4,'gy'=2,'gz'=32] {'gz'}, dimensions={0} | all-to-all | bytes 131072 | tf_op jit(solution)/shard_map/all_to_all | solution.py:721
  49.7 1.4 %shard_map.61 = f32[256,256]{1,0:T(8,128)} custom-call(f32[40,256]{1,0:T(8,128)S(1)} %get-tuple-element.31.coef, f32[256,256]{1,0:T(8,128)S(1)} %get-tuple-element.45.source, f32[256,256]{1,0:T(8,128)S(1)} %get-tuple-element.36.inv, f32[128,128]{1,0:T(8,128)S(1)} %get-tuple-element.54.h_source, f32[128,128]{1,0:T(8,128)S(1)} %get-tuple-element.48.h_inv, ...), custom_call_target="tpu_custom_call" | custom-call | flops 2097152 | bytes 2097152 | tf_op jit(solution)/shard_map/pallas_call | solution.py:669
  (3 shorter events, 0.0 us)
Async XLA Ops:
  0.0 3.9 %copy-start.2 = (f32[16,16,256]{2,1,0:T(8,128)S(1)}, f32[16,16,256]{2,1,0:T(8,128)}, u32[]{:S(2)}) copy-start(f32[16,16,256]{2,1,0:T(8,128)} %state.1) | copy-start | bytes 786436
  0.0 3.9 %copy-start = (f32[16,16,256]{2,1,0:T(8,128)S(1)}, f32[16,16,256]{2,1,0:T(8,128)}, u32[]{:S(2)}) copy-start(f32[16,16,256]{2,1,0:T(8,128)} %corr.1) | copy-start | bytes 786436
  0.0 3.9 %copy-start.1 = (f32[16,16,256]{2,1,0:T(8,128)S(1)}, f32[16,16,256]{2,1,0:T(8,128)}, u32[]{:S(2)}) copy-start(f32[16,16,256]{2,1,0:T(8,128)} %res.1) | copy-start | bytes 786436
  0.0 3.9 %copy-start.3 = (s32[16,256]{1,0:T(8,128)S(1)}, s32[16,256]{1,0:T(8,128)}, u32[]{:S(2)}) copy-start(s32[16,256]{1,0:T(8,128)} %colour.9) | copy-start | bytes 49156
  1.6 4.6 %collective-permute-start = (f32[72,256]{1,0:T(8,128)}, f32[72,256]{1,0:T(8,128)S(1)}, u32[]{:S(2)}, u32[]{:S(2)}) collective-permute-start(f32[72,256]{1,0:T(8,128)} %get-tuple-element.32.own_hi), channel_id=1, source_target_pairs={{0,64},{64,128},{128,192},{192,0},{1,65},{65,129},{129,193},{193,1... | collective-permute-start | bytes 221192 | tf_op jit(solution)/shard_map/ppermute | solution.py:691
  3.9 5.8 %collective-permute-start.1 = (f32[72,256]{1,0:T(8,128)}, f32[72,256]{1,0:T(8,128)S(1)}, u32[]{:S(2)}, u32[]{:S(2)}) collective-permute-start(f32[72,256]{1,0:T(8,128)} %get-tuple-element.33.own_lo), channel_id=1, source_target_pairs={{64,0},{128,64},{192,128},{0,192},{65,1},{129,65},{193,129},{1,193... | collective-permute-start | bytes 221192 | tf_op jit(solution)/shard_map/ppermute | solution.py:692
  4.0 0.7 %copy-start.6 = (s32[512]{0:T(512)S(1)}, s32[512]{0:T(512)}, u32[]{:S(2)}) copy-start(s32[512]{0:T(512)} %level.1) | copy-start | bytes 6148
  4.2 1.5 %collective-permute-start.2 = (f32[8,256]{1,0:T(8,128)S(1)}, f32[8,256]{1,0:T(8,128)S(1)}, u32[]{:S(2)}, u32[]{:S(2)}) collective-permute-start(f32[8,256]{1,0:T(8,128)S(1)} %get-tuple-element.34.own_y), channel_id=1, source_target_pairs={{0,32},{32,0},{1,33},{33,1},{2,34},{34,2},{3,35},{35,3},{4,36},{36... | collective-permute-start | bytes 24584 | tf_op jit(solution)/shard_map/ppermute | solution.py:697
  4.6 5.2 %copy-start.5 = (f32[72,256]{1,0:T(8,128)S(1)}, f32[72,256]{1,0:T(8,128)}, u32[]{:S(2)}) copy-start(f32[72,256]{1,0:T(8,128)} %get-tuple-element.32.own_hi) | copy-start | bytes 221188
  5.7 4.1 %copy-start.4 = (f32[72,256]{1,0:T(8,128)S(1)}, f32[72,256]{1,0:T(8,128)}, u32[]{:S(2)}) copy-start(f32[72,256]{1,0:T(8,128)} %get-tuple-element.33.own_lo) | copy-start | bytes 221188
  9.7 1.3 %collective-permute-start.3 = (f32[32,256]{1,0:T(8,128)S(1)}, f32[32,256]{1,0:T(8,128)S(1)}, u32[]{:S(2)}, u32[]{:S(2)}) collective-permute-start(f32[32,256]{1,0:T(8,128)S(1)} %pad_maximum_fusion), channel_id=1, source_target_pairs={{0,32},{32,0},{1,33},{33,1},{2,34},{34,2},{3,35},{35,3},{4,36},{36... | collective-permute-start | bytes 98312 | tf_op jit(solution)/shard_map/ppermute | solution.py:705
